TPU v7x, 512 devices: a whole 4x8x8 slice. The times are simulated.
512 devices in a mesh: plane: 128 (over z, y, core), layer: 4 (over x).
Axes of the slice: x: 4, y: 8, z: 8, core: 2. Of those that a mesh axis runs over, the one named last changes fastest.
Arguments:
- nodal_motion_vector: float32 [3, 32, 2048, 256], P(None, 'layer', 'plane'), may hold values from -6 to 6
- nodal_speed_vector: float32 [3, 32, 2048, 256], P(None, 'layer', 'plane'), may hold values from -6 to 6
- element_heating_increment: float32 [32, 2048, 256], P('layer', 'plane'), may hold values from -2 to -0.5
- element_medium_label: int32 [32, 2048, 256], P('layer', 'plane'), may hold values from 0 to 3
- medium_parameter_matrix: float32 [4, 4], replicated, may hold values from 0.5 to 2
- solder_vertex_position: int32 [128, 5, 128], P('plane'), may hold values from 0 to 4095
- landing_vertex_position: int32 [128, 5, 128], P('plane'), may hold values from 0 to 4095
- link_spring_coefficient: float32 [128, 5, 128], P('plane'), may hold values from 0.5 to 2
- active_link_tally: int32 [128, 5], P('plane'), may hold values from 0 to 128, as said below
Outputs:
- displacement_out: float32 [3, 32, 2048, 256], P(None, 'layer', 'plane')
- velocity_out: float32 [3, 32, 2048, 256], P(None, 'layer', 'plane')
Inputs may be any that keep to these rules, and one draw needn't show every extreme that they name: `active_link_tally`: the live slots of a bucket are its first ones; in every draw some pad block receives 128 live pairs from every bump block within 2 blocks of it.
All inputs are finite; a program needn't handle non-finite values.
Results may differ from a plain program's by a relative error of at most 0.0001.
Values sent between devices are 32-bit elements; how exact they have to be, the bound alone decides.
No kernel may reach another device: no remote copies, remote signals or barrier semaphores. Data moves between devices by JAX's collectives and lax.ppermute only.
A program may use at most 64 MiB of HBM per device.

v0:
```python
import math

import jax
import jax.numpy as jnp
import numpy as np
from jax import lax
from jax.sharding import PartitionSpec as P

STEPS = 2


time_step = 0.05
lumped_extra = 0.25


def shifted(value, axis, steps):
    count = lax.axis_size(axis)
    leading, last = (max(0, -steps), min(count, count - steps))
    return lax.ppermute(value, axis, [(source, source + steps) for source in range(leading, last)])


def with_halo(block, sides, width):
    for axis, dim in sides:
        count = lax.axis_size(axis)
        forward = [(i, i + 1) for i in range(count - 1)]
        backward = [(target, source) for source, target in forward]
        low = lax.ppermute(
            lax.slice_in_dim(block, block.shape[dim] - width, None, axis=dim), axis, forward
        )
        high = lax.ppermute(lax.slice_in_dim(block, 0, width, axis=dim), axis, backward)
        block = jnp.concatenate([low, block, high], axis=dim)
    return block


def element_tables():
    points = [0.5 - 0.5 / math.sqrt(3.0), 0.5 + 0.5 / math.sqrt(3.0)]
    corner_bits = [(dz, dx, dy) for dz in (0, 1) for dx in (0, 1) for dy in (0, 1)]
    first = np.zeros((24, 24))
    second = np.zeros((24, 24))
    thermal = np.zeros(24)
    for point_z in points:
        for point_x in points:
            for point_y in points:
                point = (point_z, point_x, point_y)
                grads = np.zeros((8, 3))
                for corner, bit in enumerate(corner_bits):
                    for axis in range(3):
                        value = 1.0
                        for other in range(3):
                            if other == axis:
                                factor = 1.0 if bit[other] else -1.0
                            else:
                                factor = point[other] if bit[other] else 1.0 - point[other]
                            value = value * factor
                        grads[corner, axis] = value
                for a in range(3):
                    for c in range(8):
                        thermal[a * 8 + c] += 0.125 * grads[c, a]
                        for b in range(3):
                            for e in range(8):
                                first[a * 8 + c, b * 8 + e] += 0.125 * grads[c, a] * grads[e, b]
                                same = 1.0 if a == b else 0.0
                                second[a * 8 + c, b * 8 + e] += 0.125 * (
                                    same * np.dot(grads[c], grads[e]) + grads[c, b] * grads[e, a]
                                )
    both = np.concatenate([first, second], axis=1)
    return (jnp.asarray(both, jnp.float32), jnp.asarray(thermal, jnp.float32))


def element_medium_entries(
    element_medium_label, medium_parameter_matrix, element_heating_increment
):
    fields = jnp.zeros((4,) + element_medium_label.shape, jnp.float32)
    for which in range(medium_parameter_matrix.shape[1]):
        chosen = (element_medium_label == which)[None]
        fields = fields + jnp.where(
            chosen, medium_parameter_matrix[:, which][:, None, None, None], jnp.float32(0.0)
        )
    lambda_elastic_parameter, rigidity_parameter, heating_dilation_measure, density = (
        fields[0],
        fields[1],
        fields[2],
        fields[3],
    )
    dilation_coefficient_value = (
        (3.0 * lambda_elastic_parameter + 2.0 * rigidity_parameter)
        * heating_dilation_measure
        * element_heating_increment
    )
    return jnp.stack(
        [lambda_elastic_parameter, rigidity_parameter, dilation_coefficient_value, density]
    )


def cell_mask(z_start, x_start, total_z, total_x, depth, width, length, gap_z):
    glob_z = z_start + jnp.arange(depth + 1) - 1
    glob_x = x_start + jnp.arange(width + 1) - 1
    inside_z = (glob_z >= 0) & (glob_z <= total_z - 2) & (glob_z != gap_z)
    inside_x = (glob_x >= 0) & (glob_x <= total_x - 2)
    inside_y = jnp.arange(length) < length - 1
    return (inside_z[:, None, None] & inside_x[None, :, None] & inside_y[None, None, :]).astype(
        jnp.float32
    )


def node_mass(cells):
    density = cells[3]
    depth = density.shape[0] - 1
    width = density.shape[1] - 1
    total = jnp.zeros((depth, width, density.shape[2]), jnp.float32)
    for dz in (0, 1):
        for dx in (0, 1):
            for dy in (0, 1):
                piece = density[1 - dz : 1 - dz + depth, 1 - dx : 1 - dx + width, :]
                if dy:
                    piece = jnp.roll(piece, 1, axis=2)
                total = total + piece
    return total * 0.125 + lumped_extra


def element_forces(padded_u, cells, stiff_both, thermal_g):
    width = cells.shape[2] - 1
    length = cells.shape[3]
    depth = cells.shape[1] - 1
    start = jnp.zeros(padded_u.shape, jnp.float32)

    def slab(k, total):
        rows = lax.dynamic_slice_in_dim(padded_u, k, 2, 1)
        cell = lax.dynamic_slice_in_dim(cells, k, 1, 1)[:, 0].reshape(4, -1)
        corners = []
        for dz in (0, 1):
            for dx in (0, 1):
                for dy in (0, 1):
                    piece = rows[:, dz, dx : dx + width + 1, :]
                    if dy:
                        piece = jnp.roll(piece, -1, axis=2)
                    corners.append(piece)
        cell_disp = jnp.stack(corners, 1).reshape(24, -1)
        stacked = jnp.concatenate([cell_disp * cell[0], cell_disp * cell[1]], 0)
        inner = jnp.dot(
            stiff_both, stacked, precision=lax.Precision.HIGHEST, preferred_element_type=jnp.float32
        )
        cell_force = (thermal_g[:, None] * cell[2] - inner).reshape(3, 8, width + 1, length)
        contrib = jnp.zeros((3, 2, width + 2, length), jnp.float32)
        corner = 0
        for dz in (0, 1):
            for dx in (0, 1):
                for dy in (0, 1):
                    value = cell_force[:, corner]
                    if dy:
                        value = jnp.roll(value, 1, axis=2)
                    contrib = contrib.at[:, dz, dx : dx + width + 1, :].add(value)
                    corner = corner + 1
        old = lax.dynamic_slice_in_dim(total, k, 2, 1)
        return lax.dynamic_update_slice_in_dim(total, old + contrib, k, 1)

    return lax.fori_loop(0, depth + 1, slab, start)


def local(
    nodal_motion_vector,
    nodal_speed_vector,
    element_heating_increment,
    element_medium_label,
    medium_parameter_matrix,
    solder_vertex_position,
    landing_vertex_position,
    link_spring_coefficient,
    active_link_tally,
):
    depth, width, length = (
        nodal_motion_vector.shape[1],
        nodal_motion_vector.shape[2],
        nodal_motion_vector.shape[3],
    )
    stiff_both, thermal_g = element_tables()
    parameter_entries = element_medium_entries(
        element_medium_label, medium_parameter_matrix, element_heating_increment
    )
    below = shifted(parameter_entries[:, depth - 1 : depth], "layer", 1)
    with_below = jnp.concatenate([below, parameter_entries], 1)
    behind = shifted(with_below[:, :, width - 1 : width], "plane", 1)
    cells = jnp.concatenate([behind, with_below], 2)
    gap_z = lax.axis_size("layer") // 2 * depth + depth // 2 - 1
    mask = cell_mask(
        lax.axis_index("layer") * depth,
        lax.axis_index("plane") * width,
        depth * lax.axis_size("layer"),
        width * lax.axis_size("plane"),
        depth,
        width,
        length,
        gap_z,
    )
    cells = cells * mask[None]
    masses = node_mass(cells)
    band = solder_vertex_position.shape[1]
    half = band // 2
    bump_local = solder_vertex_position.reshape(band, -1)
    pad_local = landing_vertex_position.reshape(band, -1)
    capacity = bump_local.shape[1]
    counts = active_link_tally.reshape(band)
    stiff_all = link_spring_coefficient.reshape(band, capacity)
    here = lax.axis_index("plane")
    blocks = lax.axis_size("plane")
    bump_z = depth // 2
    on_face = (lax.axis_index("layer") == lax.axis_size("layer") // 2).astype(jnp.float32)
    stiff_list = []
    request_list = []
    for k in range(band):
        offset = k - half
        target = here + offset
        valid = (target >= 0) & (target < blocks)
        live = (jnp.arange(capacity) < counts[k]) & valid
        stiff_k = jnp.where(live, stiff_all[k], jnp.float32(0.0))
        stiff_list.append(stiff_k)
        if offset == 0:
            request_list.append(pad_local[k])
        else:
            request_list.append(shifted(pad_local[k], "plane", offset))
    for step in range(STEPS):
        padded = with_halo(nodal_motion_vector, (("plane", 2), ("layer", 1)), 1)
        forces = element_forces(padded, cells, stiff_both, thermal_g)[:, 1:-1, 1:-1, :]
        bump_face = nodal_motion_vector[:, bump_z].reshape(3, -1)
        pad_face = nodal_motion_vector[:, bump_z - 1].reshape(3, -1)
        bump_total = jnp.zeros(bump_face.shape, jnp.float32)
        pad_total = jnp.zeros(pad_face.shape, jnp.float32)
        for contact_k in range(band):
            contact_offset = contact_k - half
            requests = request_list[contact_k]
            pad_values = pad_face[:, requests]
            own_values = bump_face[:, bump_local[contact_k]]
            if contact_offset == 0:
                got_pad = pad_values
            else:
                got_pad = shifted(pad_values, "plane", -contact_offset)
            spring_own = stiff_list[contact_k] * (got_pad - own_values)
            if contact_offset == 0:
                spring_pad = spring_own
            else:
                spring_pad = shifted(spring_own, "plane", contact_offset)
            bump_total = bump_total.at[:, bump_local[contact_k]].add(spring_own)
            pad_total = pad_total.at[:, requests].add(-spring_pad)
        contact = jnp.zeros(nodal_motion_vector.shape, jnp.float32)
        contact = contact.at[:, bump_z].set(bump_total.reshape(3, width, length))
        contact = contact.at[:, bump_z - 1].set(pad_total.reshape(3, width, length))
        forces = forces + contact * on_face
        nodal_speed_vector = nodal_speed_vector + time_step * forces / masses
        nodal_motion_vector = nodal_motion_vector + time_step * nodal_speed_vector
    return (nodal_motion_vector, nodal_speed_vector)


def solution(mesh):
    in_specs = (
        P(None, "layer", "plane", None),
        P(None, "layer", "plane", None),
        P("layer", "plane", None),
        P("layer", "plane", None),
        P(),
        P("plane", None, None),
        P("plane", None, None),
        P("plane", None, None),
        P("plane", None),
    )
    out_specs = (P(None, "layer", "plane", None), P(None, "layer", "plane", None))
    return jax.shard_map(local, mesh=mesh, in_specs=in_specs, out_specs=out_specs, check_vma=False)
```

profile of v0, /device:TPU:249, one launch (start us, length us, event | category | flops | bytes accessed | tf_op | source)
XLA Modules:
  0.0 430.7 jit_solution(14288059192519203859)
XLA Ops:
  1.4 4.4 %collective-permute-start.12 = (s32[128]{0:T(128)S(1)}, s32[128]{0:T(128)S(1)}, u32[]{:S(2)}, u32[]{:S(2)}) collective-permute-start(s32[128]{0:T(128)S(1)} %get-tuple-element.917), channel_id=1, source_target_pairs={{0,8},{4,12},{8,16},{12,20},{16,24},{20,28},{24,32},{28,36},{32,40... | collective-permute-start | bytes 1544 | tf_op jit(solution)/shard_map/ppermute | solution.py:19
  5.8 2.9 collective-permute-start.8
  10.6 6.9 %collective-permute-start.10 = (s32[128]{0:T(128)S(1)}, s32[128]{0:T(128)S(1)}, u32[]{:S(2)}, u32[]{:S(2)}) collective-permute-start(s32[128]{0:T(128)S(1)} %get-tuple-element.920), channel_id=1, source_target_pairs={{0,4},{4,8},{8,12},{12,16},{16,20},{20,24},{24,28},{28,32},{32,36}... | collective-permute-start | bytes 1544 | tf_op jit(solution)/shard_map/ppermute | solution.py:19
  28.2 3.1 and_select_fusion
  39.5 3.0 collective-permute-start.9
  53.5 3.0 collective-permute-start.13
  56.6 3.1 collective-permute-start.15
  61.9 6.9 %collective-permute-start.16 = (f32[3,128]{0,1:T(8,128)S(1)}, f32[3,128]{0,1:T(8,128)S(1)}, u32[]{:S(2)}, u32[]{:S(2)}) collective-permute-start(f32[3,128]{0,1:T(8,128)S(1)} %fusion.77), channel_id=1, source_target_pairs={{0,4},{4,8},{8,12},{12,16},{16,20},{20,24},{24,28},{28,32},{32,36}... | collective-permute-start | bytes 4616 | tf_op jit(solution)/shard_map/ppermute | solution.py:19
  68.9 2.8 collective-permute-start.17
  88.9 3.7 collective-permute-start
  103.3 2.5 collective-permute-start.4
  107.9 7.7 %collective-permute-start.1 = (f32[4,9,1,256]{3,2,1,0:T(1,128)S(1)}, f32[4,9,1,256]{3,2,1,0:T(1,128)S(1)}, u32[]{:S(2)}, u32[]{:S(2)}) collective-permute-start(f32[4,9,1,256]{3,2,1,0:T(1,128)S(1)} %pad_maximum_fusion.10), channel_id=1, source_target_pairs={{0,4},{4,8},{8,12},{12,16},{16,20},{20,24},{24,28},{28,32},{32,36}... | collective-permute-start | bytes 110600 | tf_op jit(solution)/shard_map/ppermute | solution.py:19
  119.5 104.0 %while.54 = (s32[]{:T(128)}, f32[3,10,18,256]{3,2,1,0:T(8,128)S(1)}, f32[4,9,17,256]{3,2,1,0:T(8,128)}, f32[3,10,18,256]{3,2,0,1:T(8,128)S(1)}, s32[]{:T(128)}, ...) while((s32[]{:T(128)}, ...), condition=%wide.region_1.2_spmd.clone, body=%wide.region_0.1_spmd.sunk.clone.sunk | while | flops 60907780 | bytes 8993233 | solution.py:157
  227.6 7.5 %collective-permute-start.23 = (f32[3,128]{0,1:T(8,128)}, f32[3,128]{0,1:T(8,128)S(1)}, u32[]{:S(2)}, u32[]{:S(2)}) collective-permute-start(f32[3,128]{0,1:T(8,128)} %bitcast.54), channel_id=1, source_target_pairs={{0,4},{4,8},{8,12},{12,16},{16,20},{20,24},{24,28},{28,32},{32,36}... | collective-permute-start | bytes 4616 | tf_op jit(solution)/shard_map/ppermute | solution.py:19
  240.1 2.9 gather_fusion.17
  253.7 2.4 collective-permute-start.19
  258.1 6.9 %collective-permute-start.24 = (f32[3,128]{0,1:T(8,128)}, f32[3,128]{0,1:T(8,128)S(1)}, u32[]{:S(2)}, u32[]{:S(2)}) collective-permute-start(f32[3,128]{0,1:T(8,128)} %bitcast.427), channel_id=1, source_target_pairs={{4,0},{8,4},{12,8},{16,12},{20,16},{24,20},{28,24},{32,28},{36,32}... | collective-permute-start | bytes 4616 | tf_op jit(solution)/shard_map/ppermute | solution.py:19
  274.7 5.6 %collective-permute-start.28 = (f32[3,128]{0,1:T(8,128)S(1)}, f32[3,128]{0,1:T(8,128)}, u32[]{:S(2)}, u32[]{:S(2)}) collective-permute-start(f32[3,128]{0,1:T(8,128)S(1)} %fusion.59), channel_id=1, source_target_pairs={{0,4},{4,8},{8,12},{12,16},{16,20},{20,24},{24,28},{28,32},{32,36}... | collective-permute-start | bytes 4616 | tf_op jit(solution)/shard_map/ppermute | solution.py:19
  281.7 3.6 collective-permute-start.29
  306.2 2.4 scatter_custom_fusion.17
  314.7 4.3 collective-permute-start.20
  321.0 3.9 collective-permute-done.21
  325.9 102.4 %while.55 = (s32[]{:T(128)}, f32[3,10,18,256]{3,2,1,0:T(8,128)S(1)}, f32[4,9,17,256]{3,2,1,0:T(8,128)}, f32[3,10,18,256]{3,2,1,0:T(8,128)S(1)}, s32[]{:T(128)}, ...) while((s32[]{:T(128)}, ...), condition=%wide.region_13.14_spmd.clone, body=%wide.region_12.13_spmd.sunk.clone.sunk | while | flops 60907780 | bytes 8968665 | solution.py:157
  428.3 2.4 multiply_add_fusion
  (1082 shorter events, 332.1 us)
Async XLA Ops:
  1.4 35.2 %collective-permute-start.12 = (s32[128]{0:T(128)S(1)}, s32[128]{0:T(128)S(1)}, u32[]{:S(2)}, u32[]{:S(2)}) collective-permute-start(s32[128]{0:T(128)S(1)} %get-tuple-element.917), channel_id=1, source_target_pairs={{0,8},{4,12},{8,16},{12,20},{16,24},{20,28},{24,32},{28,36},{32,40... | collective-permute-start | bytes 1544 | tf_op jit(solution)/shard_map/ppermute | solution.py:19
  5.8 30.8 %collective-permute-start.8 = (s32[128]{0:T(128)S(1)}, s32[128]{0:T(128)S(1)}, u32[]{:S(2)}, u32[]{:S(2)}) collective-permute-start(s32[128]{0:T(128)S(1)} %get-tuple-element.918), channel_id=1, source_target_pairs={{4,0},{8,4},{12,8},{16,12},{20,16},{24,20},{28,24},{32,28},{36,32}... | collective-permute-start | bytes 1544 | tf_op jit(solution)/shard_map/ppermute | solution.py:19
  8.7 28.0 %collective-permute-start.6 = (s32[128]{0:T(128)S(1)}, s32[128]{0:T(128)S(1)}, u32[]{:S(2)}, u32[]{:S(2)}) collective-permute-start(s32[128]{0:T(128)S(1)} %get-tuple-element.919), channel_id=1, source_target_pairs={{8,0},{12,4},{16,8},{20,12},{24,16},{28,20},{32,24},{36,28},{40,32... | collective-permute-start | bytes 1544 | tf_op jit(solution)/shard_map/ppermute | solution.py:19
  10.6 31.8 %collective-permute-start.10 = (s32[128]{0:T(128)S(1)}, s32[128]{0:T(128)S(1)}, u32[]{:S(2)}, u32[]{:S(2)}) collective-permute-start(s32[128]{0:T(128)S(1)} %get-tuple-element.920), channel_id=1, source_target_pairs={{0,4},{4,8},{8,12},{12,16},{16,20},{20,24},{24,28},{28,32},{32,36}... | collective-permute-start | bytes 1544 | tf_op jit(solution)/shard_map/ppermute | solution.py:19
  19.2 83.1 %collective-permute-start.2 = (f32[3,8,1,256]{3,2,0,1:T(1,128)}, f32[3,8,1,256]{3,2,0,1:T(1,128)}, u32[]{:S(2)}, u32[]{:S(2)}) collective-permute-start(f32[3,8,1,256]{3,2,0,1:T(1,128)} %get-tuple-element.896), channel_id=1, source_target_pairs={{0,4},{4,8},{8,12},{12,16},{16,20},{20,24},{24,28},{28,32},{32,36}... | collective-permute-start | bytes 73736 | tf_op jit(solution)/shard_map/ppermute | solution.py:27
  39.5 17.0 %collective-permute-start.9 = (f32[3,128]{0,1:T(8,128)S(1)}, f32[3,128]{0,1:T(8,128)S(1)}, u32[]{:S(2)}, u32[]{:S(2)}) collective-permute-start(f32[3,128]{0,1:T(8,128)S(1)} %bitcast.430), channel_id=1, source_target_pairs={{0,4},{4,8},{8,12},{12,16},{16,20},{20,24},{24,28},{28,32},{32,36}... | collective-permute-start | bytes 4616 | tf_op jit(solution)/shard_map/ppermute | solution.py:19
  51.2 10.6 %collective-permute-start.11 = (f32[3,128]{0,1:T(8,128)S(1)}, f32[3,128]{0,1:T(8,128)S(1)}, u32[]{:S(2)}, u32[]{:S(2)}) collective-permute-start(f32[3,128]{0,1:T(8,128)S(1)} %bitcast.428), channel_id=1, source_target_pairs={{4,0},{8,4},{12,8},{16,12},{20,16},{24,20},{28,24},{32,28},{36,32}... | collective-permute-start | bytes 4616 | tf_op jit(solution)/shard_map/ppermute | solution.py:19
  53.5 15.3 %collective-permute-start.13 = (f32[3,128]{0,1:T(8,128)S(1)}, f32[3,128]{0,1:T(8,128)S(1)}, u32[]{:S(2)}, u32[]{:S(2)}) collective-permute-start(f32[3,128]{0,1:T(8,128)S(1)} %bitcast.426), channel_id=1, source_target_pairs={{8,0},{12,4},{16,8},{20,12},{24,16},{28,20},{32,24},{36,28},{40,32... | collective-permute-start | bytes 4616 | tf_op jit(solution)/shard_map/ppermute | solution.py:19
  56.6 32.3 %collective-permute-start.15 = (f32[3,128]{0,1:T(8,128)S(1)}, f32[3,128]{0,1:T(8,128)}, u32[]{:S(2)}, u32[]{:S(2)}) collective-permute-start(f32[3,128]{0,1:T(8,128)S(1)} %fusion.80), channel_id=1, source_target_pairs={{4,0},{8,4},{12,8},{16,12},{20,16},{24,20},{28,24},{32,28},{36,32}... | collective-permute-start | bytes 4616 | tf_op jit(solution)/shard_map/ppermute | solution.py:19
  59.9 25.2 %collective-permute-start.14 = (f32[3,128]{0,1:T(8,128)S(1)}, f32[3,128]{0,1:T(8,128)}, u32[]{:S(2)}, u32[]{:S(2)}) collective-permute-start(f32[3,128]{0,1:T(8,128)S(1)} %fusion.82), channel_id=1, source_target_pairs={{8,0},{12,4},{16,8},{20,12},{24,16},{28,20},{32,24},{36,28},{40,32... | collective-permute-start | bytes 4616 | tf_op jit(solution)/shard_map/ppermute | solution.py:19
  61.9 35.3 %collective-permute-start.16 = (f32[3,128]{0,1:T(8,128)S(1)}, f32[3,128]{0,1:T(8,128)S(1)}, u32[]{:S(2)}, u32[]{:S(2)}) collective-permute-start(f32[3,128]{0,1:T(8,128)S(1)} %fusion.77), channel_id=1, source_target_pairs={{0,4},{4,8},{8,12},{12,16},{16,20},{20,24},{24,28},{28,32},{32,36}... | collective-permute-start | bytes 4616 | tf_op jit(solution)/shard_map/ppermute | solution.py:19
  68.9 30.5 %collective-permute-start.17 = (f32[3,128]{0,1:T(8,128)S(1)}, f32[3,128]{0,1:T(8,128)}, u32[]{:S(2)}, u32[]{:S(2)}) collective-permute-start(f32[3,128]{0,1:T(8,128)S(1)} %fusion.74), channel_id=1, source_target_pairs={{0,8},{4,12},{8,16},{12,20},{16,24},{20,28},{24,32},{28,36},{32,40... | collective-permute-start | bytes 4616 | tf_op jit(solution)/shard_map/ppermute | solution.py:19
  85.1 17.3 %collective-permute-start.3 = (f32[3,8,1,256]{3,2,0,1:T(1,128)}, f32[3,8,1,256]{3,2,0,1:T(1,128)}, u32[]{:S(2)}, u32[]{:S(2)}) collective-permute-start(f32[3,8,1,256]{3,2,0,1:T(1,128)} %get-tuple-element.897), channel_id=1, source_target_pairs={{4,0},{8,4},{12,8},{16,12},{20,16},{24,20},{28,24},{32,28},{36,32}... | collective-permute-start | bytes 73736 | tf_op jit(solution)/shard_map/ppermute | solution.py:30
  88.9 18.3 %collective-permute-start = (f32[4,1,16,256]{3,2,1,0:T(8,128)}, f32[4,1,16,256]{3,2,1,0:T(8,128)}, u32[]{:S(2)}, u32[]{:S(2)}) collective-permute-start(f32[4,1,16,256]{3,2,1,0:T(8,128)} %pad_maximum_fusion.8), channel_id=1, source_target_pairs={{0,1},{1,2},{2,3},{4,5},{5,6},{6,7},{8,9},{9,10},{10,11},{12,13},{... | collective-permute-start | bytes 196616 | tf_op jit(solution)/shard_map/ppermute | solution.py:19
  103.3 12.3 %collective-permute-start.4 = (f32[3,1,18,256]{3,2,0,1:T(8,128)S(1)}, f32[3,1,18,256]{3,2,0,1:T(8,128)S(1)}, u32[]{:S(2)}, u32[]{:S(2)}) collective-permute-start(f32[3,1,18,256]{3,2,0,1:T(8,128)S(1)} %get-tuple-element.890), channel_id=1, source_target_pairs={{0,1},{1,2},{2,3},{4,5},{5,6},{6,7},{8,9},{9,10},{10,11},{12,13},{... | collective-permute-start | bytes 165896 | tf_op jit(solution)/shard_map/ppermute | solution.py:27
  227.6 37.3 %collective-permute-start.23 = (f32[3,128]{0,1:T(8,128)}, f32[3,128]{0,1:T(8,128)S(1)}, u32[]{:S(2)}, u32[]{:S(2)}) collective-permute-start(f32[3,128]{0,1:T(8,128)} %bitcast.54), channel_id=1, source_target_pairs={{0,4},{4,8},{8,12},{12,16},{16,20},{20,24},{24,28},{28,32},{32,36}... | collective-permute-start | bytes 4616 | tf_op jit(solution)/shard_map/ppermute | solution.py:19
  251.8 62.2 %collective-permute-start.18 = (f32[3,8,1,256]{3,2,1,0:T(1,128)}, f32[3,8,1,256]{3,2,1,0:T(1,128)S(1)}, u32[]{:S(2)}, u32[]{:S(2)}) collective-permute-start(f32[3,8,1,256]{3,2,1,0:T(1,128)} %get-tuple-element.892), channel_id=1, source_target_pairs={{0,4},{4,8},{8,12},{12,16},{16,20},{20,24},{24,28},{28,32},{32,36}... | collective-permute-start | bytes 73736 | tf_op jit(solution)/shard_map/ppermute | solution.py:27
  253.7 60.3 %collective-permute-start.19 = (f32[3,8,1,256]{3,2,1,0:T(1,128)}, f32[3,8,1,256]{3,2,1,0:T(1,128)}, u32[]{:S(2)}, u32[]{:S(2)}) collective-permute-start(f32[3,8,1,256]{3,2,1,0:T(1,128)} %get-tuple-element.893), channel_id=1, source_target_pairs={{4,0},{8,4},{12,8},{16,12},{20,16},{24,20},{28,24},{32,28},{36,32}... | collective-permute-start | bytes 73736 | tf_op jit(solution)/shard_map/ppermute | solution.py:30
  256.1 12.3 %collective-permute-start.22 = (f32[3,128]{0,1:T(8,128)}, f32[3,128]{0,1:T(8,128)S(1)}, u32[]{:S(2)}, u32[]{:S(2)}) collective-permute-start(f32[3,128]{0,1:T(8,128)} %bitcast.429), channel_id=1, source_target_pairs={{0,8},{4,12},{8,16},{12,20},{16,24},{20,28},{24,32},{28,36},{32,40... | collective-permute-start | bytes 4616 | tf_op jit(solution)/shard_map/ppermute | solution.py:19
  258.1 12.4 %collective-permute-start.24 = (f32[3,128]{0,1:T(8,128)}, f32[3,128]{0,1:T(8,128)S(1)}, u32[]{:S(2)}, u32[]{:S(2)}) collective-permute-start(f32[3,128]{0,1:T(8,128)} %bitcast.427), channel_id=1, source_target_pairs={{4,0},{8,4},{12,8},{16,12},{20,16},{24,20},{28,24},{32,28},{36,32}... | collective-permute-start | bytes 4616 | tf_op jit(solution)/shard_map/ppermute | solution.py:19
  268.4 35.4 %collective-permute-start.27 = (f32[3,128]{0,1:T(8,128)S(1)}, f32[3,128]{0,1:T(8,128)}, u32[]{:S(2)}, u32[]{:S(2)}) collective-permute-start(f32[3,128]{0,1:T(8,128)S(1)} %fusion.62), channel_id=1, source_target_pairs={{4,0},{8,4},{12,8},{16,12},{20,16},{24,20},{28,24},{32,28},{36,32}... | collective-permute-start | bytes 4616 | tf_op jit(solution)/shard_map/ppermute | solution.py:19
  270.5 10.6 %collective-permute-start.26 = (f32[3,128]{0,1:T(8,128)S(1)}, f32[3,128]{0,1:T(8,128)S(1)}, u32[]{:S(2)}, u32[]{:S(2)}) collective-permute-start(f32[3,128]{0,1:T(8,128)S(1)} %fusion.64), channel_id=1, source_target_pairs={{8,0},{12,4},{16,8},{20,12},{24,16},{28,20},{32,24},{36,28},{40,32... | collective-permute-start | bytes 4616 | tf_op jit(solution)/shard_map/ppermute | solution.py:19
  274.7 33.9 %collective-permute-start.28 = (f32[3,128]{0,1:T(8,128)S(1)}, f32[3,128]{0,1:T(8,128)}, u32[]{:S(2)}, u32[]{:S(2)}) collective-permute-start(f32[3,128]{0,1:T(8,128)S(1)} %fusion.59), channel_id=1, source_target_pairs={{0,4},{4,8},{8,12},{12,16},{16,20},{20,24},{24,28},{28,32},{32,36}... | collective-permute-start | bytes 4616 | tf_op jit(solution)/shard_map/ppermute | solution.py:19
  281.7 29.3 %collective-permute-start.29 = (f32[3,128]{0,1:T(8,128)}, f32[3,128]{0,1:T(8,128)}, u32[]{:S(2)}, u32[]{:S(2)}) collective-permute-start(f32[3,128]{0,1:T(8,128)} %fusion.56), channel_id=1, source_target_pairs={{0,8},{4,12},{8,16},{12,20},{16,24},{20,28},{24,32},{28,36},{32,40... | collective-permute-start | bytes 4616 | tf_op jit(solution)/shard_map/ppermute | solution.py:19
  (55 other events, 1528.8 us)
where the time goes:
time: 436 us; the launch traced here: 431 us
  local copies, waits for them, and re-layouts  177 us (41%)
  other arithmetic  122 us (28%)
  starting transfers between devices  101 us (23%)
  matrix products  18.1 us (4%)
  waiting for transfers between devices  5.46 us (1%)
  loops' own time  4.58 us (1%)
    ppermute x22, starting transfers between devices, shifted(): lax.ppermute(value, axis, [(source, source + steps) for source in range(l...  83.6 us
    scatter-add x144, local copies, waits for them, and re-layouts, slab(): contrib = contrib.at[:, dz, dx:dx + width + 1, :].add(value)  76.8 us
    add x90, other arithmetic, slab(): contrib = contrib.at[:, dz, dx:dx + width + 1, :].add(value)  54 us
    scatter-add x10, other arithmetic, local(): pad_total = pad_total.at[:, requests].add(-spring_pad)  22.1 us
    scatter-add x10, other arithmetic, local(): bump_total = bump_total.at[:, bump_local[contact_k]].add(spring_own)  20.3 us
    dot_general x36, matrix products, slab(): jnp.dot(stiff_both, stacked, precision=lax.Precision.HIGHEST, preferred_e...  18.1 us
    gather x10, local copies, waits for them, and re-layouts, local(): pad_values = pad_face[:, requests]  17.4 us
    gather x10, local copies, waits for them, and re-layouts, local(): own_values = bump_face[:, bump_local[contact_k]]  15.6 us
  transfers between devices with their start and end apart: 30, of which 3 were waited for; matrix products, arithmetic and copies ran while one was open for 24% of the time, Pallas kernels for 0%

commit v1 on v0

v1 whole, which is shorter than its diff:
```python
import functools

import jax
import jax.numpy as jnp
from jax import lax
from jax.experimental import pallas as pl
from jax.experimental.pallas import tpu as pltpu
from jax.sharding import PartitionSpec as P

DT = 0.05
LUMPED = 0.25
F32 = jnp.float32
BF16 = jnp.bfloat16
QUADS = ((0, 0), (0, 1), (1, 0), (1, 1))

COL_U, COL_LAB, COL_DT, LISTS, FACES, R1_ROWS = 0, 24, 32, 40, 48, 144
R2_LISTS, R2_FACES, R2_ROWS = 0, 8, 104
ZU_U, ZU_V, ZU_LAB, ZU_DT, ZU_CL, ZU_CH, ZU_CLAB, ZU_CDT, ZU_ROWS = 0, 96, 144, 176, 208, 214, 220, 222, 224
ZD_U, ZD_V, ZD_LAB, ZD_DT, ZD_CL, ZD_CH, ZD_CLAB, ZD_CDT, ZD_ROWS = 0, 96, 144, 160, 176, 182, 188, 189, 192
S1_ROWS, S1_VALS = 40, 32


def iota(shape, dim):
    return lax.broadcasted_iota(jnp.int32, shape, dim)


def masked_stiffness(k, half, stiff_ref, tally_ref, blocks):
    target = lax.axis_index("plane") + (k - half)
    valid = (target >= 0) & (target < blocks)
    count = jnp.where(valid, tally_ref[0, k], 0)
    row = stiff_ref[0, k : k + 1, :]
    return jnp.where(iota(row.shape, 1) < count, row, 0.0)


def pack_plane(blocks, u, dt, lab, sol, land, stiff, tally, up, dn, up2, dn2):
    pad_z = u.shape[1] // 2 - 1
    for out, x in ((up, 15), (dn, 0)):
        for c in range(3):
            out[COL_U + 8 * c : COL_U + 8 * c + 8, :] = u[c, :, x, :]
        out[COL_LAB : COL_LAB + 8, :] = lab[:, x, :].astype(F32)
        out[COL_DT : COL_DT + 8, :] = dt[:, x, :]
    for out, k, lists, faces in (
        (up, 3, LISTS, FACES),
        (dn, 1, LISTS, FACES),
        (up2, 4, R2_LISTS, R2_FACES),
        (dn2, 0, R2_LISTS, R2_FACES),
    ):
        out[lists : lists + 8, :] = jnp.zeros((8, 256), F32)
        out[lists : lists + 1, 0:128] = sol[0, k : k + 1, :].astype(F32)
        out[lists + 1 : lists + 2, 0:128] = land[0, k : k + 1, :].astype(F32)
        out[lists + 2 : lists + 3, 0:128] = masked_stiffness(k, 2, stiff, tally, blocks)
        for c in range(3):
            for face in (0, 1):
                row = faces + 48 * face + 16 * c
                out[row : row + 16, :] = u[c, pad_z + face]


def pack_layer(u, v, dt, lab, lo, hi, up, dn):
    for c in range(3):
        for zz in (0, 1):
            row = 16 * (2 * c + zz)
            up[ZU_U + row : ZU_U + row + 16, :] = u[c, 6 + zz]
            dn[ZD_U + row : ZD_U + row + 16, :] = u[c, zz]
        up[ZU_V + 16 * c : ZU_V + 16 * c + 16, :] = v[c, 7]
        dn[ZD_V + 16 * c : ZD_V + 16 * c + 16, :] = v[c, 0]
        row = COL_U + 8 * c
        up[ZU_CL + 2 * c : ZU_CL + 2 * c + 2, :] = lo[row + 6 : row + 8, :]
        up[ZU_CH + 2 * c : ZU_CH + 2 * c + 2, :] = hi[row + 6 : row + 8, :]
        dn[ZD_CL + 2 * c : ZD_CL + 2 * c + 2, :] = lo[row : row + 2, :]
        dn[ZD_CH + 2 * c : ZD_CH + 2 * c + 2, :] = hi[row : row + 2, :]
    for zz in (0, 1):
        up[ZU_LAB + 16 * zz : ZU_LAB + 16 * zz + 16, :] = lab[6 + zz].astype(F32)
        up[ZU_DT + 16 * zz : ZU_DT + 16 * zz + 16, :] = dt[6 + zz]
    up[ZU_CLAB : ZU_CLAB + 2, :] = lo[COL_LAB + 6 : COL_LAB + 8, :]
    up[ZU_CDT : ZU_CDT + 2, :] = lo[COL_DT + 6 : COL_DT + 8, :]
    dn[ZD_LAB : ZD_LAB + 16, :] = lab[0].astype(F32)
    dn[ZD_DT : ZD_DT + 16, :] = dt[0]
    dn[ZD_CLAB : ZD_CLAB + 1, :] = lo[COL_LAB : COL_LAB + 1, :]
    dn[ZD_CDT : ZD_CDT + 1, :] = lo[COL_DT : COL_DT + 1, :]
    dn[ZD_CDT + 1 : ZD_ROWS, :] = jnp.zeros((ZD_ROWS - ZD_CDT - 1, 256), F32)


def material_scalars(par):
    out = []
    for m in range(4):
        lam, mu, alpha, rho = par[0, m], par[1, m], par[2, m], par[3, m]
        out.append(
            (
                lam * (1.0 / 16.0),
                mu * (1.0 / 16.0),
                (lam + 4.0 * mu) * (1.0 / 144.0),
                (3.0 * lam + 2.0 * mu) * alpha * 0.25,
                rho * 0.125,
            )
        )
    return out


def cell_fields(mats, lab, dt, mask, with_mass):
    is0, is1, is2 = lab == 0.0, lab == 1.0, lab == 2.0

    def pick(i):
        rest = jnp.where(is2, mats[2][i], mats[3][i])
        return jnp.where(is0, mats[0][i], jnp.where(is1, mats[1][i], rest)) * mask

    return pick(0), pick(1), pick(2), pick(3) * dt, pick(4) if with_mass else None


def plane_modes(u, ux):
    s, d = u + ux, ux - u
    sy, dy = pltpu.roll(s, 255, 1), pltpu.roll(d, 255, 1)
    return [s + sy, sy - s, d + dy, dy - d]


def cell_forces(lower, upper, l1, m1, k3, th):
    z, x, y = (
        {
            (i, j, k): (upper[c][q] - lower[c][q]) if i else (upper[c][q] + lower[c][q])
            for q, (j, k) in enumerate(QUADS)
            for i in (0, 1)
            if i + j + k
        }
        for c in range(3)
    )
    l2, m2 = l1 * (1.0 / 3.0), m1 * (1.0 / 3.0)
    p0 = l1 * (z[1, 0, 0] + x[0, 1, 0] + y[0, 0, 1]) - th
    m1x2 = m1 + m1
    zx = m1 * (x[1, 0, 0] + z[0, 1, 0])
    zy = m1 * (y[1, 0, 0] + z[0, 0, 1])
    xy = m1 * (y[0, 1, 0] + x[0, 0, 1])
    pz = l2 * (x[1, 1, 0] + y[1, 0, 1])
    px = l2 * (z[1, 1, 0] + y[0, 1, 1])
    py = l2 * (z[1, 0, 1] + x[0, 1, 1])
    tw = z[0, 1, 1] + x[1, 0, 1] + y[1, 1, 0]
    fz = {
        (1, 0, 0): p0 + m1x2 * z[1, 0, 0],
        (0, 1, 0): zx,
        (0, 0, 1): zy,
        (1, 1, 0): px + m1 * z[1, 1, 0],
        (1, 0, 1): py + m1 * z[1, 0, 1],
        (0, 1, 1): m2 * (tw + z[0, 1, 1]),
        (1, 1, 1): k3 * z[1, 1, 1],
    }
    fx = {
        (0, 1, 0): p0 + m1x2 * x[0, 1, 0],
        (1, 0, 0): zx,
        (0, 0, 1): xy,
        (1, 1, 0): pz + m1 * x[1, 1, 0],
        (0, 1, 1): py + m1 * x[0, 1, 1],
        (1, 0, 1): m2 * (tw + x[1, 0, 1]),
        (1, 1, 1): k3 * x[1, 1, 1],
    }
    fy = {
        (0, 0, 1): p0 + m1x2 * y[0, 0, 1],
        (1, 0, 0): zy,
        (0, 1, 0): xy,
        (1, 0, 1): pz + m1 * y[1, 0, 1],
        (0, 1, 1): px + m1 * y[0, 1, 1],
        (1, 1, 0): m2 * (tw + y[1, 1, 0]),
        (1, 1, 1): k3 * y[1, 1, 1],
    }
    low, high = [], []
    for f in (fz, fx, fy):
        low_c, high_c = [], []
        for j, k in QUADS:
            d = f[1, j, k]
            if j + k:
                s = f[0, j, k]
                low_c.append(s - d)
                high_c.append(s + d)
            else:
                low_c.append(-d)
                high_c.append(d)
        low.append(low_c)
        high.append(high_c)
    return low, high


def fold_y(a, b):
    return (a - b) + pltpu.roll(a + b, 1, 1)


def column_forces(blocks, layers, zbase, mats, col_lo, col_own, col_lab, col_dt, col_f, col_m):
    rows = col_lab.shape[0]
    shape = (rows, 256)
    zg = iota(shape, 0) + zbase
    gap = layers // 2 * 8 + 3
    ok = (zg >= 0) & (zg <= layers * 8 - 2) & (zg != gap) & (iota(shape, 1) < 255)
    mask = jnp.where(ok & (lax.axis_index("plane") > 0), 1.0, 0.0)
    l1, m1, k3, th, rho = cell_fields(mats, col_lab[...], col_dt[...], mask, col_m is not None)
    lower = [plane_modes(col_lo[c], col_own[c]) for c in range(3)]
    upper = [[pltpu.roll(a, rows - 1, 0) for a in comp] for comp in lower]
    low, high = cell_forces(lower, upper, l1, m1, k3, th)
    for c in range(3):
        node = [low[c][q] + pltpu.roll(high[c][q], 1, 0) for q in range(4)]
        col_f[c] = fold_y(node[0], node[1]) + fold_y(node[2], node[3])
    if col_m is not None:
        rho = rho + pltpu.roll(rho, 1, 1)
        col_m[...] = rho + pltpu.roll(rho, 1, 0)


def elastic_steps(
    blocks, layers, cells, zbase, mats, u, lab, dt, col_hi, col_f, col_m, modes, saved, saved_m, finish
):
    shape = (16, 256)
    row, lane = iota(shape, 0), iota(shape, 1)
    last = jnp.where(lax.axis_index("plane") == blocks - 1, 15, 16)
    in_plane = jnp.where((lane < 255) & (row < last), 1.0, 0.0)
    gap = layers // 2 * 8 + 3
    first_row, last_row = row == 0, row == 15

    def forward(e, c):
        a = u[c, e]
        halo = jnp.broadcast_to(col_hi[c, pl.ds(e, 1), :], shape)
        return plane_modes(a, jnp.where(last_row, halo, pltpu.roll(a, 15, 0)))

    for c in range(3):
        for q, value in enumerate(forward(0, c)):
            modes[4 * c + q] = value

    def body(e, carry):
        zg = zbase + e
        ok = (zg >= 0) & (zg <= layers * 8 - 2) & (zg != gap)
        scale = jnp.where(ok, 1.0, 0.0)
        l1, m1, k3, th, rho = cell_fields(mats, lab[e], dt[e], in_plane * scale, col_m is not None)
        lower = [[modes[4 * c + q] for q in range(4)] for c in range(3)]
        upper = [forward(e + 1, c) for c in range(3)]
        for c in range(3):
            for q in range(4):
                modes[4 * c + q] = upper[c][q]
        low, high = cell_forces(lower, upper, l1, m1, k3, th)
        force = []
        for c in range(3):
            node = [low[c][q] + saved[4 * c + q] for q in range(4)]
            for q in range(4):
                saved[4 * c + q] = high[c][q]
            t0, t1 = fold_y(node[0], node[1]), fold_y(node[2], node[3])
            halo = jnp.broadcast_to(col_f[c, pl.ds(e, 1), :], shape)
            force.append((t0 - t1) + jnp.where(first_row, halo, pltpu.roll(t0 + t1, 1, 0)))
        mass = None
        if col_m is not None:
            rho = rho + pltpu.roll(rho, 1, 1)
            rho = rho + jnp.where(first_row, 0.0, pltpu.roll(rho, 1, 0))
            halo = jnp.broadcast_to(col_m[pl.ds(e, 1), :], shape)
            mass = LUMPED + (rho + saved_m[...]) + jnp.where(first_row, halo, 0.0)
            saved_m[...] = rho
        finish(e, force, mass)
        return carry

    lax.fori_loop(0, cells, body, 0)


def split3(a):
    hi = a.astype(BF16)
    rest = a - hi.astype(F32)
    mid = rest.astype(BF16)
    lo = (rest - mid.astype(F32)).astype(BF16)
    return jnp.concatenate([hi, mid, lo], axis=0)


def join3(a):
    n = a.shape[0] // 3
    return (a[:n] + a[n : 2 * n]) + a[2 * n :]


def one_hots(position):
    pos = position.astype(jnp.int32)
    n = pos.shape[1]
    y, x = pos & 255, pos >> 8
    ohy = jnp.where(iota((256, n), 0) == y, 1.0, 0.0).astype(BF16)
    ohx = jnp.where(iota((16, n), 0) == x, 1.0, 0.0)
    return ohy, ohx


def gather(face, ohy, ohx):
    n = ohx.shape[1]
    rows = join3(jnp.dot(split3(face), ohy, preferred_element_type=F32))
    return jnp.sum(rows.reshape(3, 16, n) * ohx[None], axis=1)


def scatter(values, ohy, ohx):
    n = ohx.shape[1]
    rows = (values[:, None, :] * ohx[None]).reshape(48, n)
    out = lax.dot_general(split3(rows), ohy, (((1,), (1,)), ((), ())), preferred_element_type=F32)
    return join3(out).reshape(3, 16, 256)


def fill_lists(blocks, sol, land, stiff, tally, r_lo, r_hi, q_lo, q_hi, lists):
    for k in range(5):
        cols = slice(128 * k, 128 * k + 128)
        lists[0:1, cols] = sol[0, k : k + 1, :].astype(F32)
        lists[1:2, cols] = land[0, k : k + 1, :].astype(F32)
        lists[2:3, cols] = masked_stiffness(k, 2, stiff, tally, blocks)
    for j, ref, row in ((0, q_lo, R2_LISTS), (1, r_lo, LISTS), (3, r_hi, LISTS), (4, q_hi, R2_LISTS)):
        lists[3:6, 128 * j : 128 * j + 128] = ref[row : row + 3, 0:128]
    lists[3:6, 256:384] = lists[0:3, 256:384]


def first_step(
    blocks, layers,
    u, v, dt, lab, par, sol, land, stiff, tally, r_lo, r_hi, q_lo, q_hi, zb, za,
    u1, v1, dtm, up, dn, up2, dn2, vals,
    ue, le, de, col_lo, col_own, col_hi, col_lab, col_dt, col_f, col_m, modes, saved, saved_m, lists,
):
    layer = lax.axis_index("layer")
    zbase = layer * 8 - 2
    zeros = jnp.zeros((8, 256), F32)
    for c in range(3):
        for zz in (0, 1):
            row = 16 * (2 * c + zz)
            ue[c, zz] = zb[ZU_U + row : ZU_U + row + 16, :]
            ue[c, 10 + zz] = za[ZD_U + row : ZD_U + row + 16, :]
        ue[c, 2:10] = u[c]
        v1[c, 0] = zb[ZU_V + 16 * c : ZU_V + 16 * c + 16, :]
        v1[c, 9] = za[ZD_V + 16 * c : ZD_V + 16 * c + 16, :]
        v1[c, 1:9] = v[c]
        for col, src, zu, zd in ((col_lo, r_lo, ZU_CL, ZD_CL), (col_hi, r_hi, ZU_CH, ZD_CH)):
            col[c, 8:16, :] = zeros
            col[c, 0:2, :] = zb[zu + 2 * c : zu + 2 * c + 2, :]
            col[c, 2:10, :] = src[COL_U + 8 * c : COL_U + 8 * c + 8, :]
            col[c, 10:12, :] = za[zd + 2 * c : zd + 2 * c + 2, :]
        col_own[c, 8:16, :] = zeros
        col_own[c, 0:8, :] = ue[c, 0:8, 0, :]
        col_own[c, 8:12, :] = ue[c, 8:12, 0, :]
    for zz in (0, 1):
        le[zz] = zb[ZU_LAB + 16 * zz : ZU_LAB + 16 * zz + 16, :]
        de[zz] = zb[ZU_DT + 16 * zz : ZU_DT + 16 * zz + 16, :]
    le[2:10] = lab[...].astype(F32)
    de[2:10] = dt[...]
    le[10] = za[ZD_LAB : ZD_LAB + 16, :]
    de[10] = za[ZD_DT : ZD_DT + 16, :]
    for col, src, zu, zd in ((col_lab, COL_LAB, ZU_CLAB, ZD_CLAB), (col_dt, COL_DT, ZU_CDT, ZD_CDT)):
        col[8:16, :] = zeros
        col[0:2, :] = zb[zu : zu + 2, :]
        col[2:10, :] = r_lo[src : src + 8, :]
        col[10:11, :] = za[zd : zd + 1, :]

    mats = material_scalars(par)
    column_forces(blocks, layers, zbase, mats, col_lo, col_own, col_lab, col_dt, col_f, col_m)

    def finish(e, force, mass):
        at = jnp.maximum(e - 1, 0)
        rate = DT / mass
        dtm[at] = rate
        for c in range(3):
            speed = v1[c, at] - rate * force[c]
            u1[c, at] = ue[c, e] + DT * speed

            @pl.when(e > 0)
            def _():
                v1[c, at] = speed

    elastic_steps(
        blocks, layers, 11, zbase, mats, ue, le, de, col_hi, col_f, col_m, modes, saved, saved_m, finish
    )

    @pl.when(layer == layers // 2)
    def _():
        fill_lists(blocks, sol, land, stiff, tally, r_lo, r_hi, q_lo, q_hi, lists)
        sol_y, sol_x = one_hots(lists[0:1, :])
        land_y, land_x = one_hots(lists[4:5, :])
        other_land_y, other_land_x = one_hots(lists[1:2, :])
        other_sol_y, other_sol_x = one_hots(lists[3:4, :])

        def face_of(k, face):
            if k == 2:
                return jnp.concatenate([u[c, 3 + face] for c in range(3)], axis=0)
            ref, row = ((q_lo, R2_FACES), (r_lo, FACES), None, (r_hi, FACES), (q_hi, R2_FACES))[k]
            return ref[row + 48 * face : row + 48 * face + 48, :]

        bump = gather(face_of(2, 1), sol_y, sol_x)
        pad = gather(face_of(2, 0), land_y, land_x)
        far_pad, far_bump = [], []
        for k in range(5):
            cols = slice(128 * k, 128 * k + 128)
            far_pad.append(gather(face_of(k, 0), other_land_y[:, cols], other_land_x[:, cols]))
            far_bump.append(gather(face_of(k, 1), other_sol_y[:, cols], other_sol_x[:, cols]))
        on_bump = lists[2:3, :] * (jnp.concatenate(far_pad, axis=1) - bump)
        on_pad = lists[5:6, :] * (jnp.concatenate(far_bump, axis=1) - pad)
        bump_force = scatter(on_bump, sol_y, sol_x)
        pad_force = scatter(on_pad, land_y, land_x)
        for c in range(3):
            for at, extra in ((4, pad_force[c]), (5, bump_force[c])):
                change = dtm[at] * extra
                v1[c, at] = v1[c, at] + change
                u1[c, at] = u1[c, at] + DT * change
        new_pad = jnp.concatenate([u1[c, 4] for c in range(3)], axis=0)
        new_bump = jnp.concatenate([u1[c, 5] for c in range(3)], axis=0)
        vals[0:3, :] = gather(new_bump, sol_y, sol_x)
        vals[3:6, :] = gather(new_pad, land_y, land_x)
        for out, k, row in ((up, 3, S1_VALS), (dn, 1, S1_VALS), (up2, 4, 0), (dn2, 0, 0)):
            out[row : row + 6, 0:128] = vals[0:6, 128 * k : 128 * k + 128]

    for out, x in ((up, 15), (dn, 0)):
        for c in range(3):
            out[10 * c : 10 * c + 8, :] = u1[c, 0:8, x, :]
            out[10 * c + 8 : 10 * c + 10, :] = u1[c, 8:10, x, :]


def second_step(
    blocks, layers,
    u, v, dtm, dt, lab, par, sol, land, stiff, tally, r_lo, r_hi, q_lo, q_hi, zb, vals, own, s_lo, s_hi, t_lo, t_hi,
    u2, v2,
    le, de, col_lo, col_own, col_hi, col_lab, col_dt, col_f, modes, saved, lists,
):
    layer = lax.axis_index("layer")
    zbase = layer * 8 - 1
    zeros = jnp.zeros((8, 256), F32)
    for c in range(3):
        for col, src in ((col_lo, s_lo), (col_hi, s_hi), (col_own, own)):
            col[c, 8:16, :] = zeros
            col[c, 0:10, :] = src[10 * c : 10 * c + 10, :]
    le[0] = zb[ZU_LAB + 16 : ZU_LAB + 32, :]
    de[0] = zb[ZU_DT + 16 : ZU_DT + 32, :]
    le[1:9] = lab[...].astype(F32)
    de[1:9] = dt[...]
    for col, src, zu in ((col_lab, COL_LAB, ZU_CLAB), (col_dt, COL_DT, ZU_CDT)):
        col[8:16, :] = zeros
        col[0:1, :] = zb[zu + 1 : zu + 2, :]
        col[1:9, :] = r_lo[src : src + 8, :]

    mats = material_scalars(par)
    column_forces(blocks, layers, zbase, mats, col_lo, col_own, col_lab, col_dt, col_f, None)

    def finish(e, force, mass):
        at = jnp.maximum(e - 1, 0)
        rate = dtm[e]
        for c in range(3):
            speed = v[c, e] - rate * force[c]
            v2[c, at] = speed
            u2[c, at] = u[c, e] + DT * speed

    elastic_steps(blocks, layers, 9, zbase, mats, u, le, de, col_hi, col_f, None, modes, saved, None, finish)

    @pl.when(layer == layers // 2)
    def _():
        fill_lists(blocks, sol, land, stiff, tally, r_lo, r_hi, q_lo, q_hi, lists)
        sol_y, sol_x = one_hots(lists[0:1, :])
        land_y, land_x = one_hots(lists[4:5, :])

        def far(first):
            parts = [
                t_lo[first : first + 3, 0:128],
                s_lo[S1_VALS + first : S1_VALS + first + 3, 0:128],
                vals[first : first + 3, 256:384],
                s_hi[S1_VALS + first : S1_VALS + first + 3, 0:128],
                t_hi[first : first + 3, 0:128],
            ]
            return jnp.concatenate(parts, axis=1)

        on_bump = lists[2:3, :] * (far(3) - vals[0:3, :])
        on_pad = lists[5:6, :] * (far(0) - vals[3:6, :])
        bump_force = scatter(on_bump, sol_y, sol_x)
        pad_force = scatter(on_pad, land_y, land_x)
        for c in range(3):
            for at, extra in ((3, pad_force[c]), (4, bump_force[c])):
                change = dtm[at + 1] * extra
                v2[c, at] = v2[c, at] + change
                u2[c, at] = u2[c, at] + DT * change


VM = pl.BlockSpec(memory_space=pltpu.VMEM)
SM = pl.BlockSpec(memory_space=pltpu.SMEM)


def call(kernel, in_specs, outs, scratch, name, flops):
    return pl.pallas_call(
        kernel,
        out_shape=[jax.ShapeDtypeStruct(shape, F32) for shape in outs],
        in_specs=in_specs,
        out_specs=[VM] * len(outs),
        scratch_shapes=[pltpu.VMEM(shape, F32) for shape in scratch],
        compiler_params=pltpu.CompilerParams(vmem_limit_bytes=32 * 1024 * 1024),
        cost_estimate=pl.CostEstimate(flops=flops, bytes_accessed=2_000_000, transcendentals=0),
        name=name,
    )


def local(u, v, dt, lab, par, sol, land, stiff, tally):
    blocks, layers = lax.axis_size("plane"), lax.axis_size("layer")
    face_layer = layers // 2

    def along_plane(value, steps):
        pairs = [(s, s + steps) for s in range(blocks) if 0 <= s + steps < blocks]
        return lax.ppermute(value, "plane", pairs)

    def along_face(value, steps):
        pairs = [
            (s * layers + face_layer, (s + steps) * layers + face_layer)
            for s in range(blocks)
            if 0 <= s + steps < blocks
        ]
        return lax.ppermute(value, ("plane", "layer"), pairs)

    def along_layer(value, steps):
        pairs = [(s, s + steps) for s in range(layers) if 0 <= s + steps < layers]
        return lax.ppermute(value, "layer", pairs)

    up, dn, up2, dn2 = call(
        functools.partial(pack_plane, blocks),
        [VM] * 6 + [SM],
        [(R1_ROWS, 256), (R1_ROWS, 256), (R2_ROWS, 256), (R2_ROWS, 256)],
        [],
        "pack_plane",
        100_000,
    )(u, dt, lab, sol, land, stiff, tally)
    r_lo, r_hi = along_plane(up, 1), along_plane(dn, -1)
    q_lo, q_hi = along_face(up2, 2), along_face(dn2, -2)
    zu, zd = call(pack_layer, [VM] * 6, [(ZU_ROWS, 256), (ZD_ROWS, 256)], [], "pack_layer", 100_000)(
        u, v, dt, lab, r_lo, r_hi
    )
    zb, za = along_layer(zu, 1), along_layer(zd, -1)

    col, plane = (3, 16, 256), (16, 256)
    u1, v1, dtm, up, dn, up2, dn2, vals = call(
        functools.partial(first_step, blocks, layers),
        [VM] * 4 + [SM] + [VM] * 3 + [SM] + [VM] * 6,
        [(3, 10, 16, 256), (3, 10, 16, 256), (10, 16, 256)]
        + [(S1_ROWS, 256)] * 2 + [(8, 128)] * 2 + [(8, 640)],
        [(3, 12, 16, 256), (11, 16, 256), (11, 16, 256), col, col, col, plane, plane, col, plane]
        + [(12, 16, 256), (12, 16, 256), plane, (8, 640)],
        "first_step",
        50_000_000,
    )(u, v, dt, lab, par, sol, land, stiff, tally, r_lo, r_hi, q_lo, q_hi, zb, za)
    s_lo, s_hi = along_plane(up, 1), along_plane(dn, -1)
    t_lo, t_hi = along_face(up2, 2), along_face(dn2, -2)
    return tuple(
        call(
            functools.partial(second_step, blocks, layers),
            [VM] * 5 + [SM] + [VM] * 3 + [SM] + [VM] * 11,
            [(3, 8, 16, 256), (3, 8, 16, 256)],
            [(9, 16, 256), (9, 16, 256), col, col, col, plane, plane, col]
            + [(12, 16, 256), (12, 16, 256), (8, 640)],
            "second_step",
            50_000_000,
        )(u1, v1, dtm, dt, lab, par, sol, land, stiff, tally, r_lo, r_hi, q_lo, q_hi, zb, vals, dn, s_lo, s_hi, t_lo, t_hi)
    )


def solution(mesh):
    in_specs = (
        P(None, "layer", "plane", None),
        P(None, "layer", "plane", None),
        P("layer", "plane", None),
        P("layer", "plane", None),
        P(),
        P("plane", None, None),
        P("plane", None, None),
        P("plane", None, None),
        P("plane", None),
    )
    out_specs = (P(None, "layer", "plane", None), P(None, "layer", "plane", None))
    return jax.shard_map(local, mesh=mesh, in_specs=in_specs, out_specs=out_specs, check_vma=False)
```

time: 436 us -> 67.2 us (0.15)
  the two profiles are of different devices: /device:TPU:249 before, /device:TPU:252 now
where the time goes in v1:
time: 67.2 us; the launch traced here: 66.7 us
  starting transfers between devices  33.8 us (50%)
  waiting for transfers between devices  17.5 us (26%)
  Pallas kernels  9.75 us (15%)
  local copies, waits for them, and re-layouts  4.86 us (7%)
  between operations  0.8 us (1%)
    ppermute x4, starting transfers between devices, along_face(): return lax.ppermute(value, ('plane', 'layer'), pairs)  16.8 us
    ppermute x4, waiting for transfers between devices, along_face(): return lax.ppermute(value, ('plane', 'layer'), pairs)  14.9 us
    ppermute x4, starting transfers between devices, along_plane(): return lax.ppermute(value, 'plane', pairs)  11.1 us
    ppermute x2, starting transfers between devices, along_layer(): return lax.ppermute(value, 'layer', pairs)  5.84 us
    unnamed x23, local copies, waits for them, and re-layouts  4.86 us
    pallas_call x1, Pallas kernels, local(): call(functools.partial(first_step, blocks, layers), [VM] * 4 + [SM] + [VM...  4.84 us
    pallas_call x1, Pallas kernels, local(): call(functools.partial(second_step, blocks, layers), [VM] * 5 + [SM] + [V...  4.28 us
    ppermute x4, waiting for transfers between devices, along_plane(): return lax.ppermute(value, 'plane', pairs)  2.66 us
  transfers between devices with their start and end apart: 10, of which 5 were waited for; matrix products, arithmetic and copies ran while one was open for 0% of the time, Pallas kernels for 0%

profile of v1, /device:TPU:252, one launch (start us, length us, event | category | flops | bytes accessed | tf_op | source)
XLA Modules:
  0.0 66.7 jit_solution(5936325480990177755)
XLA Ops:
  0.6 0.7 %copy.14.sol = s32[1,5,128]{2,1,0:T(8,128)S(1)} copy(s32[1,5,128]{2,0,1:T(1,128)} %param.14) | data formatting | bytes 5120 | tf_op args[5]
  1.3 0.7 %copy-done.9 = f32[1,5,128]{2,0,1:T(1,128)S(1)} copy-done((f32[1,5,128]{2,0,1:T(1,128)S(1)}, f32[1,5,128]{2,0,1:T(1,128)}, u32[]{:S(2)}) %copy-start.9) | copy-done | bytes 2584
  2.0 0.7 copy-done.7
  2.7 1.0 %copy-done = f32[3,8,16,256]{3,2,1,0:T(8,128)S(1)} copy-done((f32[3,8,16,256]{3,2,1,0:T(8,128)S(1)}, f32[3,8,16,256]{3,2,1,0:T(8,128)}, u32[]{:S(2)}) %copy-start) | copy-done | bytes 393240
  3.7 0.9 %copy-done.1 = f32[8,16,256]{2,1,0:T(8,128)S(1)} copy-done((f32[8,16,256]{2,1,0:T(8,128)S(1)}, f32[8,16,256]{2,1,0:T(8,128)}, u32[]{:S(2)}) %copy-start.1) | copy-done | bytes 131096
  4.6 0.9 %copy-done.3 = s32[8,16,256]{2,1,0:T(8,128)S(1)} copy-done((s32[8,16,256]{2,1,0:T(8,128)S(1)}, s32[8,16,256]{2,1,0:T(8,128)}, u32[]{:S(2)}) %copy-start.3) | copy-done | bytes 131096
  5.5 0.6 pack_plane.1
  6.1 1.9 %collective-permute-start = (f32[144,256]{1,0:T(8,128)S(1)}, f32[144,256]{1,0:T(8,128)S(1)}, u32[]{:S(2)}, u32[]{:S(2)}) collective-permute-start(f32[144,256]{1,0:T(8,128)S(1)} %get-tuple-element.16), channel_id=1, source_target_pairs={{0,4},{4,8},{8,12},{12,16},{16,20},{20,24},{24,28},{28,32},{32,36}... | collective-permute-start | bytes 442376 | tf_op jit(solution)/shard_map/ppermute | solution.py:485
  8.0 3.6 %collective-permute-start.1 = (f32[144,256]{1,0:T(8,128)S(1)}, f32[144,256]{1,0:T(8,128)S(1)}, u32[]{:S(2)}, u32[]{:S(2)}) collective-permute-start(f32[144,256]{1,0:T(8,128)S(1)} %get-tuple-element.17), channel_id=1, source_target_pairs={{4,0},{8,4},{12,8},{16,12},{20,16},{24,20},{28,24},{32,28},{36,32}... | collective-permute-start | bytes 442376 | tf_op jit(solution)/shard_map/ppermute | solution.py:485
  11.7 0.9 %collective-permute-done.lo.r_lo = f32[144,256]{1,0:T(8,128)S(1)} collective-permute-done((f32[144,256]{1,0:T(8,128)S(1)}, f32[144,256]{1,0:T(8,128)S(1)}, u32[]{:S(2)}, u32[]{:S(2)}) %collective-permute-start) | collective-permute-done | bytes 147488 | tf_op jit(solution)/shard_map/ppermute | solution.py:485
  12.5 1.8 %collective-permute-done.1.hi.r_hi = f32[144,256]{1,0:T(8,128)S(1)} collective-permute-done((f32[144,256]{1,0:T(8,128)S(1)}, f32[144,256]{1,0:T(8,128)S(1)}, u32[]{:S(2)}, u32[]{:S(2)}) %collective-permute-start.1) | collective-permute-done | bytes 147488 | tf_op jit(solution)/shard_map/ppermute | solution.py:485
  14.4 3.1 %collective-permute-start.4 = (f32[224,256]{1,0:T(8,128)S(1)}, f32[224,256]{1,0:T(8,128)S(1)}, u32[]{:S(2)}, u32[]{:S(2)}) collective-permute-start(f32[224,256]{1,0:T(8,128)S(1)} %get-tuple-element.20), channel_id=1, source_target_pairs={{0,1},{1,2},{2,3},{4,5},{5,6},{6,7},{8,9},{9,10},{10,11},{12,13},{... | collective-permute-start | bytes 688136 | tf_op jit(solution)/shard_map/ppermute | solution.py:497
  17.5 2.7 %collective-permute-start.5 = (f32[192,256]{1,0:T(8,128)S(1)}, f32[192,256]{1,0:T(8,128)S(1)}, u32[]{:S(2)}, u32[]{:S(2)}) collective-permute-start(f32[192,256]{1,0:T(8,128)S(1)} %get-tuple-element.21), channel_id=1, source_target_pairs={{1,0},{2,1},{3,2},{5,4},{6,5},{7,6},{9,8},{10,9},{11,10},{13,12},{... | collective-permute-start | bytes 589832 | tf_op jit(solution)/shard_map/ppermute | solution.py:497
  20.2 8.0 %collective-permute-start.2 = (f32[104,256]{1,0:T(8,128)S(1)}, f32[104,256]{1,0:T(8,128)S(1)}, u32[]{:S(2)}, u32[]{:S(2)}) collective-permute-start(f32[104,256]{1,0:T(8,128)S(1)} %get-tuple-element.18), channel_id=1, source_target_pairs={{2,10},{6,14},{10,18},{14,22},{18,26},{22,30},{26,34},{30,38},{34,... | collective-permute-start | bytes 319496 | tf_op jit(solution)/shard_map/ppermute | solution.py:493
  28.3 2.1 %collective-permute-start.3 = (f32[104,256]{1,0:T(8,128)S(1)}, f32[104,256]{1,0:T(8,128)S(1)}, u32[]{:S(2)}, u32[]{:S(2)}) collective-permute-start(f32[104,256]{1,0:T(8,128)S(1)} %get-tuple-element.19), channel_id=1, source_target_pairs={{10,2},{14,6},{18,10},{22,14},{26,18},{30,22},{34,26},{38,30},{42,... | collective-permute-start | bytes 319496 | tf_op jit(solution)/shard_map/ppermute | solution.py:493
  30.3 0.3 collective-permute-done.2.q_lo
  30.6 7.7 %collective-permute-done.3.q_hi = f32[104,256]{1,0:T(8,128)S(1)} collective-permute-done((f32[104,256]{1,0:T(8,128)S(1)}, f32[104,256]{1,0:T(8,128)S(1)}, u32[]{:S(2)}, u32[]{:S(2)}) %collective-permute-start.3) | collective-permute-done | bytes 106528 | tf_op jit(solution)/shard_map/ppermute | solution.py:493
  38.3 4.8 %first_step.1 = (f32[3,10,16,256]{3,2,1,0:T(8,128)S(1)}, f32[3,10,16,256]{3,2,1,0:T(8,128)S(1)}, f32[10,16,256]{2,1,0:T(8,128)S(1)}, f32[40,256]{1,0:T(8,128)S(1...) custom-call(f32[3,8,16,256]{3,2,1,0:T(8,128)S(1)} %copy-done, ...), custom_call_target="tpu_custom_call" | custom-call | flops 50000000 | bytes 2000000 | tf_op jit(solution)/shard_map/first_step/pallas_call | solution.py:515
  43.2 1.9 %collective-permute-start.6 = (f32[40,256]{1,0:T(8,128)S(1)}, f32[40,256]{1,0:T(8,128)S(1)}, u32[]{:S(2)}, u32[]{:S(2)}) collective-permute-start(f32[40,256]{1,0:T(8,128)S(1)} %get-tuple-element.27), channel_id=1, source_target_pairs={{0,4},{4,8},{8,12},{12,16},{16,20},{20,24},{24,28},{28,32},{32,36}... | collective-permute-start | bytes 122888 | tf_op jit(solution)/shard_map/ppermute | solution.py:485
  45.1 3.6 %collective-permute-start.7 = (f32[40,256]{1,0:T(8,128)S(1)}, f32[40,256]{1,0:T(8,128)S(1)}, u32[]{:S(2)}, u32[]{:S(2)}) collective-permute-start(f32[40,256]{1,0:T(8,128)S(1)} %get-tuple-element.26.own), channel_id=1, source_target_pairs={{4,0},{8,4},{12,8},{16,12},{20,16},{24,20},{28,24},{32,28},{36,32}... | collective-permute-start | bytes 122888 | tf_op jit(solution)/shard_map/ppermute | solution.py:485
  48.8 4.8 %collective-permute-start.8 = (f32[8,128]{1,0:T(8,128)S(1)}, f32[8,128]{1,0:T(8,128)S(1)}, u32[]{:S(2)}, u32[]{:S(2)}) collective-permute-start(f32[8,128]{1,0:T(8,128)S(1)} %get-tuple-element.28), channel_id=1, source_target_pairs={{2,10},{6,14},{10,18},{14,22},{18,26},{22,30},{26,34},{30,38},{34,... | collective-permute-start | bytes 12296 | tf_op jit(solution)/shard_map/ppermute | solution.py:493
  53.6 1.9 %collective-permute-start.9 = (f32[8,128]{1,0:T(8,128)S(1)}, f32[8,128]{1,0:T(8,128)S(1)}, u32[]{:S(2)}, u32[]{:S(2)}) collective-permute-start(f32[8,128]{1,0:T(8,128)S(1)} %get-tuple-element.29), channel_id=1, source_target_pairs={{10,2},{14,6},{18,10},{22,14},{26,18},{30,22},{34,26},{38,30},{42,... | collective-permute-start | bytes 12296 | tf_op jit(solution)/shard_map/ppermute | solution.py:493
  55.5 6.9 %collective-permute-done.9.t_hi = f32[8,128]{1,0:T(8,128)S(1)} collective-permute-done((f32[8,128]{1,0:T(8,128)S(1)}, f32[8,128]{1,0:T(8,128)S(1)}, u32[]{:S(2)}, u32[]{:S(2)}) %collective-permute-start.9) | collective-permute-done | bytes 4128 | tf_op jit(solution)/shard_map/ppermute | solution.py:493
  62.5 4.3 %second_step.1 = (f32[3,8,16,256]{3,2,1,0:T(8,128)}, f32[3,8,16,256]{3,2,1,0:T(8,128)}) custom-call(f32[3,10,16,256]{3,2,1,0:T(8,128)S(1)} %get-tuple-element.22.u, f32[3,10,16,256]{3,2,1,0:T(8,128)S(1)} %get-tuple-element.23.v, f32[10,16,256]{2,1,0:T(8,128)S(1)} %get-tuple-element.24.dtm, f32[8,16,256]{2,1,0:T(8,128)S(1)} %copy-done.2, ...), custom_call_target="tpu_custom_call" | custom-call | flops 50000000 | bytes 2000000 | tf_op jit(solution)/shard_map/second_step/pallas_call | solution.py:528
  (23 shorter events, 0.1 us)
Async XLA Ops:
  0.6 0.7 %copy-start.8 = (s32[1,5,128]{2,0,1:T(1,128)S(1)}, s32[1,5,128]{2,0,1:T(1,128)}, u32[]{:S(2)}) copy-start(s32[1,5,128]{2,0,1:T(1,128)} %param.15) | copy-start | bytes 7684
  1.3 0.7 %copy-start.9 = (f32[1,5,128]{2,0,1:T(1,128)S(1)}, f32[1,5,128]{2,0,1:T(1,128)}, u32[]{:S(2)}) copy-start(f32[1,5,128]{2,0,1:T(1,128)} %param.16) | copy-start | bytes 7684
  2.0 0.7 copy-start.7
  2.7 1.0 %copy-start = (f32[3,8,16,256]{3,2,1,0:T(8,128)S(1)}, f32[3,8,16,256]{3,2,1,0:T(8,128)}, u32[]{:S(2)}) copy-start(f32[3,8,16,256]{3,2,1,0:T(8,128)} %u.5) | copy-start | bytes 1179652
  3.7 0.9 %copy-start.1 = (f32[8,16,256]{2,1,0:T(8,128)S(1)}, f32[8,16,256]{2,1,0:T(8,128)}, u32[]{:S(2)}) copy-start(f32[8,16,256]{2,1,0:T(8,128)} %dt.7) | copy-start | bytes 393220
  4.6 0.9 %copy-start.3 = (s32[8,16,256]{2,1,0:T(8,128)S(1)}, s32[8,16,256]{2,1,0:T(8,128)}, u32[]{:S(2)}) copy-start(s32[8,16,256]{2,1,0:T(8,128)} %lab.7) | copy-start | bytes 393220
  5.5 8.8 %copy-start.5 = (f32[3,8,16,256]{3,2,1,0:T(8,128)S(1)}, f32[3,8,16,256]{3,2,1,0:T(8,128)}, u32[]{:S(2)}) copy-start(f32[3,8,16,256]{3,2,1,0:T(8,128)} %v.3) | copy-start | bytes 1179652
  6.1 6.5 %collective-permute-start = (f32[144,256]{1,0:T(8,128)S(1)}, f32[144,256]{1,0:T(8,128)S(1)}, u32[]{:S(2)}, u32[]{:S(2)}) collective-permute-start(f32[144,256]{1,0:T(8,128)S(1)} %get-tuple-element.16), channel_id=1, source_target_pairs={{0,4},{4,8},{8,12},{12,16},{16,20},{20,24},{24,28},{28,32},{32,36}... | collective-permute-start | bytes 442376 | tf_op jit(solution)/shard_map/ppermute | solution.py:485
  8.0 6.3 %collective-permute-start.1 = (f32[144,256]{1,0:T(8,128)S(1)}, f32[144,256]{1,0:T(8,128)S(1)}, u32[]{:S(2)}, u32[]{:S(2)}) collective-permute-start(f32[144,256]{1,0:T(8,128)S(1)} %get-tuple-element.17), channel_id=1, source_target_pairs={{4,0},{8,4},{12,8},{16,12},{20,16},{24,20},{28,24},{32,28},{36,32}... | collective-permute-start | bytes 442376 | tf_op jit(solution)/shard_map/ppermute | solution.py:485
  14.4 24.0 %collective-permute-start.4 = (f32[224,256]{1,0:T(8,128)S(1)}, f32[224,256]{1,0:T(8,128)S(1)}, u32[]{:S(2)}, u32[]{:S(2)}) collective-permute-start(f32[224,256]{1,0:T(8,128)S(1)} %get-tuple-element.20), channel_id=1, source_target_pairs={{0,1},{1,2},{2,3},{4,5},{5,6},{6,7},{8,9},{9,10},{10,11},{12,13},{... | collective-permute-start | bytes 688136 | tf_op jit(solution)/shard_map/ppermute | solution.py:497
  17.5 20.9 %copy-start.6 = (f32[4,4]{1,0:T(4,128)S(1)}, f32[4,4]{1,0:T(4,128)}, u32[]{:S(2)}) copy-start(f32[4,4]{1,0:T(4,128)} %par.3) | copy-start | bytes 196
  17.5 20.8 %collective-permute-start.5 = (f32[192,256]{1,0:T(8,128)S(1)}, f32[192,256]{1,0:T(8,128)S(1)}, u32[]{:S(2)}, u32[]{:S(2)}) collective-permute-start(f32[192,256]{1,0:T(8,128)S(1)} %get-tuple-element.21), channel_id=1, source_target_pairs={{1,0},{2,1},{3,2},{5,4},{6,5},{7,6},{9,8},{10,9},{11,10},{13,12},{... | collective-permute-start | bytes 589832 | tf_op jit(solution)/shard_map/ppermute | solution.py:497
  20.2 10.4 %collective-permute-start.2 = (f32[104,256]{1,0:T(8,128)S(1)}, f32[104,256]{1,0:T(8,128)S(1)}, u32[]{:S(2)}, u32[]{:S(2)}) collective-permute-start(f32[104,256]{1,0:T(8,128)S(1)} %get-tuple-element.18), channel_id=1, source_target_pairs={{2,10},{6,14},{10,18},{14,22},{18,26},{22,30},{26,34},{30,38},{34,... | collective-permute-start | bytes 319496 | tf_op jit(solution)/shard_map/ppermute | solution.py:493
  28.3 34.2 %copy-start.2 = (f32[8,16,256]{2,1,0:T(8,128)S(1)}, f32[8,16,256]{2,1,0:T(8,128)}, u32[]{:S(2)}) copy-start(f32[8,16,256]{2,1,0:T(8,128)} %dt.7) | copy-start | bytes 393220
  28.3 34.2 %copy-start.4 = (s32[8,16,256]{2,1,0:T(8,128)S(1)}, s32[8,16,256]{2,1,0:T(8,128)}, u32[]{:S(2)}) copy-start(s32[8,16,256]{2,1,0:T(8,128)} %lab.7) | copy-start | bytes 393220
  28.3 10.1 %collective-permute-start.3 = (f32[104,256]{1,0:T(8,128)S(1)}, f32[104,256]{1,0:T(8,128)S(1)}, u32[]{:S(2)}, u32[]{:S(2)}) collective-permute-start(f32[104,256]{1,0:T(8,128)S(1)} %get-tuple-element.19), channel_id=1, source_target_pairs={{10,2},{14,6},{18,10},{22,14},{26,18},{30,22},{34,26},{38,30},{42,... | collective-permute-start | bytes 319496 | tf_op jit(solution)/shard_map/ppermute | solution.py:493
  43.2 19.2 %collective-permute-start.6 = (f32[40,256]{1,0:T(8,128)S(1)}, f32[40,256]{1,0:T(8,128)S(1)}, u32[]{:S(2)}, u32[]{:S(2)}) collective-permute-start(f32[40,256]{1,0:T(8,128)S(1)} %get-tuple-element.27), channel_id=1, source_target_pairs={{0,4},{4,8},{8,12},{12,16},{16,20},{20,24},{24,28},{28,32},{32,36}... | collective-permute-start | bytes 122888 | tf_op jit(solution)/shard_map/ppermute | solution.py:485
  45.1 17.3 %collective-permute-start.7 = (f32[40,256]{1,0:T(8,128)S(1)}, f32[40,256]{1,0:T(8,128)S(1)}, u32[]{:S(2)}, u32[]{:S(2)}) collective-permute-start(f32[40,256]{1,0:T(8,128)S(1)} %get-tuple-element.26.own), channel_id=1, source_target_pairs={{4,0},{8,4},{12,8},{16,12},{20,16},{24,20},{28,24},{32,28},{36,32}... | collective-permute-start | bytes 122888 | tf_op jit(solution)/shard_map/ppermute | solution.py:485
  48.8 6.8 %collective-permute-start.8 = (f32[8,128]{1,0:T(8,128)S(1)}, f32[8,128]{1,0:T(8,128)S(1)}, u32[]{:S(2)}, u32[]{:S(2)}) collective-permute-start(f32[8,128]{1,0:T(8,128)S(1)} %get-tuple-element.28), channel_id=1, source_target_pairs={{2,10},{6,14},{10,18},{14,22},{18,26},{22,30},{26,34},{30,38},{34,... | collective-permute-start | bytes 12296 | tf_op jit(solution)/shard_map/ppermute | solution.py:493
  53.6 8.8 %collective-permute-start.9 = (f32[8,128]{1,0:T(8,128)S(1)}, f32[8,128]{1,0:T(8,128)S(1)}, u32[]{:S(2)}, u32[]{:S(2)}) collective-permute-start(f32[8,128]{1,0:T(8,128)S(1)} %get-tuple-element.29), channel_id=1, source_target_pairs={{10,2},{14,6},{18,10},{22,14},{26,18},{30,22},{34,26},{38,30},{42,... | collective-permute-start | bytes 12296 | tf_op jit(solution)/shard_map/ppermute | solution.py:493

commit v2 on v1

--- a/solution.py
+++ b/solution.py
@@ -13,49 +13,98 @@
 BF16 = jnp.bfloat16
 QUADS = ((0, 0), (0, 1), (1, 0), (1, 1))
 
-COL_U, COL_LAB, COL_DT, LISTS, FACES, R1_ROWS = 0, 24, 32, 40, 48, 144
-R2_LISTS, R2_FACES, R2_ROWS = 0, 8, 104
+COL_HI, COL_LO, LISTS, PAD, EXPORT_ROWS = 0, 40, 64, 88, 136
+OWN_LISTS, MATE_LISTS, OWN_PAD, MATE_PAD, CROSS_ROWS = 40, 64, 88, 136, 184
+COL_LAB, COL_DT, COL_BEYOND, COLS_ROWS = 24, 32, 40, 64
 ZU_U, ZU_V, ZU_LAB, ZU_DT, ZU_CL, ZU_CH, ZU_CLAB, ZU_CDT, ZU_ROWS = 0, 96, 144, 176, 208, 214, 220, 222, 224
 ZD_U, ZD_V, ZD_LAB, ZD_DT, ZD_CL, ZD_CH, ZD_CLAB, ZD_CDT, ZD_ROWS = 0, 96, 144, 160, 176, 182, 188, 189, 192
-S1_ROWS, S1_VALS = 40, 32
+NEW_HI, NEW_LO, NEW_VALS, NEW_ROWS = 0, 32, 64, 88
+CROSS_OWN, CROSS_MATE, CROSS_ON, NEW_CROSS_ROWS = 32, 36, 40, 48
+NEAR, FAR1, OWN, FAR2, OPP2 = range(5)
+OFFSETS = (1, -1, 0, -2, 2)
 
 
 def iota(shape, dim):
     return lax.broadcasted_iota(jnp.int32, shape, dim)
 
 
-def masked_stiffness(k, half, stiff_ref, tally_ref, blocks):
-    target = lax.axis_index("plane") + (k - half)
-    valid = (target >= 0) & (target < blocks)
-    count = jnp.where(valid, tally_ref[0, k], 0)
-    row = stiff_ref[0, k : k + 1, :]
-    return jnp.where(iota(row.shape, 1) < count, row, 0.0)
-
-
-def pack_plane(blocks, u, dt, lab, sol, land, stiff, tally, up, dn, up2, dn2):
+def on_even():
+    return lax.rem(lax.axis_index("plane"), 2) == 0
+
+
+def role_offset(role):
+    return jnp.where(on_even(), OFFSETS[role], -OFFSETS[role])
+
+
+def pack_export(
+    blocks, layers,
+    u_hbm, dt_hbm, lab_hbm, sol_hbm, land_hbm, stiff_hbm, tally_hbm,
+    out,
+    u, dt, lab, sol, land, stiff, tally, pos, sems,
+):
+    copies = [
+        pltpu.make_async_copy(src, dst, sems.at[i])
+        for i, (src, dst) in enumerate(
+            (
+                (u_hbm, u), (dt_hbm, dt), (lab_hbm, lab), (sol_hbm, sol),
+                (land_hbm, land), (stiff_hbm, stiff), (tally_hbm, tally),
+            )
+        )
+    ]
+    for copy in copies:
+        copy.start()
+    for copy in copies:
+        copy.wait()
     pad_z = u.shape[1] // 2 - 1
-    for out, x in ((up, 15), (dn, 0)):
-        for c in range(3):
-            out[COL_U + 8 * c : COL_U + 8 * c + 8, :] = u[c, :, x, :]
-        out[COL_LAB : COL_LAB + 8, :] = lab[:, x, :].astype(F32)
-        out[COL_DT : COL_DT + 8, :] = dt[:, x, :]
-    for out, k, lists, faces in (
-        (up, 3, LISTS, FACES),
-        (dn, 1, LISTS, FACES),
-        (up2, 4, R2_LISTS, R2_FACES),
-        (dn2, 0, R2_LISTS, R2_FACES),
-    ):
-        out[lists : lists + 8, :] = jnp.zeros((8, 256), F32)
-        out[lists : lists + 1, 0:128] = sol[0, k : k + 1, :].astype(F32)
-        out[lists + 1 : lists + 2, 0:128] = land[0, k : k + 1, :].astype(F32)
-        out[lists + 2 : lists + 3, 0:128] = masked_stiffness(k, 2, stiff, tally, blocks)
-        for c in range(3):
-            for face in (0, 1):
-                row = faces + 48 * face + 16 * c
-                out[row : row + 16, :] = u[c, pad_z + face]
-
-
-def pack_layer(u, v, dt, lab, lo, hi, up, dn):
+    here = lax.axis_index("plane")
+    for x, row in ((15, COL_HI), (0, COL_LO)):
+        for c in range(3):
+            out[row + 8 * c : row + 8 * c + 8, :] = u[c, :, x, :]
+    out[COL_HI + COL_LAB : COL_HI + COL_LAB + 8, :] = lab[:, 15, :].astype(F32)
+    out[COL_HI + COL_DT : COL_HI + COL_DT + 8, :] = dt[:, 15, :]
+
+    @pl.when(lax.axis_index("layer") == layers // 2)
+    def _():
+        out[LISTS : LISTS + 24, :] = jnp.zeros((24, 256), F32)
+        for k in range(5):
+            row = LISTS + 4 * k
+            target = here + (k - 2)
+            count = jnp.where((target >= 0) & (target < blocks), tally[0, k], 0)
+            live = iota((1, 128), 1) < count
+            out[row : row + 1, 0:128] = sol[k].astype(F32)
+            out[row : row + 1, 128:256] = land[k].astype(F32)
+            out[row + 1 : row + 2, 0:128] = jnp.where(live, stiff[k], 0.0)
+            pos[0:1, 128 * k : 128 * k + 128] = sol[k]
+        bump = gather(jnp.concatenate([u[c, pad_z + 1] for c in range(3)], axis=0), *one_hots(pos[0:1, :]))
+        for k in range(5):
+            row, cols = LISTS + 4 * k, slice(128 * k, 128 * k + 128)
+            out[row + 1 : row + 2, 128:256] = bump[0:1, cols]
+            out[row + 2 : row + 3, 0:128] = bump[1:2, cols]
+            out[row + 2 : row + 3, 128:256] = bump[2:3, cols]
+        for c in range(3):
+            out[PAD + 16 * c : PAD + 16 * c + 16, :] = u[c, pad_z]
+
+
+def pack_cross(own, mate, out):
+    out[24:40, :] = mate[COL_HI + 24 : COL_HI + 40, :]
+    out[0:24, :] = jnp.where(on_even(), mate[COL_HI : COL_HI + 24, :], mate[COL_LO : COL_LO + 24, :])
+    out[OWN_LISTS : OWN_LISTS + 24, :] = own[LISTS : LISTS + 24, :]
+    out[MATE_LISTS : MATE_LISTS + 24, :] = mate[LISTS : LISTS + 24, :]
+    out[OWN_PAD : OWN_PAD + 48, :] = own[PAD : PAD + 48, :]
+    out[MATE_PAD : MATE_PAD + 48, :] = mate[PAD : PAD + 48, :]
+
+
+def pack_new_cross(own, mate, out):
+    out[0:32, :] = jnp.where(on_even(), mate[NEW_HI : NEW_HI + 32, :], mate[NEW_LO : NEW_LO + 32, :])
+    for row, src, role in ((CROSS_OWN, own, OPP2), (CROSS_MATE, mate, FAR1), (CROSS_ON, mate, FAR2)):
+        out[row : row + 4, :] = src[NEW_VALS + 4 * role : NEW_VALS + 4 * role + 4, :]
+    out[44:48, :] = jnp.zeros((4, 256), F32)
+
+
+def pack_layer(u, v, dt, lab, near, far, up, dn, cols):
+    even = on_even()
+    cols[0:40, :] = jnp.where(even, far[0:40, :], near[COL_HI : COL_HI + 40, :])
+    cols[COL_BEYOND : COL_BEYOND + 24, :] = jnp.where(even, near[COL_LO : COL_LO + 24, :], far[0:24, :])
     for c in range(3):
         for zz in (0, 1):
             row = 16 * (2 * c + zz)
@@ -63,20 +112,20 @@
             dn[ZD_U + row : ZD_U + row + 16, :] = u[c, zz]
         up[ZU_V + 16 * c : ZU_V + 16 * c + 16, :] = v[c, 7]
         dn[ZD_V + 16 * c : ZD_V + 16 * c + 16, :] = v[c, 0]
-        row = COL_U + 8 * c
-        up[ZU_CL + 2 * c : ZU_CL + 2 * c + 2, :] = lo[row + 6 : row + 8, :]
-        up[ZU_CH + 2 * c : ZU_CH + 2 * c + 2, :] = hi[row + 6 : row + 8, :]
-        dn[ZD_CL + 2 * c : ZD_CL + 2 * c + 2, :] = lo[row : row + 2, :]
-        dn[ZD_CH + 2 * c : ZD_CH + 2 * c + 2, :] = hi[row : row + 2, :]
+        lo, hi = 8 * c, COL_BEYOND + 8 * c
+        up[ZU_CL + 2 * c : ZU_CL + 2 * c + 2, :] = cols[lo + 6 : lo + 8, :]
+        up[ZU_CH + 2 * c : ZU_CH + 2 * c + 2, :] = cols[hi + 6 : hi + 8, :]
+        dn[ZD_CL + 2 * c : ZD_CL + 2 * c + 2, :] = cols[lo : lo + 2, :]
+        dn[ZD_CH + 2 * c : ZD_CH + 2 * c + 2, :] = cols[hi : hi + 2, :]
     for zz in (0, 1):
         up[ZU_LAB + 16 * zz : ZU_LAB + 16 * zz + 16, :] = lab[6 + zz].astype(F32)
         up[ZU_DT + 16 * zz : ZU_DT + 16 * zz + 16, :] = dt[6 + zz]
-    up[ZU_CLAB : ZU_CLAB + 2, :] = lo[COL_LAB + 6 : COL_LAB + 8, :]
-    up[ZU_CDT : ZU_CDT + 2, :] = lo[COL_DT + 6 : COL_DT + 8, :]
+    up[ZU_CLAB : ZU_CLAB + 2, :] = cols[COL_LAB + 6 : COL_LAB + 8, :]
+    up[ZU_CDT : ZU_CDT + 2, :] = cols[COL_DT + 6 : COL_DT + 8, :]
     dn[ZD_LAB : ZD_LAB + 16, :] = lab[0].astype(F32)
     dn[ZD_DT : ZD_DT + 16, :] = dt[0]
-    dn[ZD_CLAB : ZD_CLAB + 1, :] = lo[COL_LAB : COL_LAB + 1, :]
-    dn[ZD_CDT : ZD_CDT + 1, :] = lo[COL_DT : COL_DT + 1, :]
+    dn[ZD_CLAB : ZD_CLAB + 1, :] = cols[COL_LAB : COL_LAB + 1, :]
+    dn[ZD_CDT : ZD_CDT + 1, :] = cols[COL_DT : COL_DT + 1, :]
     dn[ZD_CDT + 1 : ZD_ROWS, :] = jnp.zeros((ZD_ROWS - ZD_CDT - 1, 256), F32)
 
 
@@ -285,22 +334,31 @@
     return join3(out).reshape(3, 16, 256)
 
 
-def fill_lists(blocks, sol, land, stiff, tally, r_lo, r_hi, q_lo, q_hi, lists):
-    for k in range(5):
-        cols = slice(128 * k, 128 * k + 128)
-        lists[0:1, cols] = sol[0, k : k + 1, :].astype(F32)
-        lists[1:2, cols] = land[0, k : k + 1, :].astype(F32)
-        lists[2:3, cols] = masked_stiffness(k, 2, stiff, tally, blocks)
-    for j, ref, row in ((0, q_lo, R2_LISTS), (1, r_lo, LISTS), (3, r_hi, LISTS), (4, q_hi, R2_LISTS)):
-        lists[3:6, 128 * j : 128 * j + 128] = ref[row : row + 3, 0:128]
-    lists[3:6, 256:384] = lists[0:3, 256:384]
+def fill_lists(own, near, far, opp, lists):
+    sources = {
+        NEAR: (near, LISTS), FAR1: (far, MATE_LISTS), OWN: (own, LISTS), FAR2: (far, OWN_LISTS), OPP2: (opp, MATE_LISTS)
+    }
+    for role, (ref, base) in sources.items():
+        cols = slice(128 * role, 128 * role + 128)
+        offset = role_offset(role)
+        row = LISTS + 4 * (2 + offset)
+        for i in range(3):
+            line = own[pl.ds(row + i, 1), :]
+            for half in (0, 1):
+                lists[2 * i + half : 2 * i + half + 1, cols] = line[:, 128 * half : 128 * half + 128]
+        row = base + 4 * (2 - offset)
+        for i in range(3):
+            line = ref[pl.ds(row + i, 1), :]
+            for half in (0, 1):
+                if i + half:
+                    lists[5 + 2 * i + half : 6 + 2 * i + half, cols] = line[:, 128 * half : 128 * half + 128]
 
 
 def first_step(
     blocks, layers,
-    u, v, dt, lab, par, sol, land, stiff, tally, r_lo, r_hi, q_lo, q_hi, zb, za,
-    u1, v1, dtm, up, dn, up2, dn2, vals,
-    ue, le, de, col_lo, col_own, col_hi, col_lab, col_dt, col_f, col_m, modes, saved, saved_m, lists,
+    u, v, dt, lab, par, own, near, far, opp, cols, zb, za,
+    u1, v1, dtm, out, lists,
+    ue, le, de, col_lo, col_own, col_hi, col_lab, col_dt, col_f, col_m, modes, saved, saved_m,
 ):
     layer = lax.axis_index("layer")
     zbase = layer * 8 - 2
@@ -314,10 +372,10 @@
         v1[c, 0] = zb[ZU_V + 16 * c : ZU_V + 16 * c + 16, :]
         v1[c, 9] = za[ZD_V + 16 * c : ZD_V + 16 * c + 16, :]
         v1[c, 1:9] = v[c]
-        for col, src, zu, zd in ((col_lo, r_lo, ZU_CL, ZD_CL), (col_hi, r_hi, ZU_CH, ZD_CH)):
+        for col, src, zu, zd in ((col_lo, 0, ZU_CL, ZD_CL), (col_hi, COL_BEYOND, ZU_CH, ZD_CH)):
             col[c, 8:16, :] = zeros
             col[c, 0:2, :] = zb[zu + 2 * c : zu + 2 * c + 2, :]
-            col[c, 2:10, :] = src[COL_U + 8 * c : COL_U + 8 * c + 8, :]
+            col[c, 2:10, :] = cols[src + 8 * c : src + 8 * c + 8, :]
             col[c, 10:12, :] = za[zd + 2 * c : zd + 2 * c + 2, :]
         col_own[c, 8:16, :] = zeros
         col_own[c, 0:8, :] = ue[c, 0:8, 0, :]
@@ -332,7 +390,7 @@
     for col, src, zu, zd in ((col_lab, COL_LAB, ZU_CLAB, ZD_CLAB), (col_dt, COL_DT, ZU_CDT, ZD_CDT)):
         col[8:16, :] = zeros
         col[0:2, :] = zb[zu : zu + 2, :]
-        col[2:10, :] = r_lo[src : src + 8, :]
+        col[2:10, :] = cols[src : src + 8, :]
         col[10:11, :] = za[zd : zd + 1, :]
 
     mats = material_scalars(par)
@@ -356,27 +414,24 @@
 
     @pl.when(layer == layers // 2)
     def _():
-        fill_lists(blocks, sol, land, stiff, tally, r_lo, r_hi, q_lo, q_hi, lists)
+        fill_lists(own, near, far, opp, lists)
         sol_y, sol_x = one_hots(lists[0:1, :])
-        land_y, land_x = one_hots(lists[4:5, :])
-        other_land_y, other_land_x = one_hots(lists[1:2, :])
-        other_sol_y, other_sol_x = one_hots(lists[3:4, :])
-
-        def face_of(k, face):
-            if k == 2:
-                return jnp.concatenate([u[c, 3 + face] for c in range(3)], axis=0)
-            ref, row = ((q_lo, R2_FACES), (r_lo, FACES), None, (r_hi, FACES), (q_hi, R2_FACES))[k]
-            return ref[row + 48 * face : row + 48 * face + 48, :]
-
-        bump = gather(face_of(2, 1), sol_y, sol_x)
-        pad = gather(face_of(2, 0), land_y, land_x)
-        far_pad, far_bump = [], []
-        for k in range(5):
-            cols = slice(128 * k, 128 * k + 128)
-            far_pad.append(gather(face_of(k, 0), other_land_y[:, cols], other_land_x[:, cols]))
-            far_bump.append(gather(face_of(k, 1), other_sol_y[:, cols], other_sol_x[:, cols]))
-        on_bump = lists[2:3, :] * (jnp.concatenate(far_pad, axis=1) - bump)
-        on_pad = lists[5:6, :] * (jnp.concatenate(far_bump, axis=1) - pad)
+        land_y, land_x = one_hots(lists[6:7, :])
+        far_y, far_x = one_hots(lists[1:2, :])
+        own_pad = own[PAD : PAD + 48, :]
+        pads = {
+            NEAR: near[PAD : PAD + 48, :],
+            FAR1: far[MATE_PAD : MATE_PAD + 48, :],
+            OWN: own_pad,
+            FAR2: far[OWN_PAD : OWN_PAD + 48, :],
+            OPP2: opp[MATE_PAD : MATE_PAD + 48, :],
+        }
+        far_pad = []
+        for role in range(5):
+            part = slice(128 * role, 128 * role + 128)
+            far_pad.append(gather(pads[role], far_y[:, part], far_x[:, part]))
+        on_bump = lists[2:3, :] * (jnp.concatenate(far_pad, axis=1) - lists[3:6, :])
+        on_pad = lists[7:8, :] * (lists[8:11, :] - gather(own_pad, land_y, land_x))
         bump_force = scatter(on_bump, sol_y, sol_x)
         pad_force = scatter(on_pad, land_y, land_x)
         for c in range(3):
@@ -386,30 +441,38 @@
                 u1[c, at] = u1[c, at] + DT * change
         new_pad = jnp.concatenate([u1[c, 4] for c in range(3)], axis=0)
         new_bump = jnp.concatenate([u1[c, 5] for c in range(3)], axis=0)
-        vals[0:3, :] = gather(new_bump, sol_y, sol_x)
-        vals[3:6, :] = gather(new_pad, land_y, land_x)
-        for out, k, row in ((up, 3, S1_VALS), (dn, 1, S1_VALS), (up2, 4, 0), (dn2, 0, 0)):
-            out[row : row + 6, 0:128] = vals[0:6, 128 * k : 128 * k + 128]
-
-    for out, x in ((up, 15), (dn, 0)):
-        for c in range(3):
-            out[10 * c : 10 * c + 8, :] = u1[c, 0:8, x, :]
-            out[10 * c + 8 : 10 * c + 10, :] = u1[c, 8:10, x, :]
+        lists[3:6, :] = gather(new_bump, sol_y, sol_x)
+        lists[8:11, :] = gather(new_pad, land_y, land_x)
+        for role in range(5):
+            part = slice(128 * role, 128 * role + 128)
+            for i, row in enumerate((3, 4, 5, 8, 9, 10)):
+                at, half = NEW_VALS + 4 * role + i // 2, i % 2
+                out[at : at + 1, 128 * half : 128 * half + 128] = lists[row : row + 1, part]
+
+    for x, row in ((15, NEW_HI), (0, NEW_LO)):
+        for c in range(3):
+            out[row + 10 * c : row + 10 * c + 8, :] = u1[c, 0:8, x, :]
+            out[row + 10 * c + 8 : row + 10 * c + 10, :] = u1[c, 8:10, x, :]
 
 
 def second_step(
     blocks, layers,
-    u, v, dtm, dt, lab, par, sol, land, stiff, tally, r_lo, r_hi, q_lo, q_hi, zb, vals, own, s_lo, s_hi, t_lo, t_hi,
+    u, v, dtm, dt, lab, par, lists, cols, zb, own, near, far, opp,
     u2, v2,
-    le, de, col_lo, col_own, col_hi, col_lab, col_dt, col_f, modes, saved, lists,
+    le, de, col_lo, col_own, col_hi, col_lab, col_dt, col_f, modes, saved,
 ):
     layer = lax.axis_index("layer")
     zbase = layer * 8 - 1
     zeros = jnp.zeros((8, 256), F32)
+    even = on_even()
     for c in range(3):
-        for col, src in ((col_lo, s_lo), (col_hi, s_hi), (col_own, own)):
-            col[c, 8:16, :] = zeros
-            col[c, 0:10, :] = src[10 * c : 10 * c + 10, :]
+        at, hi, lo = 10 * c, NEW_HI + 10 * c, NEW_LO + 10 * c
+        col_lo[c, 8:16, :] = zeros
+        col_hi[c, 8:16, :] = zeros
+        col_own[c, 8:16, :] = zeros
+        col_lo[c, 0:10, :] = jnp.where(even, far[at : at + 10, :], near[hi : hi + 10, :])
+        col_hi[c, 0:10, :] = jnp.where(even, near[lo : lo + 10, :], far[at : at + 10, :])
+        col_own[c, 0:10, :] = own[lo : lo + 10, :]
     le[0] = zb[ZU_LAB + 16 : ZU_LAB + 32, :]
     de[0] = zb[ZU_DT + 16 : ZU_DT + 32, :]
     le[1:9] = lab[...].astype(F32)
@@ -417,7 +480,7 @@
     for col, src, zu in ((col_lab, COL_LAB, ZU_CLAB), (col_dt, COL_DT, ZU_CDT)):
         col[8:16, :] = zeros
         col[0:1, :] = zb[zu + 1 : zu + 2, :]
-        col[1:9, :] = r_lo[src : src + 8, :]
+        col[1:9, :] = cols[src : src + 8, :]
 
     mats = material_scalars(par)
     column_forces(blocks, layers, zbase, mats, col_lo, col_own, col_lab, col_dt, col_f, None)
@@ -434,22 +497,26 @@
 
     @pl.when(layer == layers // 2)
     def _():
-        fill_lists(blocks, sol, land, stiff, tally, r_lo, r_hi, q_lo, q_hi, lists)
         sol_y, sol_x = one_hots(lists[0:1, :])
-        land_y, land_x = one_hots(lists[4:5, :])
-
-        def far(first):
+        land_y, land_x = one_hots(lists[6:7, :])
+
+        def values(i):
+            half = slice(128 * (i % 2), 128 * (i % 2) + 128)
+            own_row = (3, 4, 5, 8, 9, 10)[i]
+            places = (
+                (near, NEW_VALS + 4 * NEAR), (far, CROSS_MATE), None, (far, CROSS_OWN), (opp, CROSS_ON)
+            )
             parts = [
-                t_lo[first : first + 3, 0:128],
-                s_lo[S1_VALS + first : S1_VALS + first + 3, 0:128],
-                vals[first : first + 3, 256:384],
-                s_hi[S1_VALS + first : S1_VALS + first + 3, 0:128],
-                t_hi[first : first + 3, 0:128],
+                lists[own_row : own_row + 1, 256:384] if place is None
+                else place[0][place[1] + i // 2 : place[1] + i // 2 + 1, half]
+                for place in places
             ]
             return jnp.concatenate(parts, axis=1)
 
-        on_bump = lists[2:3, :] * (far(3) - vals[0:3, :])
-        on_pad = lists[5:6, :] * (far(0) - vals[3:6, :])
+        far_bump = jnp.concatenate([values(i) for i in range(3)], axis=0)
+        far_pad = jnp.concatenate([values(i) for i in range(3, 6)], axis=0)
+        on_bump = lists[2:3, :] * (far_pad - lists[3:6, :])
+        on_pad = lists[7:8, :] * (far_bump - lists[8:11, :])
         bump_force = scatter(on_bump, sol_y, sol_x)
         pad_force = scatter(on_pad, land_y, land_x)
         for c in range(3):
@@ -461,6 +528,7 @@
 
 VM = pl.BlockSpec(memory_space=pltpu.VMEM)
 SM = pl.BlockSpec(memory_space=pltpu.SMEM)
+HBM = pl.BlockSpec(memory_space=pltpu.HBM)
 
 
 def call(kernel, in_specs, outs, scratch, name, flops):
@@ -469,7 +537,7 @@
         out_shape=[jax.ShapeDtypeStruct(shape, F32) for shape in outs],
         in_specs=in_specs,
         out_specs=[VM] * len(outs),
-        scratch_shapes=[pltpu.VMEM(shape, F32) for shape in scratch],
+        scratch_shapes=[pltpu.VMEM(s, F32) if isinstance(s, tuple) else s for s in scratch],
         compiler_params=pltpu.CompilerParams(vmem_limit_bytes=32 * 1024 * 1024),
         cost_estimate=pl.CostEstimate(flops=flops, bytes_accessed=2_000_000, transcendentals=0),
         name=name,
@@ -478,62 +546,56 @@
 
 def local(u, v, dt, lab, par, sol, land, stiff, tally):
     blocks, layers = lax.axis_size("plane"), lax.axis_size("layer")
-    face_layer = layers // 2
-
-    def along_plane(value, steps):
-        pairs = [(s, s + steps) for s in range(blocks) if 0 <= s + steps < blocks]
-        return lax.ppermute(value, "plane", pairs)
-
-    def along_face(value, steps):
-        pairs = [
-            (s * layers + face_layer, (s + steps) * layers + face_layer)
-            for s in range(blocks)
-            if 0 <= s + steps < blocks
-        ]
-        return lax.ppermute(value, ("plane", "layer"), pairs)
+    swaps = [(s, s ^ 1) for s in range(blocks)]
+    crossings = [(s, s + 2 - 4 * (s % 2)) for s in range(blocks) if 0 <= s + 2 - 4 * (s % 2) < blocks]
+    face_swaps = [(a * layers + layers // 2, b * layers + layers // 2) for a, b in swaps]
 
     def along_layer(value, steps):
         pairs = [(s, s + steps) for s in range(layers) if 0 <= s + steps < layers]
         return lax.ppermute(value, "layer", pairs)
 
-    up, dn, up2, dn2 = call(
-        functools.partial(pack_plane, blocks),
-        [VM] * 6 + [SM],
-        [(R1_ROWS, 256), (R1_ROWS, 256), (R2_ROWS, 256), (R2_ROWS, 256)],
-        [],
-        "pack_plane",
+    own = call(
+        functools.partial(pack_export, blocks, layers),
+        [HBM] * 7,
+        [(EXPORT_ROWS, 256)],
+        [u.shape, dt.shape, pltpu.VMEM(lab.shape, jnp.int32)]
+        + [pltpu.VMEM((5, 1, 128), jnp.int32)] * 2
+        + [(5, 1, 128), pltpu.SMEM((1, 5), jnp.int32), pltpu.VMEM((8, 640), jnp.int32), pltpu.SemaphoreType.DMA((7,))],
+        "pack_export",
         100_000,
-    )(u, dt, lab, sol, land, stiff, tally)
-    r_lo, r_hi = along_plane(up, 1), along_plane(dn, -1)
-    q_lo, q_hi = along_face(up2, 2), along_face(dn2, -2)
-    zu, zd = call(pack_layer, [VM] * 6, [(ZU_ROWS, 256), (ZD_ROWS, 256)], [], "pack_layer", 100_000)(
-        u, v, dt, lab, r_lo, r_hi
-    )
-    zb, za = along_layer(zu, 1), along_layer(zd, -1)
+    )(u, dt, lab, sol.reshape(5, 1, 128), land.reshape(5, 1, 128), stiff.reshape(5, 1, 128), tally)[0]
+    near = lax.ppermute(own, "plane", swaps)
+    cross = call(pack_cross, [VM] * 2, [(CROSS_ROWS, 256)], [], "pack_cross", 100_000)(own, near)[0]
+    far = lax.ppermute(cross, "plane", crossings)
+    up, dn, cols = call(
+        pack_layer, [VM] * 6, [(ZU_ROWS, 256), (ZD_ROWS, 256), (COLS_ROWS, 256)], [], "pack_layer", 100_000
+    )(u, v, dt, lab, near, far)
+    zb, za = along_layer(up, 1), along_layer(dn, -1)
+    opp = lax.ppermute(far, ("plane", "layer"), face_swaps)
 
     col, plane = (3, 16, 256), (16, 256)
-    u1, v1, dtm, up, dn, up2, dn2, vals = call(
+    u1, v1, dtm, own, lists = call(
         functools.partial(first_step, blocks, layers),
-        [VM] * 4 + [SM] + [VM] * 3 + [SM] + [VM] * 6,
-        [(3, 10, 16, 256), (3, 10, 16, 256), (10, 16, 256)]
-        + [(S1_ROWS, 256)] * 2 + [(8, 128)] * 2 + [(8, 640)],
+        [VM] * 4 + [SM] + [VM] * 7,
+        [(3, 10, 16, 256), (3, 10, 16, 256), (10, 16, 256), (NEW_ROWS, 256), (16, 640)],
         [(3, 12, 16, 256), (11, 16, 256), (11, 16, 256), col, col, col, plane, plane, col, plane]
-        + [(12, 16, 256), (12, 16, 256), plane, (8, 640)],
+        + [(12, 16, 256), (12, 16, 256), plane],
         "first_step",
         50_000_000,
-    )(u, v, dt, lab, par, sol, land, stiff, tally, r_lo, r_hi, q_lo, q_hi, zb, za)
-    s_lo, s_hi = along_plane(up, 1), along_plane(dn, -1)
-    t_lo, t_hi = along_face(up2, 2), along_face(dn2, -2)
+    )(u, v, dt, lab, par, own, near, far, opp, cols, zb, za)
+    near = lax.ppermute(own, "plane", swaps)
+    cross = call(pack_new_cross, [VM] * 2, [(NEW_CROSS_ROWS, 256)], [], "pack_new_cross", 100_000)(own, near)[0]
+    far = lax.ppermute(cross, "plane", crossings)
+    opp = lax.ppermute(far, ("plane", "layer"), face_swaps)
     return tuple(
         call(
             functools.partial(second_step, blocks, layers),
-            [VM] * 5 + [SM] + [VM] * 3 + [SM] + [VM] * 11,
+            [VM] * 5 + [SM] + [VM] * 7,
             [(3, 8, 16, 256), (3, 8, 16, 256)],
-            [(9, 16, 256), (9, 16, 256), col, col, col, plane, plane, col]
-            + [(12, 16, 256), (12, 16, 256), (8, 640)],
+            [(9, 16, 256), (9, 16, 256), col, col, col, plane, plane, col] + [(12, 16, 256), (12, 16, 256)],
             "second_step",
             50_000_000,
-        )(u1, v1, dtm, dt, lab, par, sol, land, stiff, tally, r_lo, r_hi, q_lo, q_hi, zb, vals, dn, s_lo, s_hi, t_lo, t_hi)
+        )(u1, v1, dtm, dt, lab, par, lists, cols, zb, own, near, far, opp)
     )
 
 

time: 67.2 us -> 56.2 us (0.84)
  the two profiles are of different devices: /device:TPU:252 before, /device:TPU:261 now
where the time goes in v2:
time: 56.2 us; the launch traced here: 55.8 us
  starting transfers between devices  32.4 us (58%)
  Pallas kernels  10.2 us (18%)
  waiting for transfers between devices  8.18 us (15%)
  local copies, waits for them, and re-layouts  4.19 us (7%)
  between operations  0.79 us (1%)
    ppermute x2, starting transfers between devices, local(): opp = lax.ppermute(far, ('plane', 'layer'), face_swaps)  13.7 us
    ppermute x2, starting transfers between devices, local(): far = lax.ppermute(cross, 'plane', crossings)  7.12 us
    ppermute x2, starting transfers between devices, local(): near = lax.ppermute(own, 'plane', swaps)  6.36 us
    ppermute x2, starting transfers between devices, along_layer(): return lax.ppermute(value, 'layer', pairs)  5.28 us
    pallas_call x1, Pallas kernels, local(): call(functools.partial(first_step, blocks, layers), [VM] * 4 + [SM] + [VM...  4.5 us
    ppermute x2, waiting for transfers between devices, local(): far = lax.ppermute(cross, 'plane', crossings)  4.39 us
    pallas_call x1, Pallas kernels, local(): call(functools.partial(second_step, blocks, layers), [VM] * 5 + [SM] + [V...  4.22 us
    unnamed x24, local copies, waits for them, and re-layouts  4.19 us
  transfers between devices with their start and end apart: 8, of which 6 were waited for; matrix products, arithmetic and copies ran while one was open for 0% of the time, Pallas kernels for 0%

profile of v2, /device:TPU:261, one launch (start us, length us, event | category | flops | bytes accessed | tf_op | source)
XLA Modules:
  0.0 55.8 jit_solution(17140468221330671983)
XLA Ops:
  0.7 0.7 %copy-done.9 = s32[1,5,128]{2,0,1:T(1,128)S(1)} copy-done((s32[1,5,128]{2,0,1:T(1,128)S(1)}, s32[1,5,128]{2,0,1:T(1,128)}, u32[]{:S(2)}) %copy-start.9) | copy-done | bytes 2584
  1.3 0.0 copy-done.8
  1.3 1.0 %copy-done = f32[3,8,16,256]{3,2,1,0:T(8,128)S(1)} copy-done((f32[3,8,16,256]{3,2,1,0:T(8,128)S(1)}, f32[3,8,16,256]{3,2,1,0:T(8,128)}, u32[]{:S(2)}) %copy-start) | copy-done | bytes 393240
  2.3 0.9 %copy-done.2 = f32[8,16,256]{2,1,0:T(8,128)S(1)} copy-done((f32[8,16,256]{2,1,0:T(8,128)S(1)}, f32[8,16,256]{2,1,0:T(8,128)}, u32[]{:S(2)}) %copy-start.2) | copy-done | bytes 131096
  3.2 0.9 %copy-done.4 = s32[8,16,256]{2,1,0:T(8,128)S(1)} copy-done((s32[8,16,256]{2,1,0:T(8,128)S(1)}, s32[8,16,256]{2,1,0:T(8,128)}, u32[]{:S(2)}) %copy-start.4) | copy-done | bytes 131096
  4.1 0.7 %copy-done.10 = f32[1,5,128]{2,0,1:T(1,128)S(1)} copy-done((f32[1,5,128]{2,0,1:T(1,128)S(1)}, f32[1,5,128]{2,0,1:T(1,128)}, u32[]{:S(2)}) %copy-start.10) | copy-done | bytes 2584
  4.8 1.4 %pack_export.1.own = f32[136,256]{1,0:T(8,128)S(1)} custom-call(f32[3,8,16,256]{3,2,1,0:T(8,128)S(1)} %copy-done, f32[8,16,256]{2,1,0:T(8,128)S(1)} %copy-done.2, s32[8,16,256]{2,1,0:T(8,128)S(1)} %copy-done.4, s32[5,1,128]{2,1,0:T(1,128)S(1)} %bitcast.3, s32[5,1,128]{2,1,0:T(1,128)S(1)} %bitcast.4, f32[5,1,128]{2,1,0:T(1,128)S(1)} %bitcast.5, ...), custom_call_target="tpu_custom_call" | custom-call | flops 100000 | bytes 2000000 | tf_op jit(solution)/shard_map/pack_export/pallas_call | solution.py:557
  6.2 2.7 %collective-permute-start = (f32[136,256]{1,0:T(8,128)S(1)}, f32[136,256]{1,0:T(8,128)S(1)}, u32[]{:S(2)}, u32[]{:S(2)}) collective-permute-start(f32[136,256]{1,0:T(8,128)S(1)} %pack_export.1.own), channel_id=1, source_target_pairs={{0,4},{4,0},{8,12},{12,8},{16,20},{20,16},{24,28},{28,24},{32,36},... | collective-permute-start | bytes 417800 | tf_op jit(solution)/shard_map/ppermute | solution.py:567
  9.0 1.0 %collective-permute-done.mate.near = f32[136,256]{1,0:T(8,128)S(1)} collective-permute-done((f32[136,256]{1,0:T(8,128)S(1)}, f32[136,256]{1,0:T(8,128)S(1)}, u32[]{:S(2)}, u32[]{:S(2)}) %collective-permute-start) | collective-permute-done | bytes 139296 | tf_op jit(solution)/shard_map/ppermute | solution.py:567
  10.0 4.2 %collective-permute-start.1 = (f32[184,256]{1,0:T(8,128)S(1)}, f32[184,256]{1,0:T(8,128)S(1)}, u32[]{:S(2)}, u32[]{:S(2)}) collective-permute-start(f32[184,256]{1,0:T(8,128)S(1)} %pack_cross.1), channel_id=1, source_target_pairs={{0,8},{8,16},{12,4},{16,24},{20,12},{24,32},{28,20},{32,40},{36,28... | collective-permute-start | bytes 565256 | tf_op jit(solution)/shard_map/ppermute | solution.py:569
  14.2 2.5 %collective-permute-done.1.far = f32[184,256]{1,0:T(8,128)S(1)} collective-permute-done((f32[184,256]{1,0:T(8,128)S(1)}, f32[184,256]{1,0:T(8,128)S(1)}, u32[]{:S(2)}, u32[]{:S(2)}) %collective-permute-start.1) | collective-permute-done | bytes 188448 | tf_op jit(solution)/shard_map/ppermute | solution.py:569
  16.7 2.6 %collective-permute-start.3 = (f32[224,256]{1,0:T(8,128)S(1)}, f32[224,256]{1,0:T(8,128)S(1)}, u32[]{:S(2)}, u32[]{:S(2)}) collective-permute-start(f32[224,256]{1,0:T(8,128)S(1)} %get-tuple-element.11), channel_id=1, source_target_pairs={{0,1},{1,2},{2,3},{4,5},{5,6},{6,7},{8,9},{9,10},{10,11},{12,13},{... | collective-permute-start | bytes 688136 | tf_op jit(solution)/shard_map/ppermute | solution.py:555
  19.3 2.7 %collective-permute-start.4 = (f32[192,256]{1,0:T(8,128)S(1)}, f32[192,256]{1,0:T(8,128)S(1)}, u32[]{:S(2)}, u32[]{:S(2)}) collective-permute-start(f32[192,256]{1,0:T(8,128)S(1)} %get-tuple-element.12), channel_id=1, source_target_pairs={{1,0},{2,1},{3,2},{5,4},{6,5},{7,6},{9,8},{10,9},{11,10},{13,12},{... | collective-permute-start | bytes 589832 | tf_op jit(solution)/shard_map/ppermute | solution.py:555
  22.0 6.9 %collective-permute-start.2 = (f32[184,256]{1,0:T(8,128)S(1)}, f32[184,256]{1,0:T(8,128)S(1)}, u32[]{:S(2)}, u32[]{:S(2)}) collective-permute-start(f32[184,256]{1,0:T(8,128)S(1)} %collective-permute-done.1.far), channel_id=1, source_target_pairs={{2,6},{6,2},{10,14},{14,10},{18,22},{22,18},{26,30},{30,26},{34,38... | collective-permute-start | bytes 565256 | tf_op jit(solution)/shard_map/ppermute | solution.py:574
  29.0 1.0 %collective-permute-done.2.opp = f32[184,256]{1,0:T(8,128)S(1)} collective-permute-done((f32[184,256]{1,0:T(8,128)S(1)}, f32[184,256]{1,0:T(8,128)S(1)}, u32[]{:S(2)}, u32[]{:S(2)}) %collective-permute-start.2) | collective-permute-done | bytes 188448 | tf_op jit(solution)/shard_map/ppermute | solution.py:574
  30.0 4.5 %first_step.1 = (f32[3,10,16,256]{3,2,1,0:T(8,128)S(1)}, f32[3,10,16,256]{3,2,1,0:T(8,128)S(1)}, f32[10,16,256]{2,1,0:T(8,128)S(1)}, f32[88,256]{1,0:T(8,128)S(1)}, f32[16,640]{1,0:T(8,128)S(1)}) custom-call(f32[3,8,16,256]{3,2,1,0:T(8,128)S(1)} %copy-done.1, f32[3,8,16,256]{3,2,1,0:T(8,128)S(1)} %copy-done.6, f32[8,16,256]{2,1,0:T(8,128)S(1)} %copy-done.3, ...), custom_call_target="tpu_custom_call" | custom-call | flops 50000000 | bytes 2000000 | tf_op jit(solution)/shard_map/first_step/pallas_call | solution.py:577
  34.5 0.0 copy-start.5
  34.5 3.6 %collective-permute-start.5 = (f32[88,256]{1,0:T(8,128)S(1)}, f32[88,256]{1,0:T(8,128)S(1)}, u32[]{:S(2)}, u32[]{:S(2)}) collective-permute-start(f32[88,256]{1,0:T(8,128)S(1)} %get-tuple-element.17.own), channel_id=1, source_target_pairs={{0,4},{4,0},{8,12},{12,8},{16,20},{20,16},{24,28},{28,24},{32,36},... | collective-permute-start | bytes 270344 | tf_op jit(solution)/shard_map/ppermute | solution.py:586
  38.2 0.9 %collective-permute-done.5.mate.near = f32[88,256]{1,0:T(8,128)S(1)} collective-permute-done((f32[88,256]{1,0:T(8,128)S(1)}, f32[88,256]{1,0:T(8,128)S(1)}, u32[]{:S(2)}, u32[]{:S(2)}) %collective-permute-start.5) | collective-permute-done | bytes 90144 | tf_op jit(solution)/shard_map/ppermute | solution.py:586
  39.1 2.9 %collective-permute-start.6 = (f32[48,256]{1,0:T(8,128)S(1)}, f32[48,256]{1,0:T(8,128)S(1)}, u32[]{:S(2)}, u32[]{:S(2)}) collective-permute-start(f32[48,256]{1,0:T(8,128)S(1)} %pack_new_cross.1), channel_id=1, source_target_pairs={{0,8},{8,16},{12,4},{16,24},{20,12},{24,32},{28,20},{32,40},{36,28... | collective-permute-start | bytes 147464 | tf_op jit(solution)/shard_map/ppermute | solution.py:588
  42.1 1.9 %collective-permute-done.6.far = f32[48,256]{1,0:T(8,128)S(1)} collective-permute-done((f32[48,256]{1,0:T(8,128)S(1)}, f32[48,256]{1,0:T(8,128)S(1)}, u32[]{:S(2)}, u32[]{:S(2)}) %collective-permute-start.6) | collective-permute-done | bytes 49184 | tf_op jit(solution)/shard_map/ppermute | solution.py:588
  44.0 6.7 %collective-permute-start.7 = (f32[48,256]{1,0:T(8,128)S(1)}, f32[48,256]{1,0:T(8,128)S(1)}, u32[]{:S(2)}, u32[]{:S(2)}) collective-permute-start(f32[48,256]{1,0:T(8,128)S(1)} %collective-permute-done.6.far), channel_id=1, source_target_pairs={{2,6},{6,2},{10,14},{14,10},{18,22},{22,18},{26,30},{30,26},{34,38... | collective-permute-start | bytes 147464 | tf_op jit(solution)/shard_map/ppermute | solution.py:589
  50.7 0.9 %collective-permute-done.7.opp = f32[48,256]{1,0:T(8,128)S(1)} collective-permute-done((f32[48,256]{1,0:T(8,128)S(1)}, f32[48,256]{1,0:T(8,128)S(1)}, u32[]{:S(2)}, u32[]{:S(2)}) %collective-permute-start.7) | collective-permute-done | bytes 49184 | tf_op jit(solution)/shard_map/ppermute | solution.py:589
  51.6 4.2 %second_step.1 = (f32[3,8,16,256]{3,2,1,0:T(8,128)}, f32[3,8,16,256]{3,2,1,0:T(8,128)}) custom-call(f32[3,10,16,256]{3,2,1,0:T(8,128)S(1)} %get-tuple-element.13.u, f32[3,10,16,256]{3,2,1,0:T(8,128)S(1)} %get-tuple-element.14.v, f32[10,16,256]{2,1,0:T(8,128)S(1)} %get-tuple-element.15.dtm, f32[8,16,256]{2,1,0:T(8,128)S(1)} %copy-done.3, ...), custom_call_target="tpu_custom_call" | custom-call | flops 50000000 | bytes 2000000 | tf_op jit(solution)/shard_map/second_step/pallas_call | solution.py:591
  (22 shorter events, 0.1 us)
Async XLA Ops:
  0.6 0.7 %copy-start.9 = (s32[1,5,128]{2,0,1:T(1,128)S(1)}, s32[1,5,128]{2,0,1:T(1,128)}, u32[]{:S(2)}) copy-start(s32[1,5,128]{2,0,1:T(1,128)} %param.15) | copy-start | bytes 7684
  0.6 0.7 %copy-start.8 = (s32[1,5,128]{2,0,1:T(1,128)S(1)}, s32[1,5,128]{2,0,1:T(1,128)}, u32[]{:S(2)}) copy-start(s32[1,5,128]{2,0,1:T(1,128)} %param.14) | copy-start | bytes 7684
  0.7 0.7 %copy-start.11 = (s32[1,5]{1,0:T(1,128)S(1)}, s32[1,5]{1,0:T(1,128)}, u32[]{:S(2)}) copy-start(s32[1,5]{1,0:T(1,128)} %tally_hbm.1) | copy-start | bytes 64
  1.3 1.0 %copy-start = (f32[3,8,16,256]{3,2,1,0:T(8,128)S(1)}, f32[3,8,16,256]{3,2,1,0:T(8,128)}, u32[]{:S(2)}) copy-start(f32[3,8,16,256]{3,2,1,0:T(8,128)} %u.3) | copy-start | bytes 1179652
  2.3 0.9 %copy-start.2 = (f32[8,16,256]{2,1,0:T(8,128)S(1)}, f32[8,16,256]{2,1,0:T(8,128)}, u32[]{:S(2)}) copy-start(f32[8,16,256]{2,1,0:T(8,128)} %dt.5) | copy-start | bytes 393220
  3.2 0.9 %copy-start.4 = (s32[8,16,256]{2,1,0:T(8,128)S(1)}, s32[8,16,256]{2,1,0:T(8,128)}, u32[]{:S(2)}) copy-start(s32[8,16,256]{2,1,0:T(8,128)} %lab.5) | copy-start | bytes 393220
  4.1 0.7 %copy-start.10 = (f32[1,5,128]{2,0,1:T(1,128)S(1)}, f32[1,5,128]{2,0,1:T(1,128)}, u32[]{:S(2)}) copy-start(f32[1,5,128]{2,0,1:T(1,128)} %param.16) | copy-start | bytes 7684
  4.8 11.8 %copy-start.3 = (f32[8,16,256]{2,1,0:T(8,128)S(1)}, f32[8,16,256]{2,1,0:T(8,128)}, u32[]{:S(2)}) copy-start(f32[8,16,256]{2,1,0:T(8,128)} %dt.5) | copy-start | bytes 393220
  4.8 11.8 %copy-start.6 = (f32[3,8,16,256]{3,2,1,0:T(8,128)S(1)}, f32[3,8,16,256]{3,2,1,0:T(8,128)}, u32[]{:S(2)}) copy-start(f32[3,8,16,256]{3,2,1,0:T(8,128)} %v.3) | copy-start | bytes 1179652
  6.2 10.4 %copy-start.1 = (f32[3,8,16,256]{3,2,1,0:T(8,128)S(1)}, f32[3,8,16,256]{3,2,1,0:T(8,128)}, u32[]{:S(2)}) copy-start(f32[3,8,16,256]{3,2,1,0:T(8,128)} %u.3) | copy-start | bytes 1179652
  6.2 3.7 %collective-permute-start = (f32[136,256]{1,0:T(8,128)S(1)}, f32[136,256]{1,0:T(8,128)S(1)}, u32[]{:S(2)}, u32[]{:S(2)}) collective-permute-start(f32[136,256]{1,0:T(8,128)S(1)} %pack_export.1.own), channel_id=1, source_target_pairs={{0,4},{4,0},{8,12},{12,8},{16,20},{20,16},{24,28},{28,24},{32,36},... | collective-permute-start | bytes 417800 | tf_op jit(solution)/shard_map/ppermute | solution.py:567
  10.0 6.7 %collective-permute-start.1 = (f32[184,256]{1,0:T(8,128)S(1)}, f32[184,256]{1,0:T(8,128)S(1)}, u32[]{:S(2)}, u32[]{:S(2)}) collective-permute-start(f32[184,256]{1,0:T(8,128)S(1)} %pack_cross.1), channel_id=1, source_target_pairs={{0,8},{8,16},{12,4},{16,24},{20,12},{24,32},{28,20},{32,40},{36,28... | collective-permute-start | bytes 565256 | tf_op jit(solution)/shard_map/ppermute | solution.py:569
  16.7 13.3 %copy-start.7 = (f32[4,4]{1,0:T(4,128)S(1)}, f32[4,4]{1,0:T(4,128)}, u32[]{:S(2)}) copy-start(f32[4,4]{1,0:T(4,128)} %par.3) | copy-start | bytes 196
  16.7 13.3 %collective-permute-start.3 = (f32[224,256]{1,0:T(8,128)S(1)}, f32[224,256]{1,0:T(8,128)S(1)}, u32[]{:S(2)}, u32[]{:S(2)}) collective-permute-start(f32[224,256]{1,0:T(8,128)S(1)} %get-tuple-element.11), channel_id=1, source_target_pairs={{0,1},{1,2},{2,3},{4,5},{5,6},{6,7},{8,9},{9,10},{10,11},{12,13},{... | collective-permute-start | bytes 688136 | tf_op jit(solution)/shard_map/ppermute | solution.py:555
  19.3 10.7 %collective-permute-start.4 = (f32[192,256]{1,0:T(8,128)S(1)}, f32[192,256]{1,0:T(8,128)S(1)}, u32[]{:S(2)}, u32[]{:S(2)}) collective-permute-start(f32[192,256]{1,0:T(8,128)S(1)} %get-tuple-element.12), channel_id=1, source_target_pairs={{1,0},{2,1},{3,2},{5,4},{6,5},{7,6},{9,8},{10,9},{11,10},{13,12},{... | collective-permute-start | bytes 589832 | tf_op jit(solution)/shard_map/ppermute | solution.py:555
  22.0 8.0 %collective-permute-start.2 = (f32[184,256]{1,0:T(8,128)S(1)}, f32[184,256]{1,0:T(8,128)S(1)}, u32[]{:S(2)}, u32[]{:S(2)}) collective-permute-start(f32[184,256]{1,0:T(8,128)S(1)} %collective-permute-done.1.far), channel_id=1, source_target_pairs={{2,6},{6,2},{10,14},{14,10},{18,22},{22,18},{26,30},{30,26},{34,38... | collective-permute-start | bytes 565256 | tf_op jit(solution)/shard_map/ppermute | solution.py:574
  34.5 17.0 %copy-start.5 = (s32[8,16,256]{2,1,0:T(8,128)S(1)}, s32[8,16,256]{2,1,0:T(8,128)}, u32[]{:S(2)}) copy-start(s32[8,16,256]{2,1,0:T(8,128)} %lab.5) | copy-start | bytes 393220
  34.5 4.6 %collective-permute-start.5 = (f32[88,256]{1,0:T(8,128)S(1)}, f32[88,256]{1,0:T(8,128)S(1)}, u32[]{:S(2)}, u32[]{:S(2)}) collective-permute-start(f32[88,256]{1,0:T(8,128)S(1)} %get-tuple-element.17.own), channel_id=1, source_target_pairs={{0,4},{4,0},{8,12},{12,8},{16,20},{20,16},{24,28},{28,24},{32,36},... | collective-permute-start | bytes 270344 | tf_op jit(solution)/shard_map/ppermute | solution.py:586
  39.1 4.8 %collective-permute-start.6 = (f32[48,256]{1,0:T(8,128)S(1)}, f32[48,256]{1,0:T(8,128)S(1)}, u32[]{:S(2)}, u32[]{:S(2)}) collective-permute-start(f32[48,256]{1,0:T(8,128)S(1)} %pack_new_cross.1), channel_id=1, source_target_pairs={{0,8},{8,16},{12,4},{16,24},{20,12},{24,32},{28,20},{32,40},{36,28... | collective-permute-start | bytes 147464 | tf_op jit(solution)/shard_map/ppermute | solution.py:588
  44.0 7.6 %collective-permute-start.7 = (f32[48,256]{1,0:T(8,128)S(1)}, f32[48,256]{1,0:T(8,128)S(1)}, u32[]{:S(2)}, u32[]{:S(2)}) collective-permute-start(f32[48,256]{1,0:T(8,128)S(1)} %collective-permute-done.6.far), channel_id=1, source_target_pairs={{2,6},{6,2},{10,14},{14,10},{18,22},{22,18},{26,30},{30,26},{34,38... | collective-permute-start | bytes 147464 | tf_op jit(solution)/shard_map/ppermute | solution.py:589

commit v3 on v2

--- a/solution.py
+++ b/solution.py
@@ -40,7 +40,7 @@
     blocks, layers,
     u_hbm, dt_hbm, lab_hbm, sol_hbm, land_hbm, stiff_hbm, tally_hbm,
     out,
-    u, dt, lab, sol, land, stiff, tally, pos, sems,
+    u, dt, lab, sol, land, stiff, tally, pos, ohy, ohx, sems,
 ):
     copies = [
         pltpu.make_async_copy(src, dst, sems.at[i])
@@ -53,17 +53,13 @@
     ]
     for copy in copies:
         copy.start()
-    for copy in copies:
+    for copy in copies[3:]:
         copy.wait()
     pad_z = u.shape[1] // 2 - 1
     here = lax.axis_index("plane")
-    for x, row in ((15, COL_HI), (0, COL_LO)):
-        for c in range(3):
-            out[row + 8 * c : row + 8 * c + 8, :] = u[c, :, x, :]
-    out[COL_HI + COL_LAB : COL_HI + COL_LAB + 8, :] = lab[:, 15, :].astype(F32)
-    out[COL_HI + COL_DT : COL_HI + COL_DT + 8, :] = dt[:, 15, :]
-
-    @pl.when(lax.axis_index("layer") == layers // 2)
+    on_face = lax.axis_index("layer") == layers // 2
+
+    @pl.when(on_face)
     def _():
         out[LISTS : LISTS + 24, :] = jnp.zeros((24, 256), F32)
         for k in range(5):
@@ -75,7 +71,19 @@
             out[row : row + 1, 128:256] = land[k].astype(F32)
             out[row + 1 : row + 2, 0:128] = jnp.where(live, stiff[k], 0.0)
             pos[0:1, 128 * k : 128 * k + 128] = sol[k]
-        bump = gather(jnp.concatenate([u[c, pad_z + 1] for c in range(3)], axis=0), *one_hots(pos[0:1, :]))
+        ohy[...], ohx[...] = one_hots(pos[0:1, :])
+
+    for copy in copies[:3]:
+        copy.wait()
+    for x, row in ((15, COL_HI), (0, COL_LO)):
+        for c in range(3):
+            out[row + 8 * c : row + 8 * c + 8, :] = u[c, :, x, :]
+    out[COL_HI + COL_LAB : COL_HI + COL_LAB + 8, :] = lab[:, 15, :].astype(F32)
+    out[COL_HI + COL_DT : COL_HI + COL_DT + 8, :] = dt[:, 15, :]
+
+    @pl.when(on_face)
+    def _():
+        bump = gather(jnp.concatenate([u[c, pad_z + 1] for c in range(3)], axis=0), ohy[...], ohx[...])
         for k in range(5):
             row, cols = LISTS + 4 * k, slice(128 * k, 128 * k + 128)
             out[row + 1 : row + 2, 128:256] = bump[0:1, cols]
@@ -83,6 +91,12 @@
             out[row + 2 : row + 3, 128:256] = bump[2:3, cols]
         for c in range(3):
             out[PAD + 16 * c : PAD + 16 * c + 16, :] = u[c, pad_z]
+
+
+def stage(src, dst, sem):
+    copy = pltpu.make_async_copy(src, dst, sem)
+    copy.start()
+    copy.wait()
 
 
 def pack_cross(own, mate, out):
@@ -229,74 +243,81 @@
     return (a - b) + pltpu.roll(a + b, 1, 1)
 
 
-def column_forces(blocks, layers, zbase, mats, col_lo, col_own, col_lab, col_dt, col_f, col_m):
-    rows = col_lab.shape[0]
+def column_forces(layers, zbase, mats, inside, side, left, right, lab, dt, with_mass):
+    rows = lab.shape[0]
     shape = (rows, 256)
     zg = iota(shape, 0) + zbase
-    gap = layers // 2 * 8 + 3
-    ok = (zg >= 0) & (zg <= layers * 8 - 2) & (zg != gap) & (iota(shape, 1) < 255)
-    mask = jnp.where(ok & (lax.axis_index("plane") > 0), 1.0, 0.0)
-    l1, m1, k3, th, rho = cell_fields(mats, col_lab[...], col_dt[...], mask, col_m is not None)
-    lower = [plane_modes(col_lo[c], col_own[c]) for c in range(3)]
+    ok = (zg >= 0) & (zg <= layers * 8 - 2) & (zg != layers // 2 * 8 + 3) & (iota(shape, 1) < 255)
+    mask = jnp.where(ok & inside, 1.0, 0.0)
+    l1, m1, k3, th, rho = cell_fields(mats, lab, dt, mask, with_mass)
+    lower = [plane_modes(left[c], right[c]) for c in range(3)]
     upper = [[pltpu.roll(a, rows - 1, 0) for a in comp] for comp in lower]
     low, high = cell_forces(lower, upper, l1, m1, k3, th)
+    forces = []
     for c in range(3):
         node = [low[c][q] + pltpu.roll(high[c][q], 1, 0) for q in range(4)]
-        col_f[c] = fold_y(node[0], node[1]) + fold_y(node[2], node[3])
-    if col_m is not None:
+        t0, t1 = fold_y(node[0], node[1]), fold_y(node[2], node[3])
+        forces.append(t0 + t1 if side > 0 else t0 - t1)
+    if with_mass:
         rho = rho + pltpu.roll(rho, 1, 1)
-        col_m[...] = rho + pltpu.roll(rho, 1, 0)
-
-
-def elastic_steps(
-    blocks, layers, cells, zbase, mats, u, lab, dt, col_hi, col_f, col_m, modes, saved, saved_m, finish
-):
+        rho = rho + pltpu.roll(rho, 1, 0)
+    return forces, rho
+
+
+def block_forces(layers, cells, zbase, mats, u, lab, dt, modes, saved, saved_m, force, mass):
     shape = (16, 256)
     row, lane = iota(shape, 0), iota(shape, 1)
-    last = jnp.where(lax.axis_index("plane") == blocks - 1, 15, 16)
-    in_plane = jnp.where((lane < 255) & (row < last), 1.0, 0.0)
-    gap = layers // 2 * 8 + 3
-    first_row, last_row = row == 0, row == 15
+    in_plane = jnp.where((lane < 255) & (row < 15), 1.0, 0.0)
 
     def forward(e, c):
         a = u[c, e]
-        halo = jnp.broadcast_to(col_hi[c, pl.ds(e, 1), :], shape)
-        return plane_modes(a, jnp.where(last_row, halo, pltpu.roll(a, 15, 0)))
+        return plane_modes(a, pltpu.roll(a, 15, 0))
 
     for c in range(3):
         for q, value in enumerate(forward(0, c)):
             modes[4 * c + q] = value
+            saved[4 * c + q] = jnp.zeros(shape, F32)
+    if mass is not None:
+        saved_m[...] = jnp.zeros(shape, F32)
+
+    def fold(e, node):
+        for c in range(3):
+            t0, t1 = fold_y(node[c][0], node[c][1]), fold_y(node[c][2], node[c][3])
+            force[c, e] = (t0 - t1) + pltpu.roll(t0 + t1, 1, 0)
 
     def body(e, carry):
         zg = zbase + e
-        ok = (zg >= 0) & (zg <= layers * 8 - 2) & (zg != gap)
-        scale = jnp.where(ok, 1.0, 0.0)
-        l1, m1, k3, th, rho = cell_fields(mats, lab[e], dt[e], in_plane * scale, col_m is not None)
+        ok = (zg >= 0) & (zg <= layers * 8 - 2) & (zg != layers // 2 * 8 + 3)
+        mask = in_plane * jnp.where(ok, 1.0, 0.0)
+        l1, m1, k3, th, rho = cell_fields(mats, lab[e].astype(F32), dt[e], mask, mass is not None)
         lower = [[modes[4 * c + q] for q in range(4)] for c in range(3)]
         upper = [forward(e + 1, c) for c in range(3)]
         for c in range(3):
             for q in range(4):
                 modes[4 * c + q] = upper[c][q]
         low, high = cell_forces(lower, upper, l1, m1, k3, th)
-        force = []
-        for c in range(3):
-            node = [low[c][q] + saved[4 * c + q] for q in range(4)]
+        fold(e, [[low[c][q] + saved[4 * c + q] for q in range(4)] for c in range(3)])
+        for c in range(3):
             for q in range(4):
                 saved[4 * c + q] = high[c][q]
-            t0, t1 = fold_y(node[0], node[1]), fold_y(node[2], node[3])
-            halo = jnp.broadcast_to(col_f[c, pl.ds(e, 1), :], shape)
-            force.append((t0 - t1) + jnp.where(first_row, halo, pltpu.roll(t0 + t1, 1, 0)))
-        mass = None
-        if col_m is not None:
+        if mass is not None:
             rho = rho + pltpu.roll(rho, 1, 1)
-            rho = rho + jnp.where(first_row, 0.0, pltpu.roll(rho, 1, 0))
-            halo = jnp.broadcast_to(col_m[pl.ds(e, 1), :], shape)
-            mass = LUMPED + (rho + saved_m[...]) + jnp.where(first_row, halo, 0.0)
+            rho = rho + pltpu.roll(rho, 1, 0)
+            mass[e] = rho + saved_m[...]
             saved_m[...] = rho
-        finish(e, force, mass)
         return carry
 
     lax.fori_loop(0, cells, body, 0)
+    fold(cells, [[saved[4 * c + q] for q in range(4)] for c in range(3)])
+    if mass is not None:
+        mass[cells] = saved_m[...]
+
+
+def with_columns(a, first, last):
+    row = iota((8, 256), 0)
+    top = a[0:8] + jnp.where(row == 0, jnp.broadcast_to(first, (8, 256)), 0.0)
+    bottom = a[8:16] + jnp.where(row == 7, jnp.broadcast_to(last, (8, 256)), 0.0)
+    return jnp.concatenate([top, bottom], axis=0)
 
 
 def split3(a):
@@ -354,65 +375,13 @@
                     lists[5 + 2 * i + half : 6 + 2 * i + half, cols] = line[:, 128 * half : 128 * half + 128]
 
 
-def first_step(
-    blocks, layers,
-    u, v, dt, lab, par, own, near, far, opp, cols, zb, za,
-    u1, v1, dtm, out, lists,
-    ue, le, de, col_lo, col_own, col_hi, col_lab, col_dt, col_f, col_m, modes, saved, saved_m,
-):
-    layer = lax.axis_index("layer")
-    zbase = layer * 8 - 2
-    zeros = jnp.zeros((8, 256), F32)
-    for c in range(3):
-        for zz in (0, 1):
-            row = 16 * (2 * c + zz)
-            ue[c, zz] = zb[ZU_U + row : ZU_U + row + 16, :]
-            ue[c, 10 + zz] = za[ZD_U + row : ZD_U + row + 16, :]
-        ue[c, 2:10] = u[c]
-        v1[c, 0] = zb[ZU_V + 16 * c : ZU_V + 16 * c + 16, :]
-        v1[c, 9] = za[ZD_V + 16 * c : ZD_V + 16 * c + 16, :]
-        v1[c, 1:9] = v[c]
-        for col, src, zu, zd in ((col_lo, 0, ZU_CL, ZD_CL), (col_hi, COL_BEYOND, ZU_CH, ZD_CH)):
-            col[c, 8:16, :] = zeros
-            col[c, 0:2, :] = zb[zu + 2 * c : zu + 2 * c + 2, :]
-            col[c, 2:10, :] = cols[src + 8 * c : src + 8 * c + 8, :]
-            col[c, 10:12, :] = za[zd + 2 * c : zd + 2 * c + 2, :]
-        col_own[c, 8:16, :] = zeros
-        col_own[c, 0:8, :] = ue[c, 0:8, 0, :]
-        col_own[c, 8:12, :] = ue[c, 8:12, 0, :]
-    for zz in (0, 1):
-        le[zz] = zb[ZU_LAB + 16 * zz : ZU_LAB + 16 * zz + 16, :]
-        de[zz] = zb[ZU_DT + 16 * zz : ZU_DT + 16 * zz + 16, :]
-    le[2:10] = lab[...].astype(F32)
-    de[2:10] = dt[...]
-    le[10] = za[ZD_LAB : ZD_LAB + 16, :]
-    de[10] = za[ZD_DT : ZD_DT + 16, :]
-    for col, src, zu, zd in ((col_lab, COL_LAB, ZU_CLAB, ZD_CLAB), (col_dt, COL_DT, ZU_CDT, ZD_CDT)):
-        col[8:16, :] = zeros
-        col[0:2, :] = zb[zu : zu + 2, :]
-        col[2:10, :] = cols[src : src + 8, :]
-        col[10:11, :] = za[zd : zd + 1, :]
-
-    mats = material_scalars(par)
-    column_forces(blocks, layers, zbase, mats, col_lo, col_own, col_lab, col_dt, col_f, col_m)
-
-    def finish(e, force, mass):
-        at = jnp.maximum(e - 1, 0)
-        rate = DT / mass
-        dtm[at] = rate
-        for c in range(3):
-            speed = v1[c, at] - rate * force[c]
-            u1[c, at] = ue[c, e] + DT * speed
-
-            @pl.when(e > 0)
-            def _():
-                v1[c, at] = speed
-
-    elastic_steps(
-        blocks, layers, 11, zbase, mats, ue, le, de, col_hi, col_f, col_m, modes, saved, saved_m, finish
-    )
-
-    @pl.when(layer == layers // 2)
+def first_block(layers, u, dt, lab, par, force, mass, modes, saved, saved_m):
+    zbase = lax.axis_index("layer") * 8
+    block_forces(layers, 7, zbase, material_scalars(par), u, lab, dt, modes, saved, saved_m, force, mass)
+
+
+def first_contact(layers, own, near, far, opp, contact, lists):
+    @pl.when(lax.axis_index("layer") == layers // 2)
     def _():
         fill_lists(own, near, far, opp, lists)
         sol_y, sol_x = one_hots(lists[0:1, :])
@@ -432,17 +401,109 @@
             far_pad.append(gather(pads[role], far_y[:, part], far_x[:, part]))
         on_bump = lists[2:3, :] * (jnp.concatenate(far_pad, axis=1) - lists[3:6, :])
         on_pad = lists[7:8, :] * (lists[8:11, :] - gather(own_pad, land_y, land_x))
-        bump_force = scatter(on_bump, sol_y, sol_x)
-        pad_force = scatter(on_pad, land_y, land_x)
-        for c in range(3):
-            for at, extra in ((4, pad_force[c]), (5, bump_force[c])):
-                change = dtm[at] * extra
+        contact[0] = scatter(on_pad, land_y, land_x)
+        contact[1] = scatter(on_bump, sol_y, sol_x)
+
+
+def first_step(
+    blocks, layers,
+    u, v, dt, lab, par, own, cols, zb, za, force, mass, contact, lists_in,
+    u1, v1, dtm, out, lists,
+    ul, uu, ll, dl, lu, du, fl, ml, fu, mu, col, col_lab, col_dt, col_f, col_m, modes, saved, saved_m,
+):
+    layer, here = lax.axis_index("layer"), lax.axis_index("plane")
+    zeros = jnp.zeros((8, 256), F32)
+    mats = material_scalars(par)
+    for c in range(3):
+        ul[c, 2], uu[c, 0] = u[c, 0], u[c, 7]
+        for zz in (0, 1):
+            row = 16 * (2 * c + zz)
+            ul[c, zz] = zb[ZU_U + row : ZU_U + row + 16, :]
+            uu[c, 1 + zz] = za[ZD_U + row : ZD_U + row + 16, :]
+        for at, src, first, zu, zd in ((0, cols, 0, ZU_CL, ZD_CL), (3, cols, COL_BEYOND, ZU_CH, ZD_CH)):
+            col[at, c, 8:16, :] = zeros
+            col[at, c, 0:2, :] = zb[zu + 2 * c : zu + 2 * c + 2, :]
+            col[at, c, 2:10, :] = src[first + 8 * c : first + 8 * c + 8, :]
+            col[at, c, 10:12, :] = za[zd + 2 * c : zd + 2 * c + 2, :]
+        for at, first, x in ((1, COL_LO, 0), (2, COL_HI, 15)):
+            col[at, c, 8:16, :] = zeros
+            col[at, c, 2:10, :] = own[first + 8 * c : first + 8 * c + 8, :]
+            for zz in (0, 1):
+                row = 16 * (2 * c + zz) + x
+                col[at, c, zz : zz + 1, :] = zb[ZU_U + row : ZU_U + row + 1, :]
+                col[at, c, 10 + zz : 11 + zz, :] = za[ZD_U + row : ZD_U + row + 1, :]
+    for zz in (0, 1):
+        ll[zz] = zb[ZU_LAB + 16 * zz : ZU_LAB + 16 * zz + 16, :]
+        dl[zz] = zb[ZU_DT + 16 * zz : ZU_DT + 16 * zz + 16, :]
+    lu[0], du[0] = lab[7].astype(F32), dt[7]
+    lu[1], du[1] = za[ZD_LAB : ZD_LAB + 16, :], za[ZD_DT : ZD_DT + 16, :]
+    for ref, first, zu, zd, zuf, zdf in (
+        (col_lab, COL_LAB, ZU_CLAB, ZD_CLAB, ZU_LAB, ZD_LAB),
+        (col_dt, COL_DT, ZU_CDT, ZD_CDT, ZU_DT, ZD_DT),
+    ):
+        for at in (0, 1):
+            ref[at, 8:16, :] = zeros
+        ref[0, 0:2, :] = zb[zu : zu + 2, :]
+        ref[0, 2:10, :] = cols[first : first + 8, :]
+        ref[0, 10:11, :] = za[zd : zd + 1, :]
+        for zz in (0, 1):
+            ref[1, zz : zz + 1, :] = zb[zuf + 16 * zz + 15 : zuf + 16 * zz + 16, :]
+        ref[1, 2:10, :] = own[COL_HI + first : COL_HI + first + 8, :]
+        ref[1, 10:11, :] = za[zdf + 15 : zdf + 16, :]
+
+    zbase = layer * 8 - 2
+    block_forces(layers, 2, zbase, mats, ul, ll, dl, modes, saved, saved_m, fl, ml)
+    block_forces(layers, 2, zbase + 9, mats, uu, lu, du, modes, saved, saved_m, fu, mu)
+    for at, inside, side in ((0, here > 0, 1), (1, here < blocks - 1, -1)):
+        left = [col[2 * at, c] for c in range(3)]
+        right = [col[2 * at + 1, c] for c in range(3)]
+        forces, rho = column_forces(
+            layers, zbase, mats, inside, side, left, right, col_lab[at], col_dt[at], True
+        )
+        for c in range(3):
+            col_f[at, c] = forces[c]
+        col_m[at] = rho
+
+    for i in range(10):
+        z, e = i - 1, i + 1
+        total = mass[z] if 0 <= z < 8 else 0.0
+        if z < 1:
+            total = total + ml[e]
+        if z > 6:
+            total = total + mu[z - 7]
+        total = LUMPED + with_columns(total, col_m[0, e : e + 1, :], col_m[1, e : e + 1, :])
+        rate = DT / total
+        dtm[i] = rate
+        for c in range(3):
+            pull = force[c, z] if 0 <= z < 8 else 0.0
+            if z < 1:
+                pull = pull + fl[c, e]
+            if z > 6:
+                pull = pull + fu[c, z - 7]
+            pull = with_columns(pull, col_f[0, c, e : e + 1, :], col_f[1, c, e : e + 1, :])
+            if z < 0:
+                speed, place = zb[ZU_V + 16 * c : ZU_V + 16 * c + 16, :], ul[c, 1]
+            elif z > 7:
+                speed, place = za[ZD_V + 16 * c : ZD_V + 16 * c + 16, :], uu[c, 1]
+            else:
+                speed, place = v[c, z], u[c, z]
+            speed = speed - rate * pull
+            v1[c, i] = speed
+            u1[c, i] = place + DT * speed
+
+    @pl.when(layer == layers // 2)
+    def _():
+        for c in range(3):
+            for face in (0, 1):
+                at = 4 + face
+                change = dtm[at] * contact[face, c]
                 v1[c, at] = v1[c, at] + change
                 u1[c, at] = u1[c, at] + DT * change
+        lists[...] = lists_in[...]
         new_pad = jnp.concatenate([u1[c, 4] for c in range(3)], axis=0)
         new_bump = jnp.concatenate([u1[c, 5] for c in range(3)], axis=0)
-        lists[3:6, :] = gather(new_bump, sol_y, sol_x)
-        lists[8:11, :] = gather(new_pad, land_y, land_x)
+        lists[3:6, :] = gather(new_bump, *one_hots(lists[0:1, :]))
+        lists[8:11, :] = gather(new_pad, *one_hots(lists[6:7, :]))
         for role in range(5):
             part = slice(128 * role, 128 * role + 128)
             for i, row in enumerate((3, 4, 5, 8, 9, 10)):
@@ -455,47 +516,76 @@
             out[row + 10 * c + 8 : row + 10 * c + 10, :] = u1[c, 8:10, x, :]
 
 
-def second_step(
-    blocks, layers,
-    u, v, dtm, dt, lab, par, lists, cols, zb, own, near, far, opp,
-    u2, v2,
-    le, de, col_lo, col_own, col_hi, col_lab, col_dt, col_f, modes, saved,
-):
-    layer = lax.axis_index("layer")
-    zbase = layer * 8 - 1
-    zeros = jnp.zeros((8, 256), F32)
-    even = on_even()
-    for c in range(3):
-        at, hi, lo = 10 * c, NEW_HI + 10 * c, NEW_LO + 10 * c
-        col_lo[c, 8:16, :] = zeros
-        col_hi[c, 8:16, :] = zeros
-        col_own[c, 8:16, :] = zeros
-        col_lo[c, 0:10, :] = jnp.where(even, far[at : at + 10, :], near[hi : hi + 10, :])
-        col_hi[c, 0:10, :] = jnp.where(even, near[lo : lo + 10, :], far[at : at + 10, :])
-        col_own[c, 0:10, :] = own[lo : lo + 10, :]
+def second_block(layers, u, dt, lab, par, zb, force, le, de, modes, saved):
     le[0] = zb[ZU_LAB + 16 : ZU_LAB + 32, :]
     de[0] = zb[ZU_DT + 16 : ZU_DT + 32, :]
     le[1:9] = lab[...].astype(F32)
     de[1:9] = dt[...]
-    for col, src, zu in ((col_lab, COL_LAB, ZU_CLAB), (col_dt, COL_DT, ZU_CDT)):
-        col[8:16, :] = zeros
-        col[0:1, :] = zb[zu + 1 : zu + 2, :]
-        col[1:9, :] = cols[src : src + 8, :]
-
+    zbase = lax.axis_index("layer") * 8 - 1
+    block_forces(layers, 9, zbase, material_scalars(par), u, le, de, modes, saved, None, force, None)
+
+
+def second_step(
+    blocks, layers,
+    u, v, dtm, dt, lab, par, force, cols, zb, own, near, far,
+    u2, v2,
+    col, col_lab, col_dt, col_f,
+):
+    layer, here = lax.axis_index("layer"), lax.axis_index("plane")
+    zeros = jnp.zeros((8, 256), F32)
     mats = material_scalars(par)
-    column_forces(blocks, layers, zbase, mats, col_lo, col_own, col_lab, col_dt, col_f, None)
-
-    def finish(e, force, mass):
-        at = jnp.maximum(e - 1, 0)
+    even = on_even()
+    for c in range(3):
+        at, hi, lo = 10 * c, NEW_HI + 10 * c, NEW_LO + 10 * c
+        for i in range(4):
+            col[i, c, 8:16, :] = zeros
+        col[0, c, 0:10, :] = jnp.where(even, far[at : at + 10, :], near[hi : hi + 10, :])
+        col[1, c, 0:10, :] = own[lo : lo + 10, :]
+        col[2, c, 0:10, :] = own[hi : hi + 10, :]
+        col[3, c, 0:10, :] = jnp.where(even, near[lo : lo + 10, :], far[at : at + 10, :])
+    for ref, src, first, zu, zuf in (
+        (col_lab, lab, COL_LAB, ZU_CLAB, ZU_LAB),
+        (col_dt, dt, COL_DT, ZU_CDT, ZU_DT),
+    ):
+        for at in (0, 1):
+            ref[at, 8:16, :] = zeros
+        ref[0, 0:1, :] = zb[zu + 1 : zu + 2, :]
+        ref[0, 1:9, :] = cols[first : first + 8, :]
+        ref[1, 0:1, :] = zb[zuf + 31 : zuf + 32, :]
+        ref[1, 1:9, :] = src[:, 15, :].astype(F32)
+    for at, inside, side in ((0, here > 0, 1), (1, here < blocks - 1, -1)):
+        left = [col[2 * at, c] for c in range(3)]
+        right = [col[2 * at + 1, c] for c in range(3)]
+        forces, _ = column_forces(
+            layers, layer * 8 - 1, mats, inside, side, left, right, col_lab[at], col_dt[at], False
+        )
+        for c in range(3):
+            col_f[at, c] = forces[c]
+    for z in range(8):
+        e = z + 1
         rate = dtm[e]
         for c in range(3):
-            speed = v[c, e] - rate * force[c]
-            v2[c, at] = speed
-            u2[c, at] = u[c, e] + DT * speed
-
-    elastic_steps(blocks, layers, 9, zbase, mats, u, le, de, col_hi, col_f, None, modes, saved, None, finish)
-
-    @pl.when(layer == layers // 2)
+            pull = with_columns(force[c, e], col_f[0, c, e : e + 1, :], col_f[1, c, e : e + 1, :])
+            speed = v[c, e] - rate * pull
+            v2[c, z] = speed
+            u2[c, z] = u[c, e] + DT * speed
+
+
+def second_contact(layers, u, v, dtm, lists, near, far, opp, u2, v2, faces, sems):
+    copies = []
+    for i, (src, dst) in enumerate(((u, u2), (v, v2))):
+        for first, last in ((0, 3), (5, 8)):
+            copies.append(
+                pltpu.make_async_copy(src.at[:, first:last], dst.at[:, first:last], sems.at[len(copies)])
+            )
+    for copy in copies:
+        copy.start()
+    for c in range(3):
+        for face in (0, 1):
+            faces[0, c, face] = u[c, 3 + face]
+            faces[1, c, face] = v[c, 3 + face]
+
+    @pl.when(lax.axis_index("layer") == layers // 2)
     def _():
         sol_y, sol_x = one_hots(lists[0:1, :])
         land_y, land_x = one_hots(lists[6:7, :])
@@ -517,13 +607,19 @@
         far_pad = jnp.concatenate([values(i) for i in range(3, 6)], axis=0)
         on_bump = lists[2:3, :] * (far_pad - lists[3:6, :])
         on_pad = lists[7:8, :] * (far_bump - lists[8:11, :])
-        bump_force = scatter(on_bump, sol_y, sol_x)
-        pad_force = scatter(on_pad, land_y, land_x)
-        for c in range(3):
-            for at, extra in ((3, pad_force[c]), (4, bump_force[c])):
-                change = dtm[at + 1] * extra
-                v2[c, at] = v2[c, at] + change
-                u2[c, at] = u2[c, at] + DT * change
+        extra = (scatter(on_pad, land_y, land_x), scatter(on_bump, sol_y, sol_x))
+        for c in range(3):
+            for face in (0, 1):
+                change = dtm[4 + face] * extra[face][c]
+                faces[0, c, face] = faces[0, c, face] + DT * change
+                faces[1, c, face] = faces[1, c, face] + change
+
+    for i, dst in enumerate((u2, v2)):
+        copy = pltpu.make_async_copy(faces.at[i], dst.at[:, 3:5], sems.at[4 + i])
+        copy.start()
+        copies.append(copy)
+    for copy in copies:
+        copy.wait()
 
 
 VM = pl.BlockSpec(memory_space=pltpu.VMEM)
@@ -531,14 +627,14 @@
 HBM = pl.BlockSpec(memory_space=pltpu.HBM)
 
 
-def call(kernel, in_specs, outs, scratch, name, flops):
+def call(kernel, in_specs, outs, scratch, name, flops, vmem=32, out_spec=VM):
     return pl.pallas_call(
         kernel,
         out_shape=[jax.ShapeDtypeStruct(shape, F32) for shape in outs],
         in_specs=in_specs,
-        out_specs=[VM] * len(outs),
+        out_specs=[out_spec] * len(outs),
         scratch_shapes=[pltpu.VMEM(s, F32) if isinstance(s, tuple) else s for s in scratch],
-        compiler_params=pltpu.CompilerParams(vmem_limit_bytes=32 * 1024 * 1024),
+        compiler_params=pltpu.CompilerParams(vmem_limit_bytes=vmem * 1024 * 1024),
         cost_estimate=pl.CostEstimate(flops=flops, bytes_accessed=2_000_000, transcendentals=0),
         name=name,
     )
@@ -560,42 +656,85 @@
         [(EXPORT_ROWS, 256)],
         [u.shape, dt.shape, pltpu.VMEM(lab.shape, jnp.int32)]
         + [pltpu.VMEM((5, 1, 128), jnp.int32)] * 2
-        + [(5, 1, 128), pltpu.SMEM((1, 5), jnp.int32), pltpu.VMEM((8, 640), jnp.int32), pltpu.SemaphoreType.DMA((7,))],
+        + [(5, 1, 128), pltpu.SMEM((1, 5), jnp.int32), pltpu.VMEM((8, 640), jnp.int32)]
+        + [pltpu.VMEM((256, 640), BF16), (16, 640), pltpu.SemaphoreType.DMA((7,))],
         "pack_export",
         100_000,
+        63,
     )(u, dt, lab, sol.reshape(5, 1, 128), land.reshape(5, 1, 128), stiff.reshape(5, 1, 128), tally)[0]
     near = lax.ppermute(own, "plane", swaps)
+    own = call(stage, [HBM], [own.shape], [pltpu.SemaphoreType.DMA], "stage", 100_000)(own)[0]
     cross = call(pack_cross, [VM] * 2, [(CROSS_ROWS, 256)], [], "pack_cross", 100_000)(own, near)[0]
     far = lax.ppermute(cross, "plane", crossings)
+    modes = [(12, 16, 256), (12, 16, 256)]
+    plane = (16, 256)
+    force, mass = call(
+        functools.partial(first_block, layers),
+        [VM] * 3 + [SM],
+        [(3, 8, 16, 256), (8, 16, 256)],
+        modes + [plane],
+        "first_block",
+        50_000_000,
+    )(u, dt, lab, par)
+    far, force, mass = lax.optimization_barrier((far, force, mass))
     up, dn, cols = call(
         pack_layer, [VM] * 6, [(ZU_ROWS, 256), (ZD_ROWS, 256), (COLS_ROWS, 256)], [], "pack_layer", 100_000
     )(u, v, dt, lab, near, far)
     zb, za = along_layer(up, 1), along_layer(dn, -1)
     opp = lax.ppermute(far, ("plane", "layer"), face_swaps)
-
-    col, plane = (3, 16, 256), (16, 256)
+    contact, lists = call(
+        functools.partial(first_contact, layers),
+        [VM] * 4,
+        [(2, 3, 16, 256), (16, 640)],
+        [],
+        "first_contact",
+        10_000_000,
+    )(own, near, far, opp)
+
+    three, two = [(3, 3, 16, 256)] * 2 + [(2, 16, 256)] * 4, (2, 16, 256)
     u1, v1, dtm, own, lists = call(
         functools.partial(first_step, blocks, layers),
-        [VM] * 4 + [SM] + [VM] * 7,
+        [VM] * 4 + [SM] + [VM] * 8,
         [(3, 10, 16, 256), (3, 10, 16, 256), (10, 16, 256), (NEW_ROWS, 256), (16, 640)],
-        [(3, 12, 16, 256), (11, 16, 256), (11, 16, 256), col, col, col, plane, plane, col, plane]
-        + [(12, 16, 256), (12, 16, 256), plane],
+        three
+        + [(3, 3, 16, 256), (3, 16, 256)] * 2
+        + [(4, 3, 16, 256), two, two, (2, 3, 16, 256), two]
+        + modes
+        + [plane],
         "first_step",
-        50_000_000,
-    )(u, v, dt, lab, par, own, near, far, opp, cols, zb, za)
+        20_000_000,
+    )(u, v, dt, lab, par, own, cols, zb, za, force, mass, contact, lists)
     near = lax.ppermute(own, "plane", swaps)
     cross = call(pack_new_cross, [VM] * 2, [(NEW_CROSS_ROWS, 256)], [], "pack_new_cross", 100_000)(own, near)[0]
     far = lax.ppermute(cross, "plane", crossings)
+    force = call(
+        functools.partial(second_block, layers),
+        [VM] * 3 + [SM, VM],
+        [(3, 10, 16, 256)],
+        [(9, 16, 256), (9, 16, 256)] + modes,
+        "second_block",
+        50_000_000,
+    )(u1, dt, lab, par, zb)[0]
+    far, force = lax.optimization_barrier((far, force))
     opp = lax.ppermute(far, ("plane", "layer"), face_swaps)
+    u2, v2 = call(
+        functools.partial(second_step, blocks, layers),
+        [VM] * 5 + [SM] + [VM] * 6,
+        [(3, 8, 16, 256)] * 2,
+        [(4, 3, 16, 256), two, two, (2, 3, 16, 256)],
+        "second_step",
+        20_000_000,
+    )(u1, v1, dtm, dt, lab, par, force, cols, zb, own, near, far)
     return tuple(
         call(
-            functools.partial(second_step, blocks, layers),
-            [VM] * 5 + [SM] + [VM] * 7,
-            [(3, 8, 16, 256), (3, 8, 16, 256)],
-            [(9, 16, 256), (9, 16, 256), col, col, col, plane, plane, col] + [(12, 16, 256), (12, 16, 256)],
-            "second_step",
-            50_000_000,
-        )(u1, v1, dtm, dt, lab, par, lists, cols, zb, own, near, far, opp)
+            functools.partial(second_contact, layers),
+            [VM] * 7,
+            [(3, 8, 16, 256)] * 2,
+            [(2, 3, 2, 16, 256), pltpu.SemaphoreType.DMA((6,))],
+            "second_contact",
+            10_000_000,
+            out_spec=HBM,
+        )(u2, v2, dtm, lists, near, far, opp)
     )
 
 

time: 56.2 us -> 48 us (0.85)
  waiting for transfers between devices: 8.18 us -> 2.14 us
  local copies, waits for them, and re-layouts: 4.19 us -> 0.93 us
  Pallas kernels: 10.2 us -> 12.9 us
  starting transfers between devices: 32.4 us -> 30.8 us
    pallas_call x0 -> x5, Pallas kernels: none -> 7.08 us  [the longest x1 2.79 us: local(): call(functools.partial(second_block, layers), [VM] * 3 + [SM, VM], [(3, 1...]
    ppermute x2, waiting for transfers between devices: 4.39 us -> 0.09 us  [local(): far = lax.ppermute(cross, 'plane', crossings)]
    unnamed x24 -> x12, local copies, waits for them, and re-layouts: 4.19 us -> 0.93 us
    pallas_call x1, Pallas kernels: 4.22 us -> 1.03 us  [local(): call(functools.partial(second_step, blocks, layers), [VM] * 5 + [SM] + [V...]
    pallas_call x1, Pallas kernels: 4.5 us -> 2.64 us  [local(): call(functools.partial(first_step, blocks, layers), [VM] * 4 + [SM] + [VM...]
    ppermute x2, starting transfers between devices: 13.7 us -> 12.7 us  [local(): opp = lax.ppermute(far, ('plane', 'layer'), face_swaps)]
    ppermute x2, waiting for transfers between devices: 1.89 us -> 0.99 us  [local(): near = lax.ppermute(own, 'plane', swaps)]
    ppermute x2, waiting for transfers between devices: 1.9 us -> 1.04 us  [local(): opp = lax.ppermute(far, ('plane', 'layer'), face_swaps)]
  transfers between devices with their start and end apart: 8 -> 8, of which waited for: 6 -> 4; matrix products, arithmetic and copies ran while one was open for 0% -> 0% of each run, Pallas kernels for 0% -> 15%
where the time goes in v3:
time: 48 us; the launch traced here: 47.7 us
  starting transfers between devices  30.8 us (64%)
  Pallas kernels  12.9 us (27%)
  waiting for transfers between devices  2.14 us (4%)
  local copies, waits for them, and re-layouts  0.93 us (2%)
  between operations  0.86 us (2%)
    ppermute x2, starting transfers between devices, local(): opp = lax.ppermute(far, ('plane', 'layer'), face_swaps)  12.7 us
    ppermute x2, starting transfers between devices, local(): far = lax.ppermute(cross, 'plane', crossings)  7.27 us
    ppermute x2, starting transfers between devices, local(): near = lax.ppermute(own, 'plane', swaps)  5.55 us
    ppermute x2, starting transfers between devices, along_layer(): return lax.ppermute(value, 'layer', pairs)  5.28 us
    pallas_call x1, Pallas kernels, local(): call(functools.partial(second_block, layers), [VM] * 3 + [SM, VM], [(3, 1...  2.79 us
    pallas_call x1, Pallas kernels, local(): call(functools.partial(first_step, blocks, layers), [VM] * 4 + [SM] + [VM...  2.64 us
    pallas_call x1, Pallas kernels, local(): call(functools.partial(first_block, layers), [VM] * 3 + [SM], [(3, 8, 16,...  2.38 us
    pallas_call x1, Pallas kernels, local(): call(functools.partial(pack_export, blocks, layers), [HBM] * 7, [(EXPORT_...  2.09 us
  transfers between devices with their start and end apart: 8, of which 4 were waited for; matrix products, arithmetic and copies ran while one was open for 0% of the time, Pallas kernels for 15%

profile of v3, /device:TPU:261, one launch (start us, length us, event | category | flops | bytes accessed | tf_op | source)
XLA Modules:
  0.0 47.7 jit_solution(12398786211529228443)
XLA Ops:
  0.6 2.1 %pack_export.1.src = f32[136,256]{1,0:T(8,128)} custom-call(f32[3,8,16,256]{3,2,1,0:T(8,128)} %u.5, f32[8,16,256]{2,1,0:T(8,128)} %dt.9, s32[8,16,256]{2,1,0:T(8,128)} %lab.9, s32[5,1,128]{2,1,0:T(1,128)} %bitcast.3, s32[5,1,128]{2,1,0:T(1,128)} %bitcast.4, f32[5,1,128]{2,1,0:T(1,128)} %bitcast.5, s32[1,5]{1,0:T(1,128)} %tally_hbm.1), custom_call_target="tpu_custom_call" | custom-call | flops 100000 | bytes 2000000 | tf_op jit(solution)/shard_map/pack_export/pallas_call | solution.py:653
  2.7 0.0 copy-start
  2.7 2.7 %collective-permute-start = (f32[136,256]{1,0:T(8,128)}, f32[136,256]{1,0:T(8,128)S(1)}, u32[]{:S(2)}, u32[]{:S(2)}) collective-permute-start(f32[136,256]{1,0:T(8,128)} %pack_export.1.src), channel_id=1, source_target_pairs={{0,4},{4,0},{8,12},{12,8},{16,20},{20,16},{24,28},{28,24},{32,36},... | collective-permute-start | bytes 417800 | tf_op jit(solution)/shard_map/ppermute | solution.py:665
  5.5 0.9 %copy-done.4 = f32[136,256]{1,0:T(8,128)S(1)} copy-done((f32[136,256]{1,0:T(8,128)S(1)}, f32[136,256]{1,0:T(8,128)}, u32[]{:S(2)}) %copy-start.4) | copy-done | bytes 139288
  6.4 0.2 stage.1.own
  6.6 0.0 copy-start.5
  6.6 0.1 collective-permute-done.mate.near
  6.7 4.3 %collective-permute-start.1 = (f32[184,256]{1,0:T(8,128)S(1)}, f32[184,256]{1,0:T(8,128)S(1)}, u32[]{:S(2)}, u32[]{:S(2)}) collective-permute-start(f32[184,256]{1,0:T(8,128)S(1)} %pack_cross.1), channel_id=1, source_target_pairs={{0,8},{8,16},{12,4},{16,24},{20,12},{24,32},{28,20},{32,40},{36,28... | collective-permute-start | bytes 565256 | tf_op jit(solution)/shard_map/ppermute | solution.py:668
  11.0 2.4 %first_block.1 = (f32[3,8,16,256]{3,2,1,0:T(8,128)S(1)}, f32[8,16,256]{2,1,0:T(8,128)S(1)}) custom-call(f32[3,8,16,256]{3,2,1,0:T(8,128)S(1)} %copy-done, f32[8,16,256]{2,1,0:T(8,128)S(1)} %copy-done.1, s32[8,16,256]{2,1,0:T(8,128)S(1)} %copy-done.2, f32[4,4]{1,0:T(4,128)S(1)} %copy-done.5), custom_call_target="tpu_custom_call" | custom-call | flops 50000000 | bytes 2000000 | tf_op jit(solution)/shard_map/first_block/pallas_call | solution.py:671
  13.4 0.1 collective-permute-done.1.far
  13.6 2.6 %collective-permute-start.2 = (f32[224,256]{1,0:T(8,128)S(1)}, f32[224,256]{1,0:T(8,128)S(1)}, u32[]{:S(2)}, u32[]{:S(2)}) collective-permute-start(f32[224,256]{1,0:T(8,128)S(1)} %get-tuple-element.25), channel_id=1, source_target_pairs={{0,1},{1,2},{2,3},{4,5},{5,6},{6,7},{8,9},{9,10},{10,11},{12,13},{... | collective-permute-start | bytes 688136 | tf_op jit(solution)/shard_map/ppermute | solution.py:651
  16.1 2.7 %collective-permute-start.3 = (f32[192,256]{1,0:T(8,128)S(1)}, f32[192,256]{1,0:T(8,128)S(1)}, u32[]{:S(2)}, u32[]{:S(2)}) collective-permute-start(f32[192,256]{1,0:T(8,128)S(1)} %get-tuple-element.26), channel_id=1, source_target_pairs={{1,0},{2,1},{3,2},{5,4},{6,5},{7,6},{9,8},{10,9},{11,10},{13,12},{... | collective-permute-start | bytes 589832 | tf_op jit(solution)/shard_map/ppermute | solution.py:651
  18.9 6.9 %collective-permute-start.4 = (f32[184,256]{1,0:T(8,128)S(1)}, f32[184,256]{1,0:T(8,128)S(1)}, u32[]{:S(2)}, u32[]{:S(2)}) collective-permute-start(f32[184,256]{1,0:T(8,128)S(1)} %collective-permute-done.1.far), channel_id=1, source_target_pairs={{2,6},{6,2},{10,14},{14,10},{18,22},{22,18},{26,30},{30,26},{34,38... | collective-permute-start | bytes 565256 | tf_op jit(solution)/shard_map/ppermute | solution.py:684
  25.8 1.0 %collective-permute-done.4.opp = f32[184,256]{1,0:T(8,128)S(1)} collective-permute-done((f32[184,256]{1,0:T(8,128)S(1)}, f32[184,256]{1,0:T(8,128)S(1)}, u32[]{:S(2)}, u32[]{:S(2)}) %collective-permute-start.4) | collective-permute-done | bytes 188448 | tf_op jit(solution)/shard_map/ppermute | solution.py:684
  26.8 0.6 %first_contact.1 = (f32[2,3,16,256]{3,2,1,0:T(8,128)S(1)}, f32[16,640]{1,0:T(8,128)S(1)}) custom-call(f32[136,256]{1,0:T(8,128)S(1)} %stage.1.own, f32[136,256]{1,0:T(8,128)S(1)} %collective-permute-done.mate.near, f32[184,256]{1,0:T(8,128)S(1)} %collective-permute-done.1.far, f32[184,256]{1,0:T(8,128)S(1)} %collective-permute-done.4.opp), custom_call_target="tpu_custom_call" | custom-call | flops 10000000 | bytes 2000000 | tf_op jit(solution)/shard_map/first_contact/pallas_call | solution.py:685
  27.5 0.0 collective-permute-done.3.za
  27.5 2.6 %first_step.1 = (f32[3,10,16,256]{3,2,1,0:T(8,128)S(1)}, f32[3,10,16,256]{3,2,1,0:T(8,128)S(1)}, f32[10,16,256]{2,1,0:T(8,128)S(1)}, f32[88,256]{1,0:T(8,128)S(1)}, f32[16,640]{1,0:T(8,128)S(1)}) custom-call(f32[3,8,16,256]{3,2,1,0:T(8,128)S(1)} %copy-done, f32[3,8,16,256]{3,2,1,0:T(8,128)S(1)} %copy-done.3, f32[8,16,256]{2,1,0:T(8,128)S(1)} %copy-done.1, ...), custom_call_target="tpu_custom_call" | custom-call | flops 20000000 | bytes 2000000 | tf_op jit(solution)/shard_map/first_step/pallas_call | solution.py:695
  30.2 2.8 %collective-permute-start.5 = (f32[88,256]{1,0:T(8,128)S(1)}, f32[88,256]{1,0:T(8,128)S(1)}, u32[]{:S(2)}, u32[]{:S(2)}) collective-permute-start(f32[88,256]{1,0:T(8,128)S(1)} %get-tuple-element.34.own), channel_id=1, source_target_pairs={{0,4},{4,0},{8,12},{12,8},{16,20},{20,16},{24,28},{28,24},{32,36},... | collective-permute-start | bytes 270344 | tf_op jit(solution)/shard_map/ppermute | solution.py:707
  33.0 0.9 %collective-permute-done.5.mate.near = f32[88,256]{1,0:T(8,128)S(1)} collective-permute-done((f32[88,256]{1,0:T(8,128)S(1)}, f32[88,256]{1,0:T(8,128)S(1)}, u32[]{:S(2)}, u32[]{:S(2)}) %collective-permute-start.5) | collective-permute-done | bytes 90144 | tf_op jit(solution)/shard_map/ppermute | solution.py:707
  33.9 2.9 %collective-permute-start.6 = (f32[48,256]{1,0:T(8,128)S(1)}, f32[48,256]{1,0:T(8,128)S(1)}, u32[]{:S(2)}, u32[]{:S(2)}) collective-permute-start(f32[48,256]{1,0:T(8,128)S(1)} %pack_new_cross.1), channel_id=1, source_target_pairs={{0,8},{8,16},{12,4},{16,24},{20,12},{24,32},{28,20},{32,40},{36,28... | collective-permute-start | bytes 147464 | tf_op jit(solution)/shard_map/ppermute | solution.py:709
  36.9 2.8 %second_block.1.force = f32[3,10,16,256]{3,2,1,0:T(8,128)S(1)} custom-call(f32[3,10,16,256]{3,2,1,0:T(8,128)S(1)} %get-tuple-element.31.u, f32[8,16,256]{2,1,0:T(8,128)S(1)} %copy-done.1, s32[8,16,256]{2,1,0:T(8,128)S(1)} %copy-done.2, f32[4,4]{1,0:T(4,128)S(1)} %copy-done.5, f32[224,256]{1,0:T(8,128)S(1)} %collective-permute-done.2.zb), custom_call_target="tpu_custom_call" | custom-call | flops 50000000 | bytes 2000000 | tf_op jit(solution)/shard_map/second_block/pallas_call | solution.py:710
  39.7 5.8 %collective-permute-start.7 = (f32[48,256]{1,0:T(8,128)S(1)}, f32[48,256]{1,0:T(8,128)S(1)}, u32[]{:S(2)}, u32[]{:S(2)}) collective-permute-start(f32[48,256]{1,0:T(8,128)S(1)} %collective-permute-done.6.far), channel_id=1, source_target_pairs={{2,6},{6,2},{10,14},{14,10},{18,22},{22,18},{26,30},{30,26},{34,38... | collective-permute-start | bytes 147464 | tf_op jit(solution)/shard_map/ppermute | solution.py:719
  45.5 1.0 %second_step.1 = (f32[3,8,16,256]{3,2,1,0:T(8,128)S(1)}, f32[3,8,16,256]{3,2,1,0:T(8,128)S(1)}) custom-call(f32[3,10,16,256]{3,2,1,0:T(8,128)S(1)} %get-tuple-element.31.u, f32[3,10,16,256]{3,2,1,0:T(8,128)S(1)} %get-tuple-element.32.v, f32[10,16,256]{2,1,0:T(8,128)S(1)} %get-tuple-element.33.dtm, f32[8,16,256]{2,1,0:T(8,128)S(1)} %copy-done.1, ...), custom_call_target="tpu_custom_call" | custom-call | flops 20000000 | bytes 2000000 | tf_op jit(solution)/shard_map/second_step/pallas_call | solution.py:720
  46.5 1.1 %second_contact.1 = (f32[3,8,16,256]{3,2,1,0:T(8,128)}, f32[3,8,16,256]{3,2,1,0:T(8,128)}) custom-call(f32[3,8,16,256]{3,2,1,0:T(8,128)S(1)} %get-tuple-element.37.u, f32[3,8,16,256]{3,2,1,0:T(8,128)S(1)} %get-tuple-element.38.v, f32[10,16,256]{2,1,0:T(8,128)S(1)} %get-tuple-element.33.dtm, f32[16,640]{1,0:T(8,128)S(1)} %get-tuple-element.39.lists, ...), custom_call_target="tpu_custom_call" | custom-call | flops 10000000 | bytes 2000000 | tf_op jit(solution)/shard_map/second_contact/pallas_call | solution.py:729
  (15 shorter events, 0.1 us)
Async XLA Ops:
  2.7 8.3 %copy-start = (f32[3,8,16,256]{3,2,1,0:T(8,128)S(1)}, f32[3,8,16,256]{3,2,1,0:T(8,128)}, u32[]{:S(2)}) copy-start(f32[3,8,16,256]{3,2,1,0:T(8,128)} %u.5) | copy-start | bytes 1179652
  2.7 3.9 %collective-permute-start = (f32[136,256]{1,0:T(8,128)}, f32[136,256]{1,0:T(8,128)S(1)}, u32[]{:S(2)}, u32[]{:S(2)}) collective-permute-start(f32[136,256]{1,0:T(8,128)} %pack_export.1.src), channel_id=1, source_target_pairs={{0,4},{4,0},{8,12},{12,8},{16,20},{20,16},{24,28},{28,24},{32,36},... | collective-permute-start | bytes 417800 | tf_op jit(solution)/shard_map/ppermute | solution.py:665
  5.5 0.9 %copy-start.4 = (f32[136,256]{1,0:T(8,128)S(1)}, f32[136,256]{1,0:T(8,128)}, u32[]{:S(2)}) copy-start(f32[136,256]{1,0:T(8,128)} %pack_export.1.src) | copy-start | bytes 417796
  6.5 4.5 %copy-start.1 = (f32[8,16,256]{2,1,0:T(8,128)S(1)}, f32[8,16,256]{2,1,0:T(8,128)}, u32[]{:S(2)}) copy-start(f32[8,16,256]{2,1,0:T(8,128)} %dt.9) | copy-start | bytes 393220
  6.5 4.5 %copy-start.2 = (s32[8,16,256]{2,1,0:T(8,128)S(1)}, s32[8,16,256]{2,1,0:T(8,128)}, u32[]{:S(2)}) copy-start(s32[8,16,256]{2,1,0:T(8,128)} %lab.9) | copy-start | bytes 393220
  6.6 4.5 %copy-start.5 = (f32[4,4]{1,0:T(4,128)S(1)}, f32[4,4]{1,0:T(4,128)}, u32[]{:S(2)}) copy-start(f32[4,4]{1,0:T(4,128)} %par.7) | copy-start | bytes 196
  6.7 6.8 %copy-start.3 = (f32[3,8,16,256]{3,2,1,0:T(8,128)S(1)}, f32[3,8,16,256]{3,2,1,0:T(8,128)}, u32[]{:S(2)}) copy-start(f32[3,8,16,256]{3,2,1,0:T(8,128)} %v.3) | copy-start | bytes 1179652
  6.7 6.8 %collective-permute-start.1 = (f32[184,256]{1,0:T(8,128)S(1)}, f32[184,256]{1,0:T(8,128)S(1)}, u32[]{:S(2)}, u32[]{:S(2)}) collective-permute-start(f32[184,256]{1,0:T(8,128)S(1)} %pack_cross.1), channel_id=1, source_target_pairs={{0,8},{8,16},{12,4},{16,24},{20,12},{24,32},{28,20},{32,40},{36,28... | collective-permute-start | bytes 565256 | tf_op jit(solution)/shard_map/ppermute | solution.py:668
  13.6 13.9 %collective-permute-start.2 = (f32[224,256]{1,0:T(8,128)S(1)}, f32[224,256]{1,0:T(8,128)S(1)}, u32[]{:S(2)}, u32[]{:S(2)}) collective-permute-start(f32[224,256]{1,0:T(8,128)S(1)} %get-tuple-element.25), channel_id=1, source_target_pairs={{0,1},{1,2},{2,3},{4,5},{5,6},{6,7},{8,9},{9,10},{10,11},{12,13},{... | collective-permute-start | bytes 688136 | tf_op jit(solution)/shard_map/ppermute | solution.py:651
  16.1 11.3 %collective-permute-start.3 = (f32[192,256]{1,0:T(8,128)S(1)}, f32[192,256]{1,0:T(8,128)S(1)}, u32[]{:S(2)}, u32[]{:S(2)}) collective-permute-start(f32[192,256]{1,0:T(8,128)S(1)} %get-tuple-element.26), channel_id=1, source_target_pairs={{1,0},{2,1},{3,2},{5,4},{6,5},{7,6},{9,8},{10,9},{11,10},{13,12},{... | collective-permute-start | bytes 589832 | tf_op jit(solution)/shard_map/ppermute | solution.py:651
  18.9 8.0 %collective-permute-start.4 = (f32[184,256]{1,0:T(8,128)S(1)}, f32[184,256]{1,0:T(8,128)S(1)}, u32[]{:S(2)}, u32[]{:S(2)}) collective-permute-start(f32[184,256]{1,0:T(8,128)S(1)} %collective-permute-done.1.far), channel_id=1, source_target_pairs={{2,6},{6,2},{10,14},{14,10},{18,22},{22,18},{26,30},{30,26},{34,38... | collective-permute-start | bytes 565256 | tf_op jit(solution)/shard_map/ppermute | solution.py:684
  30.2 3.8 %collective-permute-start.5 = (f32[88,256]{1,0:T(8,128)S(1)}, f32[88,256]{1,0:T(8,128)S(1)}, u32[]{:S(2)}, u32[]{:S(2)}) collective-permute-start(f32[88,256]{1,0:T(8,128)S(1)} %get-tuple-element.34.own), channel_id=1, source_target_pairs={{0,4},{4,0},{8,12},{12,8},{16,20},{20,16},{24,28},{28,24},{32,36},... | collective-permute-start | bytes 270344 | tf_op jit(solution)/shard_map/ppermute | solution.py:707
  33.9 5.8 %collective-permute-start.6 = (f32[48,256]{1,0:T(8,128)S(1)}, f32[48,256]{1,0:T(8,128)S(1)}, u32[]{:S(2)}, u32[]{:S(2)}) collective-permute-start(f32[48,256]{1,0:T(8,128)S(1)} %pack_new_cross.1), channel_id=1, source_target_pairs={{0,8},{8,16},{12,4},{16,24},{20,12},{24,32},{28,20},{32,40},{36,28... | collective-permute-start | bytes 147464 | tf_op jit(solution)/shard_map/ppermute | solution.py:709
  39.7 6.8 %collective-permute-start.7 = (f32[48,256]{1,0:T(8,128)S(1)}, f32[48,256]{1,0:T(8,128)S(1)}, u32[]{:S(2)}, u32[]{:S(2)}) collective-permute-start(f32[48,256]{1,0:T(8,128)S(1)} %collective-permute-done.6.far), channel_id=1, source_target_pairs={{2,6},{6,2},{10,14},{14,10},{18,22},{22,18},{26,30},{30,26},{34,38... | collective-permute-start | bytes 147464 | tf_op jit(solution)/shard_map/ppermute | solution.py:719

commit v4 on v3

--- a/solution.py
+++ b/solution.py
@@ -14,11 +14,11 @@
 QUADS = ((0, 0), (0, 1), (1, 0), (1, 1))
 
 COL_HI, COL_LO, LISTS, PAD, EXPORT_ROWS = 0, 40, 64, 88, 136
-OWN_LISTS, MATE_LISTS, OWN_PAD, MATE_PAD, CROSS_ROWS = 40, 64, 88, 136, 184
+OWN_OPP2, MATE_FAR1, MATE_FAR2, OWN_PAD, MATE_PAD, CROSS_ROWS = 40, 44, 48, 56, 104, 152
 COL_LAB, COL_DT, COL_BEYOND, COLS_ROWS = 24, 32, 40, 64
 ZU_U, ZU_V, ZU_LAB, ZU_DT, ZU_CL, ZU_CH, ZU_CLAB, ZU_CDT, ZU_ROWS = 0, 96, 144, 176, 208, 214, 220, 222, 224
 ZD_U, ZD_V, ZD_LAB, ZD_DT, ZD_CL, ZD_CH, ZD_CLAB, ZD_CDT, ZD_ROWS = 0, 96, 144, 160, 176, 182, 188, 189, 192
-NEW_HI, NEW_LO, NEW_VALS, NEW_ROWS = 0, 32, 64, 88
+NEW_HI, NEW_LO, NEW_ROWS, VALUES_ROWS = 0, 32, 64, 24
 CROSS_OWN, CROSS_MATE, CROSS_ON, NEW_CROSS_ROWS = 32, 36, 40, 48
 NEAR, FAR1, OWN, FAR2, OPP2 = range(5)
 OFFSETS = (1, -1, 0, -2, 2)
@@ -100,19 +100,20 @@
 
 
 def pack_cross(own, mate, out):
+    even = on_even()
+
+    def bucket(ref, if_even, if_odd):
+        a, b = LISTS + 4 * if_even, LISTS + 4 * if_odd
+        return jnp.where(even, ref[a : a + 4, :], ref[b : b + 4, :])
+
     out[24:40, :] = mate[COL_HI + 24 : COL_HI + 40, :]
-    out[0:24, :] = jnp.where(on_even(), mate[COL_HI : COL_HI + 24, :], mate[COL_LO : COL_LO + 24, :])
-    out[OWN_LISTS : OWN_LISTS + 24, :] = own[LISTS : LISTS + 24, :]
-    out[MATE_LISTS : MATE_LISTS + 24, :] = mate[LISTS : LISTS + 24, :]
+    out[0:24, :] = jnp.where(even, mate[COL_HI : COL_HI + 24, :], mate[COL_LO : COL_LO + 24, :])
+    out[OWN_OPP2 : OWN_OPP2 + 4, :] = bucket(own, 4, 0)
+    out[MATE_FAR1 : MATE_FAR1 + 4, :] = bucket(mate, 3, 1)
+    out[MATE_FAR2 : MATE_FAR2 + 4, :] = bucket(mate, 4, 0)
+    out[MATE_FAR2 + 4 : OWN_PAD, :] = jnp.zeros((OWN_PAD - MATE_FAR2 - 4, 256), F32)
     out[OWN_PAD : OWN_PAD + 48, :] = own[PAD : PAD + 48, :]
     out[MATE_PAD : MATE_PAD + 48, :] = mate[PAD : PAD + 48, :]
-
-
-def pack_new_cross(own, mate, out):
-    out[0:32, :] = jnp.where(on_even(), mate[NEW_HI : NEW_HI + 32, :], mate[NEW_LO : NEW_LO + 32, :])
-    for row, src, role in ((CROSS_OWN, own, OPP2), (CROSS_MATE, mate, FAR1), (CROSS_ON, mate, FAR2)):
-        out[row : row + 4, :] = src[NEW_VALS + 4 * role : NEW_VALS + 4 * role + 4, :]
-    out[44:48, :] = jnp.zeros((4, 256), F32)
 
 
 def pack_layer(u, v, dt, lab, near, far, up, dn, cols):
@@ -243,12 +244,11 @@
     return (a - b) + pltpu.roll(a + b, 1, 1)
 
 
-def column_forces(layers, zbase, mats, inside, side, left, right, lab, dt, with_mass):
+def column_forces(layers, zg, valid, mats, inside, side, left, right, lab, dt, with_mass):
     rows = lab.shape[0]
     shape = (rows, 256)
-    zg = iota(shape, 0) + zbase
     ok = (zg >= 0) & (zg <= layers * 8 - 2) & (zg != layers // 2 * 8 + 3) & (iota(shape, 1) < 255)
-    mask = jnp.where(ok & inside, 1.0, 0.0)
+    mask = jnp.where(ok & valid & inside, 1.0, 0.0)
     l1, m1, k3, th, rho = cell_fields(mats, lab, dt, mask, with_mass)
     lower = [plane_modes(left[c], right[c]) for c in range(3)]
     upper = [[pltpu.roll(a, rows - 1, 0) for a in comp] for comp in lower]
@@ -313,6 +313,29 @@
         mass[cells] = saved_m[...]
 
 
+def two_layers(layers, z, mats, nodes, lab, dt):
+    shape = (16, 256)
+    in_plane = jnp.where((iota(shape, 1) < 255) & (iota(shape, 0) < 15), 1.0, 0.0)
+    modes = [[plane_modes(a, pltpu.roll(a, 15, 0)) for a in node] for node in nodes]
+    parts, masses = [], []
+    for i in (0, 1):
+        zg = z + i
+        ok = (zg >= 0) & (zg <= layers * 8 - 2) & (zg != layers // 2 * 8 + 3)
+        mask = in_plane * jnp.where(ok, 1.0, 0.0)
+        l1, m1, k3, th, rho = cell_fields(mats, lab[i], dt[i], mask, True)
+        parts.append(cell_forces(modes[i], modes[i + 1], l1, m1, k3, th))
+        rho = rho + pltpu.roll(rho, 1, 1)
+        masses.append(rho + pltpu.roll(rho, 1, 0))
+    (low0, high0), (low1, high1) = parts
+    middle = [[high0[c][q] + low1[c][q] for q in range(4)] for c in range(3)]
+    return (low0, middle, high1), (masses[0], masses[0] + masses[1], masses[1])
+
+
+def fold_node(node):
+    t0, t1 = fold_y(node[0], node[1]), fold_y(node[2], node[3])
+    return (t0 - t1) + pltpu.roll(t0 + t1, 1, 0)
+
+
 def with_columns(a, first, last):
     row = iota((8, 256), 0)
     top = a[0:8] + jnp.where(row == 0, jnp.broadcast_to(first, (8, 256)), 0.0)
@@ -357,22 +380,22 @@
 
 def fill_lists(own, near, far, opp, lists):
     sources = {
-        NEAR: (near, LISTS), FAR1: (far, MATE_LISTS), OWN: (own, LISTS), FAR2: (far, OWN_LISTS), OPP2: (opp, MATE_LISTS)
+        NEAR: (near, LISTS + 4 * (2 - role_offset(NEAR))),
+        FAR1: (far, MATE_FAR1),
+        OWN: (own, LISTS + 8),
+        FAR2: (far, OWN_OPP2),
+        OPP2: (opp, MATE_FAR2),
     }
     for role, (ref, base) in sources.items():
         cols = slice(128 * role, 128 * role + 128)
-        offset = role_offset(role)
-        row = LISTS + 4 * (2 + offset)
+        row = LISTS + 4 * (2 + role_offset(role))
         for i in range(3):
-            line = own[pl.ds(row + i, 1), :]
+            mine, other = own[pl.ds(row + i, 1), :], ref[pl.ds(base + i, 1), :]
             for half in (0, 1):
-                lists[2 * i + half : 2 * i + half + 1, cols] = line[:, 128 * half : 128 * half + 128]
-        row = base + 4 * (2 - offset)
-        for i in range(3):
-            line = ref[pl.ds(row + i, 1), :]
-            for half in (0, 1):
+                part = slice(128 * half, 128 * half + 128)
+                lists[2 * i + half : 2 * i + half + 1, cols] = mine[:, part]
                 if i + half:
-                    lists[5 + 2 * i + half : 6 + 2 * i + half, cols] = line[:, 128 * half : 128 * half + 128]
+                    lists[5 + 2 * i + half : 6 + 2 * i + half, cols] = other[:, part]
 
 
 def first_block(layers, u, dt, lab, par, force, mass, modes, saved, saved_m):
@@ -380,7 +403,38 @@
     block_forces(layers, 7, zbase, material_scalars(par), u, lab, dt, modes, saved, saved_m, force, mass)
 
 
-def first_contact(layers, own, near, far, opp, contact, lists):
+def first_inner(
+    blocks, layers, u, v, par, own, cols, force, mass, u1, v1, dtm, col_f, col_m
+):
+    here = lax.axis_index("plane")
+    mats = material_scalars(par)
+    row = iota((8, 256), 0)
+    for at, inside, side in ((0, here > 0, 1), (1, here < blocks - 1, -1)):
+        first = COL_LO if at == 0 else COL_HI
+        mine = [own[first + 8 * c : first + 8 * c + 8, :] for c in range(3)]
+        beyond = COL_BEYOND if at else 0
+        theirs = [cols[beyond + 8 * c : beyond + 8 * c + 8, :] for c in range(3)]
+        left, right = (mine, theirs) if at else (theirs, mine)
+        ref = own if at else cols
+        forces, rho = column_forces(
+            layers, row + lax.axis_index("layer") * 8, row < 7, mats, inside, side, left, right,
+            ref[COL_LAB : COL_LAB + 8, :], ref[COL_DT : COL_DT + 8, :], True,
+        )
+        for c in range(3):
+            col_f[at, c] = forces[c]
+        col_m[at] = rho
+    for i in range(6):
+        z = i + 1
+        rate = DT / (LUMPED + with_columns(mass[z], col_m[0, z : z + 1, :], col_m[1, z : z + 1, :]))
+        dtm[i] = rate
+        for c in range(3):
+            pull = with_columns(force[c, z], col_f[0, c, z : z + 1, :], col_f[1, c, z : z + 1, :])
+            speed = v[c, z] - rate * pull
+            v1[c, i] = speed
+            u1[c, i] = u[c, z] + DT * speed
+
+
+def first_contact(layers, own, near, far, opp, u1, v1, dtm, u_face, v_face, out, lists):
     @pl.when(lax.axis_index("layer") == layers // 2)
     def _():
         fill_lists(own, near, far, opp, lists)
@@ -401,119 +455,135 @@
             far_pad.append(gather(pads[role], far_y[:, part], far_x[:, part]))
         on_bump = lists[2:3, :] * (jnp.concatenate(far_pad, axis=1) - lists[3:6, :])
         on_pad = lists[7:8, :] * (lists[8:11, :] - gather(own_pad, land_y, land_x))
-        contact[0] = scatter(on_pad, land_y, land_x)
-        contact[1] = scatter(on_bump, sol_y, sol_x)
+        extra = (scatter(on_pad, land_y, land_x), scatter(on_bump, sol_y, sol_x))
+        faces = []
+        for face in (0, 1):
+            new = []
+            for c in range(3):
+                change = dtm[2 + face] * extra[face][c]
+                v_face[face, c] = v1[c, 2 + face] + change
+                new.append(u1[c, 2 + face] + DT * change)
+                u_face[face, c] = new[c]
+            faces.append(jnp.concatenate(new, axis=0))
+        lists[3:6, :] = gather(faces[1], sol_y, sol_x)
+        lists[8:11, :] = gather(faces[0], land_y, land_x)
+        for role in range(5):
+            part = slice(128 * role, 128 * role + 128)
+            for i, row in enumerate((3, 4, 5, 8, 9, 10)):
+                at, half = 4 * role + i // 2, i % 2
+                out[at : at + 1, 128 * half : 128 * half + 128] = lists[row : row + 1, part]
 
 
 def first_step(
     blocks, layers,
-    u, v, dt, lab, par, own, cols, zb, za, force, mass, contact, lists_in,
-    u1, v1, dtm, out, lists,
-    ul, uu, ll, dl, lu, du, fl, ml, fu, mu, col, col_lab, col_dt, col_f, col_m, modes, saved, saved_m,
+    u, v, dt, lab, par, own, cols, zb, za, force, mass, in_f, in_m, ui, vi, dtmi, u_face, v_face, values, mate,
+    u1, v1, dtm, ends, cross, swap,
+    col, col_lab, col_dt, col_f, col_m,
 ):
     layer, here = lax.axis_index("layer"), lax.axis_index("plane")
-    zeros = jnp.zeros((8, 256), F32)
+    even = on_even()
     mats = material_scalars(par)
     for c in range(3):
-        ul[c, 2], uu[c, 0] = u[c, 0], u[c, 7]
-        for zz in (0, 1):
-            row = 16 * (2 * c + zz)
-            ul[c, zz] = zb[ZU_U + row : ZU_U + row + 16, :]
-            uu[c, 1 + zz] = za[ZD_U + row : ZD_U + row + 16, :]
-        for at, src, first, zu, zd in ((0, cols, 0, ZU_CL, ZD_CL), (3, cols, COL_BEYOND, ZU_CH, ZD_CH)):
-            col[at, c, 8:16, :] = zeros
+        for at, first, zu, zd in ((0, 0, ZU_CL, ZD_CL), (3, COL_BEYOND, ZU_CH, ZD_CH)):
             col[at, c, 0:2, :] = zb[zu + 2 * c : zu + 2 * c + 2, :]
-            col[at, c, 2:10, :] = src[first + 8 * c : first + 8 * c + 8, :]
-            col[at, c, 10:12, :] = za[zd + 2 * c : zd + 2 * c + 2, :]
+            col[at, c, 2:3, :] = cols[first + 8 * c : first + 8 * c + 1, :]
+            col[at, c, 3:4, :] = cols[first + 8 * c + 7 : first + 8 * c + 8, :]
+            col[at, c, 4:6, :] = za[zd + 2 * c : zd + 2 * c + 2, :]
+            col[at, c, 6:8, :] = jnp.zeros((2, 256), F32)
         for at, first, x in ((1, COL_LO, 0), (2, COL_HI, 15)):
-            col[at, c, 8:16, :] = zeros
-            col[at, c, 2:10, :] = own[first + 8 * c : first + 8 * c + 8, :]
             for zz in (0, 1):
                 row = 16 * (2 * c + zz) + x
                 col[at, c, zz : zz + 1, :] = zb[ZU_U + row : ZU_U + row + 1, :]
-                col[at, c, 10 + zz : 11 + zz, :] = za[ZD_U + row : ZD_U + row + 1, :]
-    for zz in (0, 1):
-        ll[zz] = zb[ZU_LAB + 16 * zz : ZU_LAB + 16 * zz + 16, :]
-        dl[zz] = zb[ZU_DT + 16 * zz : ZU_DT + 16 * zz + 16, :]
-    lu[0], du[0] = lab[7].astype(F32), dt[7]
-    lu[1], du[1] = za[ZD_LAB : ZD_LAB + 16, :], za[ZD_DT : ZD_DT + 16, :]
+                col[at, c, 4 + zz : 5 + zz, :] = za[ZD_U + row : ZD_U + row + 1, :]
+            col[at, c, 2:3, :] = own[first + 8 * c : first + 8 * c + 1, :]
+            col[at, c, 3:4, :] = own[first + 8 * c + 7 : first + 8 * c + 8, :]
+            col[at, c, 6:8, :] = jnp.zeros((2, 256), F32)
     for ref, first, zu, zd, zuf, zdf in (
         (col_lab, COL_LAB, ZU_CLAB, ZD_CLAB, ZU_LAB, ZD_LAB),
         (col_dt, COL_DT, ZU_CDT, ZD_CDT, ZU_DT, ZD_DT),
     ):
         for at in (0, 1):
-            ref[at, 8:16, :] = zeros
+            ref[at] = jnp.zeros((8, 256), F32)
         ref[0, 0:2, :] = zb[zu : zu + 2, :]
-        ref[0, 2:10, :] = cols[first : first + 8, :]
-        ref[0, 10:11, :] = za[zd : zd + 1, :]
-        for zz in (0, 1):
-            ref[1, zz : zz + 1, :] = zb[zuf + 16 * zz + 15 : zuf + 16 * zz + 16, :]
-        ref[1, 2:10, :] = own[COL_HI + first : COL_HI + first + 8, :]
-        ref[1, 10:11, :] = za[zdf + 15 : zdf + 16, :]
-
-    zbase = layer * 8 - 2
-    block_forces(layers, 2, zbase, mats, ul, ll, dl, modes, saved, saved_m, fl, ml)
-    block_forces(layers, 2, zbase + 9, mats, uu, lu, du, modes, saved, saved_m, fu, mu)
+        ref[0, 3:4, :] = cols[first + 7 : first + 8, :]
+        ref[0, 4:5, :] = za[zd : zd + 1, :]
+        ref[1, 0:1, :] = zb[zuf + 15 : zuf + 16, :]
+        ref[1, 1:2, :] = zb[zuf + 31 : zuf + 32, :]
+        ref[1, 3:4, :] = own[COL_HI + first + 7 : COL_HI + first + 8, :]
+        ref[1, 4:5, :] = za[zdf + 15 : zdf + 16, :]
+    row = iota((8, 256), 0)
+    zg = layer * 8 + jnp.where(row < 3, row - 2, row + 4)
+    valid = (row < 5) & (row != 2)
     for at, inside, side in ((0, here > 0, 1), (1, here < blocks - 1, -1)):
         left = [col[2 * at, c] for c in range(3)]
         right = [col[2 * at + 1, c] for c in range(3)]
         forces, rho = column_forces(
-            layers, zbase, mats, inside, side, left, right, col_lab[at], col_dt[at], True
+            layers, zg, valid, mats, inside, side, left, right, col_lab[at], col_dt[at], True
         )
         for c in range(3):
             col_f[at, c] = forces[c]
         col_m[at] = rho
 
-    for i in range(10):
-        z, e = i - 1, i + 1
-        total = mass[z] if 0 <= z < 8 else 0.0
-        if z < 1:
-            total = total + ml[e]
-        if z > 6:
-            total = total + mu[z - 7]
-        total = LUMPED + with_columns(total, col_m[0, e : e + 1, :], col_m[1, e : e + 1, :])
-        rate = DT / total
+    def face(ref, row):
+        return ref[row : row + 16, :]
+
+    below = [[face(zb, ZU_U + 16 * (2 * c + zz)) for c in range(3)] for zz in (0, 1)]
+    above = [[face(za, ZD_U + 16 * (2 * c + zz)) for c in range(3)] for zz in (0, 1)]
+    first, last = [u[c, 0] for c in range(3)], [u[c, 7] for c in range(3)]
+    low_f, low_m = two_layers(
+        layers, layer * 8 - 2, mats, below + [first],
+        (face(zb, ZU_LAB), face(zb, ZU_LAB + 16)), (face(zb, ZU_DT), face(zb, ZU_DT + 16)),
+    )
+    high_f, high_m = two_layers(
+        layers, layer * 8 + 7, mats, [last] + above,
+        (lab[7].astype(F32), face(za, ZD_LAB)), (dt[7], face(za, ZD_DT)),
+    )
+    v_below = [face(zb, ZU_V + 16 * c) for c in range(3)]
+    v_above = [face(za, ZD_V + 16 * c) for c in range(3)]
+    for i, z, at, pulls, weight, place, speeds in (
+        (0, -1, 1, low_f[1], low_m[1], below[1], v_below),
+        (1, 0, 2, low_f[2], low_m[2], first, [v[c, 0] for c in range(3)]),
+        (8, 7, 3, high_f[0], high_m[0], last, [v[c, 7] for c in range(3)]),
+        (9, 8, 4, high_f[1], high_m[1], above[0], v_above),
+    ):
+        inner = 0 <= z < 8
+        edges = [col_m[side, at : at + 1, :] for side in (0, 1)]
+        if inner:
+            weight = weight + mass[z]
+            edges = [edges[side] + in_m[side, z : z + 1, :] for side in (0, 1)]
+        rate = DT / (LUMPED + with_columns(weight, *edges))
         dtm[i] = rate
         for c in range(3):
-            pull = force[c, z] if 0 <= z < 8 else 0.0
-            if z < 1:
-                pull = pull + fl[c, e]
-            if z > 6:
-                pull = pull + fu[c, z - 7]
-            pull = with_columns(pull, col_f[0, c, e : e + 1, :], col_f[1, c, e : e + 1, :])
-            if z < 0:
-                speed, place = zb[ZU_V + 16 * c : ZU_V + 16 * c + 16, :], ul[c, 1]
-            elif z > 7:
-                speed, place = za[ZD_V + 16 * c : ZD_V + 16 * c + 16, :], uu[c, 1]
-            else:
-                speed, place = v[c, z], u[c, z]
-            speed = speed - rate * pull
+            pull = fold_node(pulls[c])
+            edges = [col_f[side, c, at : at + 1, :] for side in (0, 1)]
+            if inner:
+                pull = pull + force[c, z]
+                edges = [edges[side] + in_f[side, c, z : z + 1, :] for side in (0, 1)]
+            speed = speeds[c] - rate * with_columns(pull, *edges)
             v1[c, i] = speed
-            u1[c, i] = place + DT * speed
+            u1[c, i] = place[c] + DT * speed
+    dtm[2:8] = dtmi[...]
+    for c in range(3):
+        u1[c, 2:8] = ui[c]
+        v1[c, 2:8] = vi[c]
 
     @pl.when(layer == layers // 2)
     def _():
         for c in range(3):
-            for face in (0, 1):
-                at = 4 + face
-                change = dtm[at] * contact[face, c]
-                v1[c, at] = v1[c, at] + change
-                u1[c, at] = u1[c, at] + DT * change
-        lists[...] = lists_in[...]
-        new_pad = jnp.concatenate([u1[c, 4] for c in range(3)], axis=0)
-        new_bump = jnp.concatenate([u1[c, 5] for c in range(3)], axis=0)
-        lists[3:6, :] = gather(new_bump, *one_hots(lists[0:1, :]))
-        lists[8:11, :] = gather(new_pad, *one_hots(lists[6:7, :]))
-        for role in range(5):
-            part = slice(128 * role, 128 * role + 128)
-            for i, row in enumerate((3, 4, 5, 8, 9, 10)):
-                at, half = NEW_VALS + 4 * role + i // 2, i % 2
-                out[at : at + 1, 128 * half : 128 * half + 128] = lists[row : row + 1, part]
+            for i in (0, 1):
+                u1[c, 4 + i] = u_face[i, c]
+                v1[c, 4 + i] = v_face[i, c]
+        for row, src, role in ((CROSS_OWN, mate, OPP2), (CROSS_MATE, values, FAR1), (CROSS_ON, values, FAR2)):
+            cross[row : row + 4, :] = src[4 * role : 4 * role + 4, :]
 
     for x, row in ((15, NEW_HI), (0, NEW_LO)):
         for c in range(3):
-            out[row + 10 * c : row + 10 * c + 8, :] = u1[c, 0:8, x, :]
-            out[row + 10 * c + 8 : row + 10 * c + 10, :] = u1[c, 8:10, x, :]
+            ends[row + 10 * c : row + 10 * c + 8, :] = u1[c, 0:8, x, :]
+            ends[row + 10 * c + 8 : row + 10 * c + 10, :] = u1[c, 8:10, x, :]
+        ends[row + 30 : row + 32, :] = jnp.zeros((2, 256), F32)
+    upper, lower = ends[NEW_HI : NEW_HI + 32, :], ends[NEW_LO : NEW_LO + 32, :]
+    cross[0:32, :] = jnp.where(even, lower, upper)
+    swap[...] = jnp.where(even, upper, lower)
 
 
 def second_block(layers, u, dt, lab, par, zb, force, le, de, modes, saved):
@@ -539,10 +609,10 @@
         at, hi, lo = 10 * c, NEW_HI + 10 * c, NEW_LO + 10 * c
         for i in range(4):
             col[i, c, 8:16, :] = zeros
-        col[0, c, 0:10, :] = jnp.where(even, far[at : at + 10, :], near[hi : hi + 10, :])
+        col[0, c, 0:10, :] = jnp.where(even, far[at : at + 10, :], near[at : at + 10, :])
         col[1, c, 0:10, :] = own[lo : lo + 10, :]
         col[2, c, 0:10, :] = own[hi : hi + 10, :]
-        col[3, c, 0:10, :] = jnp.where(even, near[lo : lo + 10, :], far[at : at + 10, :])
+        col[3, c, 0:10, :] = jnp.where(even, near[at : at + 10, :], far[at : at + 10, :])
     for ref, src, first, zu, zuf in (
         (col_lab, lab, COL_LAB, ZU_CLAB, ZU_LAB),
         (col_dt, dt, COL_DT, ZU_CDT, ZU_DT),
@@ -553,11 +623,12 @@
         ref[0, 1:9, :] = cols[first : first + 8, :]
         ref[1, 0:1, :] = zb[zuf + 31 : zuf + 32, :]
         ref[1, 1:9, :] = src[:, 15, :].astype(F32)
+    zg = iota((16, 256), 0) + (layer * 8 - 1)
     for at, inside, side in ((0, here > 0, 1), (1, here < blocks - 1, -1)):
         left = [col[2 * at, c] for c in range(3)]
         right = [col[2 * at + 1, c] for c in range(3)]
         forces, _ = column_forces(
-            layers, layer * 8 - 1, mats, inside, side, left, right, col_lab[at], col_dt[at], False
+            layers, zg, zg < layer * 8 + 8, mats, inside, side, left, right, col_lab[at], col_dt[at], False
         )
         for c in range(3):
             col_f[at, c] = forces[c]
@@ -571,7 +642,7 @@
             u2[c, z] = u[c, e] + DT * speed
 
 
-def second_contact(layers, u, v, dtm, lists, near, far, opp, u2, v2, faces, sems):
+def second_contact(layers, u, v, dtm, lists, mate, far, opp, u2, v2, faces, sems):
     copies = []
     for i, (src, dst) in enumerate(((u, u2), (v, v2))):
         for first, last in ((0, 3), (5, 8)):
@@ -594,7 +665,7 @@
             half = slice(128 * (i % 2), 128 * (i % 2) + 128)
             own_row = (3, 4, 5, 8, 9, 10)[i]
             places = (
-                (near, NEW_VALS + 4 * NEAR), (far, CROSS_MATE), None, (far, CROSS_OWN), (opp, CROSS_ON)
+                (mate, 4 * NEAR), (far, CROSS_MATE), None, (far, CROSS_OWN), (opp, CROSS_ON)
             )
             parts = [
                 lists[own_row : own_row + 1, 256:384] if place is None
@@ -682,31 +753,37 @@
     )(u, v, dt, lab, near, far)
     zb, za = along_layer(up, 1), along_layer(dn, -1)
     opp = lax.ppermute(far, ("plane", "layer"), face_swaps)
-    contact, lists = call(
+    u1, v1, dtm, in_f, in_m = call(
+        functools.partial(first_inner, blocks, layers),
+        [VM] * 2 + [SM] + [VM] * 4,
+        [(3, 6, 16, 256), (3, 6, 16, 256), (6, 16, 256), (2, 3, 8, 256), (2, 8, 256)],
+        [],
+        "first_inner",
+        10_000_000,
+    )(u, v, par, own, cols, force, mass)
+    opp, u1, v1 = lax.optimization_barrier((opp, u1, v1))
+    u_face, v_face, values, lists = call(
         functools.partial(first_contact, layers),
-        [VM] * 4,
-        [(2, 3, 16, 256), (16, 640)],
+        [VM] * 7,
+        [(2, 3, 16, 256), (2, 3, 16, 256), (VALUES_ROWS, 256), (16, 640)],
         [],
         "first_contact",
         10_000_000,
-    )(own, near, far, opp)
-
-    three, two = [(3, 3, 16, 256)] * 2 + [(2, 16, 256)] * 4, (2, 16, 256)
-    u1, v1, dtm, own, lists = call(
+    )(own, near, far, opp, u1, v1, dtm)
+    mate = lax.ppermute(values, ("plane", "layer"), face_swaps)
+
+    two = (2, 8, 256)
+    u1, v1, dtm, ends, cross, swap = call(
         functools.partial(first_step, blocks, layers),
-        [VM] * 4 + [SM] + [VM] * 8,
-        [(3, 10, 16, 256), (3, 10, 16, 256), (10, 16, 256), (NEW_ROWS, 256), (16, 640)],
-        three
-        + [(3, 3, 16, 256), (3, 16, 256)] * 2
-        + [(4, 3, 16, 256), two, two, (2, 3, 16, 256), two]
-        + modes
-        + [plane],
+        [VM] * 4 + [SM] + [VM] * 15,
+        [(3, 10, 16, 256), (3, 10, 16, 256), (10, 16, 256), (NEW_ROWS, 256), (NEW_CROSS_ROWS, 256), (32, 256)],
+        [(4, 3, 8, 256), two, two, (2, 3, 8, 256), two],
         "first_step",
         20_000_000,
-    )(u, v, dt, lab, par, own, cols, zb, za, force, mass, contact, lists)
-    near = lax.ppermute(own, "plane", swaps)
-    cross = call(pack_new_cross, [VM] * 2, [(NEW_CROSS_ROWS, 256)], [], "pack_new_cross", 100_000)(own, near)[0]
-    far = lax.ppermute(cross, "plane", crossings)
+    )(u, v, dt, lab, par, own, cols, zb, za, force, mass, in_f, in_m, u1, v1, dtm, u_face, v_face, values, mate)
+    across = [(s, s + 1) for s in range(1, blocks - 1, 2)] + [(s, s - 1) for s in range(2, blocks, 2)]
+    far = lax.ppermute(cross, "plane", across)
+    near = lax.ppermute(swap, "plane", swaps)
     force = call(
         functools.partial(second_block, layers),
         [VM] * 3 + [SM, VM],
@@ -715,8 +792,9 @@
         "second_block",
         50_000_000,
     )(u1, dt, lab, par, zb)[0]
-    far, force = lax.optimization_barrier((far, force))
+    far, near, force = lax.optimization_barrier((far, near, force))
     opp = lax.ppermute(far, ("plane", "layer"), face_swaps)
+    two = (2, 16, 256)
     u2, v2 = call(
         functools.partial(second_step, blocks, layers),
         [VM] * 5 + [SM] + [VM] * 6,
@@ -724,7 +802,7 @@
         [(4, 3, 16, 256), two, two, (2, 3, 16, 256)],
         "second_step",
         20_000_000,
-    )(u1, v1, dtm, dt, lab, par, force, cols, zb, own, near, far)
+    )(u1, v1, dtm, dt, lab, par, force, cols, zb, ends, near, far)
     return tuple(
         call(
             functools.partial(second_contact, layers),
@@ -734,7 +812,7 @@
             "second_contact",
             10_000_000,
             out_spec=HBM,
-        )(u2, v2, dtm, lists, near, far, opp)
+        )(u2, v2, dtm, lists, mate, far, opp)
     )
 
 

time: 48 us -> 46.3 us (0.965)
  the two profiles are of different devices: /device:TPU:261 before, /device:TPU:253 now
where the time goes in v4:
time: 46.3 us; the launch traced here: 45.9 us
  starting transfers between devices  25.8 us (56%)
  Pallas kernels  12.8 us (28%)
  waiting for transfers between devices  5.46 us (12%)
  local copies, waits for them, and re-layouts  0.93 us (2%)
  between operations  0.87 us (2%)
    ppermute x1, starting transfers between devices, local(): far = lax.ppermute(cross, 'plane', across)  6.37 us
    ppermute x2, starting transfers between devices, along_layer(): return lax.ppermute(value, 'layer', pairs)  5.28 us
    ppermute x2, starting transfers between devices, local(): opp = lax.ppermute(far, ('plane', 'layer'), face_swaps)  4.33 us
    ppermute x1, waiting for transfers between devices, local(): far = lax.ppermute(cross, 'plane', crossings)  3.89 us
    ppermute x1, starting transfers between devices, local(): far = lax.ppermute(cross, 'plane', crossings)  3.11 us
    pallas_call x1, Pallas kernels, local(): call(functools.partial(second_block, layers), [VM] * 3 + [SM, VM], [(3, 1...  2.79 us
    ppermute x1, starting transfers between devices, local(): near = lax.ppermute(own, 'plane', swaps)  2.72 us
    pallas_call x1, Pallas kernels, local(): call(functools.partial(first_block, layers), [VM] * 3 + [SM], [(3, 8, 16,...  2.38 us
  transfers between devices with their start and end apart: 9, of which 4 were waited for; matrix products, arithmetic and copies ran while one was open for 0% of the time, Pallas kernels for 18%

profile of v4, /device:TPU:253, one launch (start us, length us, event | category | flops | bytes accessed | tf_op | source)
XLA Modules:
  0.0 45.9 jit_solution(9138047393093462454)
XLA Ops:
  0.6 2.1 %pack_export.1.src = f32[136,256]{1,0:T(8,128)} custom-call(f32[3,8,16,256]{3,2,1,0:T(8,128)} %u.7, f32[8,16,256]{2,1,0:T(8,128)} %dt.9, s32[8,16,256]{2,1,0:T(8,128)} %lab.9, s32[5,1,128]{2,1,0:T(1,128)} %bitcast.3, s32[5,1,128]{2,1,0:T(1,128)} %bitcast.4, f32[5,1,128]{2,1,0:T(1,128)} %bitcast.5, s32[1,5]{1,0:T(1,128)} %tally_hbm.1), custom_call_target="tpu_custom_call" | custom-call | flops 100000 | bytes 2000000 | tf_op jit(solution)/shard_map/pack_export/pallas_call | solution.py:724
  2.7 0.0 copy-start
  2.7 2.7 %collective-permute-start = (f32[136,256]{1,0:T(8,128)}, f32[136,256]{1,0:T(8,128)S(1)}, u32[]{:S(2)}, u32[]{:S(2)}) collective-permute-start(f32[136,256]{1,0:T(8,128)} %pack_export.1.src), channel_id=1, source_target_pairs={{0,4},{4,0},{8,12},{12,8},{16,20},{20,16},{24,28},{28,24},{32,36},... | collective-permute-start | bytes 417800 | tf_op jit(solution)/shard_map/ppermute | solution.py:736
  5.5 0.9 %copy-done.4 = f32[136,256]{1,0:T(8,128)S(1)} copy-done((f32[136,256]{1,0:T(8,128)S(1)}, f32[136,256]{1,0:T(8,128)}, u32[]{:S(2)}) %copy-start.4) | copy-done | bytes 139288
  6.4 0.2 stage.1.own
  6.6 0.1 collective-permute-done.mate.near
  6.7 3.1 %collective-permute-start.1 = (f32[152,256]{1,0:T(8,128)S(1)}, f32[152,256]{1,0:T(8,128)S(1)}, u32[]{:S(2)}, u32[]{:S(2)}) collective-permute-start(f32[152,256]{1,0:T(8,128)S(1)} %pack_cross.1), channel_id=1, source_target_pairs={{0,8},{8,16},{12,4},{16,24},{20,12},{24,32},{28,20},{32,40},{36,28... | collective-permute-start | bytes 466952 | tf_op jit(solution)/shard_map/ppermute | solution.py:739
  9.8 2.4 %first_block.1 = (f32[3,8,16,256]{3,2,1,0:T(8,128)S(1)}, f32[8,16,256]{2,1,0:T(8,128)S(1)}) custom-call(f32[3,8,16,256]{3,2,1,0:T(8,128)S(1)} %copy-done, f32[8,16,256]{2,1,0:T(8,128)S(1)} %copy-done.1, s32[8,16,256]{2,1,0:T(8,128)S(1)} %copy-done.2, f32[4,4]{1,0:T(4,128)S(1)} %copy-done.5), custom_call_target="tpu_custom_call" | custom-call | flops 50000000 | bytes 2000000 | tf_op jit(solution)/shard_map/first_block/pallas_call | solution.py:742
  12.2 3.9 %collective-permute-done.1.far = f32[152,256]{1,0:T(8,128)S(1)} collective-permute-done((f32[152,256]{1,0:T(8,128)S(1)}, f32[152,256]{1,0:T(8,128)S(1)}, u32[]{:S(2)}, u32[]{:S(2)}) %collective-permute-start.1) | collective-permute-done | bytes 155680 | tf_op jit(solution)/shard_map/ppermute | solution.py:739
  16.2 2.6 %collective-permute-start.2 = (f32[224,256]{1,0:T(8,128)S(1)}, f32[224,256]{1,0:T(8,128)S(1)}, u32[]{:S(2)}, u32[]{:S(2)}) collective-permute-start(f32[224,256]{1,0:T(8,128)S(1)} %get-tuple-element.37), channel_id=1, source_target_pairs={{0,1},{1,2},{2,3},{4,5},{5,6},{6,7},{8,9},{9,10},{10,11},{12,13},{... | collective-permute-start | bytes 688136 | tf_op jit(solution)/shard_map/ppermute | solution.py:722
  18.7 2.7 %collective-permute-start.3 = (f32[192,256]{1,0:T(8,128)S(1)}, f32[192,256]{1,0:T(8,128)S(1)}, u32[]{:S(2)}, u32[]{:S(2)}) collective-permute-start(f32[192,256]{1,0:T(8,128)S(1)} %get-tuple-element.38), channel_id=1, source_target_pairs={{1,0},{2,1},{3,2},{5,4},{6,5},{7,6},{9,8},{10,9},{11,10},{13,12},{... | collective-permute-start | bytes 589832 | tf_op jit(solution)/shard_map/ppermute | solution.py:722
  21.5 1.9 %collective-permute-start.4 = (f32[152,256]{1,0:T(8,128)S(1)}, f32[152,256]{1,0:T(8,128)S(1)}, u32[]{:S(2)}, u32[]{:S(2)}) collective-permute-start(f32[152,256]{1,0:T(8,128)S(1)} %collective-permute-done.1.far), channel_id=1, source_target_pairs={{2,6},{6,2},{10,14},{14,10},{18,22},{22,18},{26,30},{30,26},{34,38... | collective-permute-start | bytes 466952 | tf_op jit(solution)/shard_map/ppermute | solution.py:755
  23.4 0.9 %first_inner.1 = (f32[3,6,16,256]{3,2,1,0:T(8,128)S(1)}, f32[3,6,16,256]{3,2,1,0:T(8,128)S(1)}, f32[6,16,256]{2,1,0:T(8,128)S(1)}, f32[2,3,8,256]{3,2,1,0:T(8,128)S(1)}, f32[2,8,256]{2,1,0:T(8,128)S(1)}) custom-call(f32[3,8,16,256]{3,2,1,0:T(8,128)S(1)} %copy-done, f32[3,8,16,256]{3,2,1,0:T(8,128)S(1)} %copy-done.3, f32[4,4]{1,0:T(4,128)S(1)} %copy-done.5, ...), custom_call_target="tpu_custom_call" | custom-call | flops 10000000 | bytes 2000000 | tf_op jit(solution)/shard_map/first_inner/pallas_call | solution.py:756
  24.3 0.5 %collective-permute-done.4.opp = f32[152,256]{1,0:T(8,128)S(1)} collective-permute-done((f32[152,256]{1,0:T(8,128)S(1)}, f32[152,256]{1,0:T(8,128)S(1)}, u32[]{:S(2)}, u32[]{:S(2)}) %collective-permute-start.4) | collective-permute-done | bytes 155680 | tf_op jit(solution)/shard_map/ppermute | solution.py:755
  24.7 0.9 %first_contact.1 = (f32[2,3,16,256]{3,2,1,0:T(8,128)S(1)}, f32[2,3,16,256]{3,2,1,0:T(8,128)S(1)}, f32[24,256]{1,0:T(8,128)S(1)}, f32[16,640]{1,0:T(8,128)S(1)}) custom-call(f32[136,256]{1,0:T(8,128)S(1)} %stage.1.own, f32[136,256]{1,0:T(8,128)S(1)} %collective-permute-done.mate.near, f32[152,256]{1,0:T(8,128)S(1)} %collective-permute-done.1.far, ...), custom_call_target="tpu_custom_call" | custom-call | flops 10000000 | bytes 2000000 | tf_op jit(solution)/shard_map/first_contact/pallas_call | solution.py:765
  25.6 2.1 %collective-permute-start.5 = (f32[24,256]{1,0:T(8,128)S(1)}, f32[24,256]{1,0:T(8,128)S(1)}, u32[]{:S(2)}, u32[]{:S(2)}) collective-permute-start(f32[24,256]{1,0:T(8,128)S(1)} %get-tuple-element.51.values), channel_id=1, source_target_pairs={{2,6},{6,2},{10,14},{14,10},{18,22},{22,18},{26,30},{30,26},{34,38... | collective-permute-start | bytes 73736 | tf_op jit(solution)/shard_map/ppermute | solution.py:773
  27.7 1.0 %collective-permute-done.5.mate = f32[24,256]{1,0:T(8,128)S(1)} collective-permute-done((f32[24,256]{1,0:T(8,128)S(1)}, f32[24,256]{1,0:T(8,128)S(1)}, u32[]{:S(2)}, u32[]{:S(2)}) %collective-permute-start.5) | collective-permute-done | bytes 24608 | tf_op jit(solution)/shard_map/ppermute | solution.py:773
  28.7 1.5 %first_step.1 = (f32[3,10,16,256]{3,2,1,0:T(8,128)S(1)}, f32[3,10,16,256]{3,2,1,0:T(8,128)S(1)}, f32[10,16,256]{2,1,0:T(8,128)S(1)}, f32[64,256]{1,0:T(8,128)S(1...) custom-call(f32[3,8,16,256]{3,2,1,0:T(8,128)S(1)} %copy-done, f32[3,8,16,256]{3,2,1,0:T(8,128)S(1)} %copy-done.3, ...), custom_call_target="tpu_custom_call" | custom-call | flops 20000000 | bytes 2000000 | tf_op jit(solution)/shard_map/first_step/pallas_call | solution.py:776
  30.2 6.4 %collective-permute-start.6 = (f32[48,256]{1,0:T(8,128)S(1)}, f32[48,256]{1,0:T(8,128)S(1)}, u32[]{:S(2)}, u32[]{:S(2)}) collective-permute-start(f32[48,256]{1,0:T(8,128)S(1)} %get-tuple-element.55), channel_id=1, source_target_pairs={{4,8},{12,16},{20,24},{28,32},{36,40},{44,48},{52,56},{60,64},{68,... | collective-permute-start | bytes 147464 | tf_op jit(solution)/shard_map/ppermute | solution.py:785
  36.6 1.9 %collective-permute-start.7 = (f32[32,256]{1,0:T(8,128)S(1)}, f32[32,256]{1,0:T(8,128)S(1)}, u32[]{:S(2)}, u32[]{:S(2)}) collective-permute-start(f32[32,256]{1,0:T(8,128)S(1)} %get-tuple-element.56), channel_id=1, source_target_pairs={{0,4},{4,0},{8,12},{12,8},{16,20},{20,16},{24,28},{28,24},{32,36},... | collective-permute-start | bytes 98312 | tf_op jit(solution)/shard_map/ppermute | solution.py:786
  38.5 2.8 %second_block.1.force = f32[3,10,16,256]{3,2,1,0:T(8,128)S(1)} custom-call(f32[3,10,16,256]{3,2,1,0:T(8,128)S(1)} %get-tuple-element.52.u, f32[8,16,256]{2,1,0:T(8,128)S(1)} %copy-done.1, s32[8,16,256]{2,1,0:T(8,128)S(1)} %copy-done.2, f32[4,4]{1,0:T(4,128)S(1)} %copy-done.5, f32[224,256]{1,0:T(8,128)S(1)} %collective-permute-done.2.zb), custom_call_target="tpu_custom_call" | custom-call | flops 50000000 | bytes 2000000 | tf_op jit(solution)/shard_map/second_block/pallas_call | solution.py:787
  41.3 2.4 %collective-permute-start.8 = (f32[48,256]{1,0:T(8,128)S(1)}, f32[48,256]{1,0:T(8,128)S(1)}, u32[]{:S(2)}, u32[]{:S(2)}) collective-permute-start(f32[48,256]{1,0:T(8,128)S(1)} %collective-permute-done.6.far), channel_id=1, source_target_pairs={{2,6},{6,2},{10,14},{14,10},{18,22},{22,18},{26,30},{30,26},{34,38... | collective-permute-start | bytes 147464 | tf_op jit(solution)/shard_map/ppermute | solution.py:796
  43.7 1.0 %second_step.1 = (f32[3,8,16,256]{3,2,1,0:T(8,128)S(1)}, f32[3,8,16,256]{3,2,1,0:T(8,128)S(1)}) custom-call(f32[3,10,16,256]{3,2,1,0:T(8,128)S(1)} %get-tuple-element.52.u, f32[3,10,16,256]{3,2,1,0:T(8,128)S(1)} %get-tuple-element.53.v, f32[10,16,256]{2,1,0:T(8,128)S(1)} %get-tuple-element.54.dtm, f32[8,16,256]{2,1,0:T(8,128)S(1)} %copy-done.1, ...), custom_call_target="tpu_custom_call" | custom-call | flops 20000000 | bytes 2000000 | tf_op jit(solution)/shard_map/second_step/pallas_call | solution.py:798
  44.8 1.1 %second_contact.1 = (f32[3,8,16,256]{3,2,1,0:T(8,128)}, f32[3,8,16,256]{3,2,1,0:T(8,128)}) custom-call(f32[3,8,16,256]{3,2,1,0:T(8,128)S(1)} %get-tuple-element.61.u, f32[3,8,16,256]{3,2,1,0:T(8,128)S(1)} %get-tuple-element.62.v, f32[10,16,256]{2,1,0:T(8,128)S(1)} %get-tuple-element.54.dtm, f32[16,640]{1,0:T(8,128)S(1)} %get-tuple-element.63.lists, ...), custom_call_target="tpu_custom_call" | custom-call | flops 10000000 | bytes 2000000 | tf_op jit(solution)/shard_map/second_contact/pallas_call | solution.py:807
  (17 shorter events, 0.1 us)
Async XLA Ops:
  2.7 7.1 %copy-start = (f32[3,8,16,256]{3,2,1,0:T(8,128)S(1)}, f32[3,8,16,256]{3,2,1,0:T(8,128)}, u32[]{:S(2)}) copy-start(f32[3,8,16,256]{3,2,1,0:T(8,128)} %u.7) | copy-start | bytes 1179652
  2.7 3.9 %collective-permute-start = (f32[136,256]{1,0:T(8,128)}, f32[136,256]{1,0:T(8,128)S(1)}, u32[]{:S(2)}, u32[]{:S(2)}) collective-permute-start(f32[136,256]{1,0:T(8,128)} %pack_export.1.src), channel_id=1, source_target_pairs={{0,4},{4,0},{8,12},{12,8},{16,20},{20,16},{24,28},{28,24},{32,36},... | collective-permute-start | bytes 417800 | tf_op jit(solution)/shard_map/ppermute | solution.py:736
  5.5 0.9 %copy-start.4 = (f32[136,256]{1,0:T(8,128)S(1)}, f32[136,256]{1,0:T(8,128)}, u32[]{:S(2)}) copy-start(f32[136,256]{1,0:T(8,128)} %pack_export.1.src) | copy-start | bytes 417796
  6.5 3.3 %copy-start.1 = (f32[8,16,256]{2,1,0:T(8,128)S(1)}, f32[8,16,256]{2,1,0:T(8,128)}, u32[]{:S(2)}) copy-start(f32[8,16,256]{2,1,0:T(8,128)} %dt.9) | copy-start | bytes 393220
  6.5 3.3 %copy-start.2 = (s32[8,16,256]{2,1,0:T(8,128)S(1)}, s32[8,16,256]{2,1,0:T(8,128)}, u32[]{:S(2)}) copy-start(s32[8,16,256]{2,1,0:T(8,128)} %lab.9) | copy-start | bytes 393220
  6.6 3.3 %copy-start.5 = (f32[4,4]{1,0:T(4,128)S(1)}, f32[4,4]{1,0:T(4,128)}, u32[]{:S(2)}) copy-start(f32[4,4]{1,0:T(4,128)} %par.9) | copy-start | bytes 196
  6.7 9.4 %copy-start.3 = (f32[3,8,16,256]{3,2,1,0:T(8,128)S(1)}, f32[3,8,16,256]{3,2,1,0:T(8,128)}, u32[]{:S(2)}) copy-start(f32[3,8,16,256]{3,2,1,0:T(8,128)} %v.5) | copy-start | bytes 1179652
  6.7 9.4 %collective-permute-start.1 = (f32[152,256]{1,0:T(8,128)S(1)}, f32[152,256]{1,0:T(8,128)S(1)}, u32[]{:S(2)}, u32[]{:S(2)}) collective-permute-start(f32[152,256]{1,0:T(8,128)S(1)} %pack_cross.1), channel_id=1, source_target_pairs={{0,8},{8,16},{12,4},{16,24},{20,12},{24,32},{28,20},{32,40},{36,28... | collective-permute-start | bytes 466952 | tf_op jit(solution)/shard_map/ppermute | solution.py:739
  16.2 12.6 %collective-permute-start.2 = (f32[224,256]{1,0:T(8,128)S(1)}, f32[224,256]{1,0:T(8,128)S(1)}, u32[]{:S(2)}, u32[]{:S(2)}) collective-permute-start(f32[224,256]{1,0:T(8,128)S(1)} %get-tuple-element.37), channel_id=1, source_target_pairs={{0,1},{1,2},{2,3},{4,5},{5,6},{6,7},{8,9},{9,10},{10,11},{12,13},{... | collective-permute-start | bytes 688136 | tf_op jit(solution)/shard_map/ppermute | solution.py:722
  18.7 10.0 %collective-permute-start.3 = (f32[192,256]{1,0:T(8,128)S(1)}, f32[192,256]{1,0:T(8,128)S(1)}, u32[]{:S(2)}, u32[]{:S(2)}) collective-permute-start(f32[192,256]{1,0:T(8,128)S(1)} %get-tuple-element.38), channel_id=1, source_target_pairs={{1,0},{2,1},{3,2},{5,4},{6,5},{7,6},{9,8},{10,9},{11,10},{13,12},{... | collective-permute-start | bytes 589832 | tf_op jit(solution)/shard_map/ppermute | solution.py:722
  21.5 3.3 %collective-permute-start.4 = (f32[152,256]{1,0:T(8,128)S(1)}, f32[152,256]{1,0:T(8,128)S(1)}, u32[]{:S(2)}, u32[]{:S(2)}) collective-permute-start(f32[152,256]{1,0:T(8,128)S(1)} %collective-permute-done.1.far), channel_id=1, source_target_pairs={{2,6},{6,2},{10,14},{14,10},{18,22},{22,18},{26,30},{30,26},{34,38... | collective-permute-start | bytes 466952 | tf_op jit(solution)/shard_map/ppermute | solution.py:755
  25.6 3.1 %collective-permute-start.5 = (f32[24,256]{1,0:T(8,128)S(1)}, f32[24,256]{1,0:T(8,128)S(1)}, u32[]{:S(2)}, u32[]{:S(2)}) collective-permute-start(f32[24,256]{1,0:T(8,128)S(1)} %get-tuple-element.51.values), channel_id=1, source_target_pairs={{2,6},{6,2},{10,14},{14,10},{18,22},{22,18},{26,30},{30,26},{34,38... | collective-permute-start | bytes 73736 | tf_op jit(solution)/shard_map/ppermute | solution.py:773
  30.2 11.1 %collective-permute-start.6 = (f32[48,256]{1,0:T(8,128)S(1)}, f32[48,256]{1,0:T(8,128)S(1)}, u32[]{:S(2)}, u32[]{:S(2)}) collective-permute-start(f32[48,256]{1,0:T(8,128)S(1)} %get-tuple-element.55), channel_id=1, source_target_pairs={{4,8},{12,16},{20,24},{28,32},{36,40},{44,48},{52,56},{60,64},{68,... | collective-permute-start | bytes 147464 | tf_op jit(solution)/shard_map/ppermute | solution.py:785
  36.6 4.7 %collective-permute-start.7 = (f32[32,256]{1,0:T(8,128)S(1)}, f32[32,256]{1,0:T(8,128)S(1)}, u32[]{:S(2)}, u32[]{:S(2)}) collective-permute-start(f32[32,256]{1,0:T(8,128)S(1)} %get-tuple-element.56), channel_id=1, source_target_pairs={{0,4},{4,0},{8,12},{12,8},{16,20},{20,16},{24,28},{28,24},{32,36},... | collective-permute-start | bytes 98312 | tf_op jit(solution)/shard_map/ppermute | solution.py:786
  41.3 3.5 %collective-permute-start.8 = (f32[48,256]{1,0:T(8,128)S(1)}, f32[48,256]{1,0:T(8,128)S(1)}, u32[]{:S(2)}, u32[]{:S(2)}) collective-permute-start(f32[48,256]{1,0:T(8,128)S(1)} %collective-permute-done.6.far), channel_id=1, source_target_pairs={{2,6},{6,2},{10,14},{14,10},{18,22},{22,18},{26,30},{30,26},{34,38... | collective-permute-start | bytes 147464 | tf_op jit(solution)/shard_map/ppermute | solution.py:796

commit v5 on v4

--- a/solution.py
+++ b/solution.py
@@ -264,7 +264,7 @@
     return forces, rho
 
 
-def block_forces(layers, cells, zbase, mats, u, lab, dt, modes, saved, saved_m, force, mass):
+def block_forces(layers, cells, group, zbase, mats, u, lab, dt, modes, saved, saved_m, force, mass):
     shape = (16, 256)
     row, lane = iota(shape, 0), iota(shape, 1)
     in_plane = jnp.where((lane < 255) & (row < 15), 1.0, 0.0)
@@ -285,29 +285,34 @@
             t0, t1 = fold_y(node[c][0], node[c][1]), fold_y(node[c][2], node[c][3])
             force[c, e] = (t0 - t1) + pltpu.roll(t0 + t1, 1, 0)
 
-    def body(e, carry):
-        zg = zbase + e
-        ok = (zg >= 0) & (zg <= layers * 8 - 2) & (zg != layers // 2 * 8 + 3)
-        mask = in_plane * jnp.where(ok, 1.0, 0.0)
-        l1, m1, k3, th, rho = cell_fields(mats, lab[e].astype(F32), dt[e], mask, mass is not None)
+    def body(i, carry):
         lower = [[modes[4 * c + q] for q in range(4)] for c in range(3)]
-        upper = [forward(e + 1, c) for c in range(3)]
+        held = [[saved[4 * c + q] for q in range(4)] for c in range(3)]
+        held_m = None if mass is None else saved_m[...]
+        for g in range(group):
+            e = i * group + g
+            zg = zbase + e
+            ok = (zg >= 0) & (zg <= layers * 8 - 2) & (zg != layers // 2 * 8 + 3)
+            mask = in_plane * jnp.where(ok, 1.0, 0.0)
+            l1, m1, k3, th, rho = cell_fields(mats, lab[e].astype(F32), dt[e], mask, mass is not None)
+            upper = [forward(e + 1, c) for c in range(3)]
+            low, high = cell_forces(lower, upper, l1, m1, k3, th)
+            fold(e, [[low[c][q] + held[c][q] for q in range(4)] for c in range(3)])
+            lower, held = upper, high
+            if mass is not None:
+                rho = rho + pltpu.roll(rho, 1, 1)
+                rho = rho + pltpu.roll(rho, 1, 0)
+                mass[e] = rho + held_m
+                held_m = rho
         for c in range(3):
             for q in range(4):
-                modes[4 * c + q] = upper[c][q]
-        low, high = cell_forces(lower, upper, l1, m1, k3, th)
-        fold(e, [[low[c][q] + saved[4 * c + q] for q in range(4)] for c in range(3)])
-        for c in range(3):
-            for q in range(4):
-                saved[4 * c + q] = high[c][q]
+                modes[4 * c + q] = lower[c][q]
+                saved[4 * c + q] = held[c][q]
         if mass is not None:
-            rho = rho + pltpu.roll(rho, 1, 1)
-            rho = rho + pltpu.roll(rho, 1, 0)
-            mass[e] = rho + saved_m[...]
-            saved_m[...] = rho
+            saved_m[...] = held_m
         return carry
 
-    lax.fori_loop(0, cells, body, 0)
+    lax.fori_loop(0, cells // group, body, 0)
     fold(cells, [[saved[4 * c + q] for q in range(4)] for c in range(3)])
     if mass is not None:
         mass[cells] = saved_m[...]
@@ -400,7 +405,7 @@
 
 def first_block(layers, u, dt, lab, par, force, mass, modes, saved, saved_m):
     zbase = lax.axis_index("layer") * 8
-    block_forces(layers, 7, zbase, material_scalars(par), u, lab, dt, modes, saved, saved_m, force, mass)
+    block_forces(layers, 7, 1, zbase, material_scalars(par), u, lab, dt, modes, saved, saved_m, force, mass)
 
 
 def first_inner(
@@ -476,12 +481,11 @@
 
 def first_step(
     blocks, layers,
-    u, v, dt, lab, par, own, cols, zb, za, force, mass, in_f, in_m, ui, vi, dtmi, u_face, v_face, values, mate,
-    u1, v1, dtm, ends, cross, swap,
+    u, v, dt, lab, par, own, cols, zb, za, force, mass, in_f, in_m, ui, vi, dtmi, u_face, v_face,
+    u1, v1, dtm, ends,
     col, col_lab, col_dt, col_f, col_m,
 ):
     layer, here = lax.axis_index("layer"), lax.axis_index("plane")
-    even = on_even()
     mats = material_scalars(par)
     for c in range(3):
         for at, first, zu, zd in ((0, 0, ZU_CL, ZD_CL), (3, COL_BEYOND, ZU_CH, ZD_CH)):
@@ -573,17 +577,24 @@
             for i in (0, 1):
                 u1[c, 4 + i] = u_face[i, c]
                 v1[c, 4 + i] = v_face[i, c]
-        for row, src, role in ((CROSS_OWN, mate, OPP2), (CROSS_MATE, values, FAR1), (CROSS_ON, values, FAR2)):
-            cross[row : row + 4, :] = src[4 * role : 4 * role + 4, :]
 
     for x, row in ((15, NEW_HI), (0, NEW_LO)):
         for c in range(3):
             ends[row + 10 * c : row + 10 * c + 8, :] = u1[c, 0:8, x, :]
             ends[row + 10 * c + 8 : row + 10 * c + 10, :] = u1[c, 8:10, x, :]
         ends[row + 30 : row + 32, :] = jnp.zeros((2, 256), F32)
-    upper, lower = ends[NEW_HI : NEW_HI + 32, :], ends[NEW_LO : NEW_LO + 32, :]
-    cross[0:32, :] = jnp.where(even, lower, upper)
-    swap[...] = jnp.where(even, upper, lower)
+
+
+def pack_new_cross(ends, values, mate, out):
+    out[0:32, :] = jnp.where(on_even(), ends[NEW_LO : NEW_LO + 32, :], ends[NEW_HI : NEW_HI + 32, :])
+    for row, src, role in ((CROSS_OWN, mate, OPP2), (CROSS_MATE, values, FAR1), (CROSS_ON, values, FAR2)):
+        out[row : row + 4, :] = src[4 * role : 4 * role + 4, :]
+    out[44:48, :] = jnp.zeros((4, 256), F32)
+
+
+def pack_last(ends, far, out):
+    out[0:32, :] = jnp.where(on_even(), ends[NEW_HI : NEW_HI + 32, :], ends[NEW_LO : NEW_LO + 32, :])
+    out[32:48, :] = far[32:48, :]
 
 
 def second_block(layers, u, dt, lab, par, zb, force, le, de, modes, saved):
@@ -592,46 +603,54 @@
     le[1:9] = lab[...].astype(F32)
     de[1:9] = dt[...]
     zbase = lax.axis_index("layer") * 8 - 1
-    block_forces(layers, 9, zbase, material_scalars(par), u, le, de, modes, saved, None, force, None)
+    block_forces(layers, 9, 3, zbase, material_scalars(par), u, le, de, modes, saved, None, force, None)
+
+
+def second_column(blocks, layers, at, src, own_row, dt, lab, par, cols, zb, ends, col, col_lab, col_dt):
+    layer, here = lax.axis_index("layer"), lax.axis_index("plane")
+    zeros = jnp.zeros((8, 256), F32)
+    for c in range(3):
+        col[0, c, 8:16, :] = zeros
+        col[1, c, 8:16, :] = zeros
+        col[0, c, 0:10, :] = src[10 * c : 10 * c + 10, :]
+        col[1, c, 0:10, :] = ends[own_row + 10 * c : own_row + 10 * c + 10, :]
+    for ref, field, first, zu, zuf in (
+        (col_lab, lab, COL_LAB, ZU_CLAB, ZU_LAB),
+        (col_dt, dt, COL_DT, ZU_CDT, ZU_DT),
+    ):
+        ref[8:16, :] = zeros
+        if at:
+            ref[0:1, :] = zb[zuf + 31 : zuf + 32, :]
+            ref[1:9, :] = field[:, 15, :].astype(F32)
+        else:
+            ref[0:1, :] = zb[zu + 1 : zu + 2, :]
+            ref[1:9, :] = cols[first : first + 8, :]
+    zg = iota((16, 256), 0) + (layer * 8 - 1)
+    inside = here < blocks - 1 if at else here > 0
+    theirs, mine = [col[0, c] for c in range(3)], [col[1, c] for c in range(3)]
+    left, right = (mine, theirs) if at else (theirs, mine)
+    return column_forces(
+        layers, zg, zg < layer * 8 + 8, material_scalars(par), inside, -1 if at else 1, left, right,
+        col_lab[...], col_dt[...], False,
+    )[0]
 
 
 def second_step(
     blocks, layers,
-    u, v, dtm, dt, lab, par, force, cols, zb, own, near, far,
+    u, v, dtm, dt, lab, par, force, cols, zb, ends, far,
     u2, v2,
     col, col_lab, col_dt, col_f,
 ):
-    layer, here = lax.axis_index("layer"), lax.axis_index("plane")
-    zeros = jnp.zeros((8, 256), F32)
-    mats = material_scalars(par)
-    even = on_even()
-    for c in range(3):
-        at, hi, lo = 10 * c, NEW_HI + 10 * c, NEW_LO + 10 * c
-        for i in range(4):
-            col[i, c, 8:16, :] = zeros
-        col[0, c, 0:10, :] = jnp.where(even, far[at : at + 10, :], near[at : at + 10, :])
-        col[1, c, 0:10, :] = own[lo : lo + 10, :]
-        col[2, c, 0:10, :] = own[hi : hi + 10, :]
-        col[3, c, 0:10, :] = jnp.where(even, near[at : at + 10, :], far[at : at + 10, :])
-    for ref, src, first, zu, zuf in (
-        (col_lab, lab, COL_LAB, ZU_CLAB, ZU_LAB),
-        (col_dt, dt, COL_DT, ZU_CDT, ZU_DT),
-    ):
-        for at in (0, 1):
-            ref[at, 8:16, :] = zeros
-        ref[0, 0:1, :] = zb[zu + 1 : zu + 2, :]
-        ref[0, 1:9, :] = cols[first : first + 8, :]
-        ref[1, 0:1, :] = zb[zuf + 31 : zuf + 32, :]
-        ref[1, 1:9, :] = src[:, 15, :].astype(F32)
-    zg = iota((16, 256), 0) + (layer * 8 - 1)
-    for at, inside, side in ((0, here > 0, 1), (1, here < blocks - 1, -1)):
-        left = [col[2 * at, c] for c in range(3)]
-        right = [col[2 * at + 1, c] for c in range(3)]
-        forces, _ = column_forces(
-            layers, zg, zg < layer * 8 + 8, mats, inside, side, left, right, col_lab[at], col_dt[at], False
-        )
-        for c in range(3):
-            col_f[at, c] = forces[c]
+    for at in (0, 1):
+        @pl.when(on_even() == (at == 0))
+        def _():
+            forces = second_column(
+                blocks, layers, at, far, NEW_HI if at else NEW_LO, dt, lab, par, cols, zb, ends, col, col_lab, col_dt
+            )
+            for c in range(3):
+                col_f[at, c] = forces[c]
+                col_f[1 - at, c] = jnp.zeros((16, 256), F32)
+
     for z in range(8):
         e = z + 1
         rate = dtm[e]
@@ -642,19 +661,35 @@
             u2[c, z] = u[c, e] + DT * speed
 
 
-def second_contact(layers, u, v, dtm, lists, mate, far, opp, u2, v2, faces, sems):
+def second_contact(
+    blocks, layers,
+    u_in, v_in, dtm, lists, mate, far, opp, dt, lab, par, cols, zb, ends,
+    u2, v2,
+    u, v, col, col_lab, col_dt, sems,
+):
+    u[...] = u_in[...]
+    v[...] = v_in[...]
+    for at in (0, 1):
+        @pl.when(on_even() == (at == 1))
+        def _():
+            forces = second_column(
+                blocks, layers, at, opp, NEW_HI if at else NEW_LO, dt, lab, par, cols, zb, ends, col, col_lab, col_dt
+            )
+            x = 15 if at else 0
+            rate = dtm[1:9, x, :]
+            for c in range(3):
+                change = rate * forces[c][1:9]
+                v[c, :, x, :] = v[c, :, x, :] - change
+                u[c, :, x, :] = u[c, :, x, :] - DT * change
+
     copies = []
-    for i, (src, dst) in enumerate(((u, u2), (v, v2))):
+    for src, dst in ((u, u2), (v, v2)):
         for first, last in ((0, 3), (5, 8)):
             copies.append(
                 pltpu.make_async_copy(src.at[:, first:last], dst.at[:, first:last], sems.at[len(copies)])
             )
     for copy in copies:
         copy.start()
-    for c in range(3):
-        for face in (0, 1):
-            faces[0, c, face] = u[c, 3 + face]
-            faces[1, c, face] = v[c, 3 + face]
 
     @pl.when(lax.axis_index("layer") == layers // 2)
     def _():
@@ -682,11 +717,11 @@
         for c in range(3):
             for face in (0, 1):
                 change = dtm[4 + face] * extra[face][c]
-                faces[0, c, face] = faces[0, c, face] + DT * change
-                faces[1, c, face] = faces[1, c, face] + change
-
-    for i, dst in enumerate((u2, v2)):
-        copy = pltpu.make_async_copy(faces.at[i], dst.at[:, 3:5], sems.at[4 + i])
+                u[c, 3 + face] = u[c, 3 + face] + DT * change
+                v[c, 3 + face] = v[c, 3 + face] + change
+
+    for i, (src, dst) in enumerate(((u, u2), (v, v2))):
+        copy = pltpu.make_async_copy(src.at[:, 3:5], dst.at[:, 3:5], sems.at[4 + i])
         copy.start()
         copies.append(copy)
     for copy in copies:
@@ -773,17 +808,17 @@
     mate = lax.ppermute(values, ("plane", "layer"), face_swaps)
 
     two = (2, 8, 256)
-    u1, v1, dtm, ends, cross, swap = call(
+    u1, v1, dtm, ends = call(
         functools.partial(first_step, blocks, layers),
-        [VM] * 4 + [SM] + [VM] * 15,
-        [(3, 10, 16, 256), (3, 10, 16, 256), (10, 16, 256), (NEW_ROWS, 256), (NEW_CROSS_ROWS, 256), (32, 256)],
+        [VM] * 4 + [SM] + [VM] * 13,
+        [(3, 10, 16, 256), (3, 10, 16, 256), (10, 16, 256), (NEW_ROWS, 256)],
         [(4, 3, 8, 256), two, two, (2, 3, 8, 256), two],
         "first_step",
         20_000_000,
-    )(u, v, dt, lab, par, own, cols, zb, za, force, mass, in_f, in_m, u1, v1, dtm, u_face, v_face, values, mate)
+    )(u, v, dt, lab, par, own, cols, zb, za, force, mass, in_f, in_m, u1, v1, dtm, u_face, v_face)
     across = [(s, s + 1) for s in range(1, blocks - 1, 2)] + [(s, s - 1) for s in range(2, blocks, 2)]
+    cross = call(pack_new_cross, [VM] * 3, [(NEW_CROSS_ROWS, 256)], [], "pack_new_cross", 100_000)(ends, values, mate)[0]
     far = lax.ppermute(cross, "plane", across)
-    near = lax.ppermute(swap, "plane", swaps)
     force = call(
         functools.partial(second_block, layers),
         [VM] * 3 + [SM, VM],
@@ -792,27 +827,28 @@
         "second_block",
         50_000_000,
     )(u1, dt, lab, par, zb)[0]
-    far, near, force = lax.optimization_barrier((far, near, force))
-    opp = lax.ppermute(far, ("plane", "layer"), face_swaps)
-    two = (2, 16, 256)
+    far, force = lax.optimization_barrier((far, force))
+    last = call(pack_last, [VM] * 2, [(NEW_CROSS_ROWS, 256)], [], "pack_last", 100_000)(ends, far)[0]
+    opp = lax.ppermute(last, "plane", swaps)
+    column = [(2, 3, 16, 256), (16, 256), (16, 256)]
     u2, v2 = call(
         functools.partial(second_step, blocks, layers),
-        [VM] * 5 + [SM] + [VM] * 6,
+        [VM] * 5 + [SM] + [VM] * 5,
         [(3, 8, 16, 256)] * 2,
-        [(4, 3, 16, 256), two, two, (2, 3, 16, 256)],
+        column + [(2, 3, 16, 256)],
         "second_step",
         20_000_000,
-    )(u1, v1, dtm, dt, lab, par, force, cols, zb, ends, near, far)
+    )(u1, v1, dtm, dt, lab, par, force, cols, zb, ends, far)
     return tuple(
         call(
-            functools.partial(second_contact, layers),
-            [VM] * 7,
+            functools.partial(second_contact, blocks, layers),
+            [VM] * 9 + [SM] + [VM] * 3,
             [(3, 8, 16, 256)] * 2,
-            [(2, 3, 2, 16, 256), pltpu.SemaphoreType.DMA((6,))],
+            [(3, 8, 16, 256)] * 2 + column + [pltpu.SemaphoreType.DMA((6,))],
             "second_contact",
             10_000_000,
             out_spec=HBM,
-        )(u2, v2, dtm, lists, mate, far, opp)
+        )(u2, v2, dtm, lists, mate, far, opp, dt, lab, par, cols, zb, ends)
     )
 
 

time: 46.3 us -> 45.3 us (0.978)
  the two profiles are of different devices: /device:TPU:253 before, /device:TPU:261 now
where the time goes in v5:
time: 45.3 us; the launch traced here: 44.9 us
  starting transfers between devices  28.5 us (63%)
  Pallas kernels  13 us (29%)
  waiting for transfers between devices  1.54 us (3%)
  local copies, waits for them, and re-layouts  0.93 us (2%)
  between operations  0.9 us (2%)
    ppermute x1, starting transfers between devices, local(): opp = lax.ppermute(far, ('plane', 'layer'), face_swaps)  6.65 us
    ppermute x1, starting transfers between devices, local(): opp = lax.ppermute(last, 'plane', swaps)  5.37 us
    ppermute x2, starting transfers between devices, along_layer(): return lax.ppermute(value, 'layer', pairs)  5.28 us
    ppermute x1, starting transfers between devices, local(): far = lax.ppermute(cross, 'plane', crossings)  4.32 us
    ppermute x1, starting transfers between devices, local(): near = lax.ppermute(own, 'plane', swaps)  2.71 us
    pallas_call x1, Pallas kernels, local(): call(functools.partial(first_block, layers), [VM] * 3 + [SM], [(3, 8, 16,...  2.37 us
    ppermute x1, starting transfers between devices, local(): mate = lax.ppermute(values, ('plane', 'layer'), face_swaps)  2.27 us
    pallas_call x1, Pallas kernels, local(): call(functools.partial(second_block, layers), [VM] * 3 + [SM, VM], [(3, 1...  2.13 us
  transfers between devices with their start and end apart: 8, of which 3 were waited for; matrix products, arithmetic and copies ran while one was open for 0% of the time, Pallas kernels for 20%

profile of v5, /device:TPU:261, one launch (start us, length us, event | category | flops | bytes accessed | tf_op | source)
XLA Modules:
  0.0 44.9 jit_solution(13489906998010183159)
XLA Ops:
  0.6 2.1 %pack_export.1.src = f32[136,256]{1,0:T(8,128)} custom-call(f32[3,8,16,256]{3,2,1,0:T(8,128)} %u.7, f32[8,16,256]{2,1,0:T(8,128)} %dt.11, s32[8,16,256]{2,1,0:T(8,128)} %lab.11, s32[5,1,128]{2,1,0:T(1,128)} %bitcast.3, s32[5,1,128]{2,1,0:T(1,128)} %bitcast.4, f32[5,1,128]{2,1,0:T(1,128)} %bitcast.5, s32[1,5]{1,0:T(1,128)} %tally_hbm.1), custom_call_target="tpu_custom_call" | custom-call | flops 100000 | bytes 2000000 | tf_op jit(solution)/shard_map/pack_export/pallas_call | solution.py:759
  2.7 0.0 copy-start
  2.7 2.7 %collective-permute-start = (f32[136,256]{1,0:T(8,128)}, f32[136,256]{1,0:T(8,128)S(1)}, u32[]{:S(2)}, u32[]{:S(2)}) collective-permute-start(f32[136,256]{1,0:T(8,128)} %pack_export.1.src), channel_id=1, source_target_pairs={{0,4},{4,0},{8,12},{12,8},{16,20},{20,16},{24,28},{28,24},{32,36},... | collective-permute-start | bytes 417800 | tf_op jit(solution)/shard_map/ppermute | solution.py:771
  5.5 0.9 %copy-done.4 = f32[136,256]{1,0:T(8,128)S(1)} copy-done((f32[136,256]{1,0:T(8,128)S(1)}, f32[136,256]{1,0:T(8,128)}, u32[]{:S(2)}) %copy-start.4) | copy-done | bytes 139288
  6.4 0.2 stage.1.own
  6.6 0.0 copy-start.5
  6.6 0.1 collective-permute-done.mate.near
  6.7 4.3 %collective-permute-start.1 = (f32[152,256]{1,0:T(8,128)S(1)}, f32[152,256]{1,0:T(8,128)S(1)}, u32[]{:S(2)}, u32[]{:S(2)}) collective-permute-start(f32[152,256]{1,0:T(8,128)S(1)} %pack_cross.1), channel_id=1, source_target_pairs={{0,8},{8,16},{12,4},{16,24},{20,12},{24,32},{28,20},{32,40},{36,28... | collective-permute-start | bytes 466952 | tf_op jit(solution)/shard_map/ppermute | solution.py:774
  11.0 2.4 %first_block.1 = (f32[3,8,16,256]{3,2,1,0:T(8,128)S(1)}, f32[8,16,256]{2,1,0:T(8,128)S(1)}) custom-call(f32[3,8,16,256]{3,2,1,0:T(8,128)S(1)} %copy-done, f32[8,16,256]{2,1,0:T(8,128)S(1)} %copy-done.1, s32[8,16,256]{2,1,0:T(8,128)S(1)} %copy-done.2, f32[4,4]{1,0:T(4,128)S(1)} %copy-done.5), custom_call_target="tpu_custom_call" | custom-call | flops 50000000 | bytes 2000000 | tf_op jit(solution)/shard_map/first_block/pallas_call | solution.py:777
  13.4 0.1 pack_layer.1
  13.5 2.6 %collective-permute-start.2 = (f32[224,256]{1,0:T(8,128)S(1)}, f32[224,256]{1,0:T(8,128)S(1)}, u32[]{:S(2)}, u32[]{:S(2)}) collective-permute-start(f32[224,256]{1,0:T(8,128)S(1)} %get-tuple-element.34), channel_id=1, source_target_pairs={{0,1},{1,2},{2,3},{4,5},{5,6},{6,7},{8,9},{9,10},{10,11},{12,13},{... | collective-permute-start | bytes 688136 | tf_op jit(solution)/shard_map/ppermute | solution.py:757
  16.1 2.7 %collective-permute-start.3 = (f32[192,256]{1,0:T(8,128)S(1)}, f32[192,256]{1,0:T(8,128)S(1)}, u32[]{:S(2)}, u32[]{:S(2)}) collective-permute-start(f32[192,256]{1,0:T(8,128)S(1)} %get-tuple-element.35), channel_id=1, source_target_pairs={{1,0},{2,1},{3,2},{5,4},{6,5},{7,6},{9,8},{10,9},{11,10},{13,12},{... | collective-permute-start | bytes 589832 | tf_op jit(solution)/shard_map/ppermute | solution.py:757
  18.8 6.6 %collective-permute-start.4 = (f32[152,256]{1,0:T(8,128)S(1)}, f32[152,256]{1,0:T(8,128)S(1)}, u32[]{:S(2)}, u32[]{:S(2)}) collective-permute-start(f32[152,256]{1,0:T(8,128)S(1)} %collective-permute-done.1.far), channel_id=1, source_target_pairs={{2,6},{6,2},{10,14},{14,10},{18,22},{22,18},{26,30},{30,26},{34,38... | collective-permute-start | bytes 466952 | tf_op jit(solution)/shard_map/ppermute | solution.py:790
  25.4 0.9 %first_inner.1 = (f32[3,6,16,256]{3,2,1,0:T(8,128)S(1)}, f32[3,6,16,256]{3,2,1,0:T(8,128)S(1)}, f32[6,16,256]{2,1,0:T(8,128)S(1)}, f32[2,3,8,256]{3,2,1,0:T(8,128)S(1)}, f32[2,8,256]{2,1,0:T(8,128)S(1)}) custom-call(f32[3,8,16,256]{3,2,1,0:T(8,128)S(1)} %copy-done, f32[3,8,16,256]{3,2,1,0:T(8,128)S(1)} %copy-done.3, f32[4,4]{1,0:T(4,128)S(1)} %copy-done.5, ...), custom_call_target="tpu_custom_call" | custom-call | flops 10000000 | bytes 2000000 | tf_op jit(solution)/shard_map/first_inner/pallas_call | solution.py:791
  26.3 0.1 collective-permute-done.4.opp
  26.4 0.9 %first_contact.1 = (f32[2,3,16,256]{3,2,1,0:T(8,128)S(1)}, f32[2,3,16,256]{3,2,1,0:T(8,128)S(1)}, f32[24,256]{1,0:T(8,128)S(1)}, f32[16,640]{1,0:T(8,128)S(1)}) custom-call(f32[136,256]{1,0:T(8,128)S(1)} %stage.1.own, f32[136,256]{1,0:T(8,128)S(1)} %collective-permute-done.mate.near, f32[152,256]{1,0:T(8,128)S(1)} %collective-permute-done.1.far, ...), custom_call_target="tpu_custom_call" | custom-call | flops 10000000 | bytes 2000000 | tf_op jit(solution)/shard_map/first_contact/pallas_call | solution.py:800
  27.3 2.3 %collective-permute-start.5 = (f32[24,256]{1,0:T(8,128)S(1)}, f32[24,256]{1,0:T(8,128)S(1)}, u32[]{:S(2)}, u32[]{:S(2)}) collective-permute-start(f32[24,256]{1,0:T(8,128)S(1)} %get-tuple-element.52.values), channel_id=1, source_target_pairs={{2,6},{6,2},{10,14},{14,10},{18,22},{22,18},{26,30},{30,26},{34,38... | collective-permute-start | bytes 73736 | tf_op jit(solution)/shard_map/ppermute | solution.py:808
  29.6 1.5 %first_step.1 = (f32[3,10,16,256]{3,2,1,0:T(8,128)S(1)}, f32[3,10,16,256]{3,2,1,0:T(8,128)S(1)}, f32[10,16,256]{2,1,0:T(8,128)S(1)}, f32[64,256]{1,0:T(8,128)S(1)}) custom-call(f32[3,8,16,256]{3,2,1,0:T(8,128)S(1)} %copy-done, f32[3,8,16,256]{3,2,1,0:T(8,128)S(1)} %copy-done.3, f32[8,16,256]{2,1,0:T(8,128)S(1)} %copy-done.1, s32[8,16,256]{2,1,0:T(8,128)S(1)} %copy-done.2, ...), custom_call_target="tpu_custom_call" | custom-call | flops 20000000 | bytes 2000000 | tf_op jit(solution)/shard_map/first_step/pallas_call | solution.py:811
  31.1 1.9 %collective-permute-start.6 = (f32[48,256]{1,0:T(8,128)S(1)}, f32[48,256]{1,0:T(8,128)S(1)}, u32[]{:S(2)}, u32[]{:S(2)}) collective-permute-start(f32[48,256]{1,0:T(8,128)S(1)} %pack_new_cross.1), channel_id=1, source_target_pairs={{4,8},{12,16},{20,24},{28,32},{36,40},{44,48},{52,56},{60,64},{68,... | collective-permute-start | bytes 147464 | tf_op jit(solution)/shard_map/ppermute | solution.py:821
  33.1 2.1 %second_block.1.force = f32[3,10,16,256]{3,2,1,0:T(8,128)S(1)} custom-call(f32[3,10,16,256]{3,2,1,0:T(8,128)S(1)} %get-tuple-element.48.u, f32[8,16,256]{2,1,0:T(8,128)S(1)} %copy-done.1, s32[8,16,256]{2,1,0:T(8,128)S(1)} %copy-done.2, f32[4,4]{1,0:T(4,128)S(1)} %copy-done.5, f32[224,256]{1,0:T(8,128)S(1)} %collective-permute-done.2.zb), custom_call_target="tpu_custom_call" | custom-call | flops 50000000 | bytes 2000000 | tf_op jit(solution)/shard_map/second_block/pallas_call | solution.py:822
  35.2 1.3 %collective-permute-done.6.far = f32[48,256]{1,0:T(8,128)S(1)} collective-permute-done((f32[48,256]{1,0:T(8,128)S(1)}, f32[48,256]{1,0:T(8,128)S(1)}, u32[]{:S(2)}, u32[]{:S(2)}) %collective-permute-start.6) | collective-permute-done | bytes 49184 | tf_op jit(solution)/shard_map/ppermute | solution.py:821
  36.5 5.4 %collective-permute-start.7 = (f32[48,256]{1,0:T(8,128)S(1)}, f32[48,256]{1,0:T(8,128)S(1)}, u32[]{:S(2)}, u32[]{:S(2)}) collective-permute-start(f32[48,256]{1,0:T(8,128)S(1)} %pack_last.1), channel_id=1, source_target_pairs={{0,4},{4,0},{8,12},{12,8},{16,20},{20,16},{24,28},{28,24},{32,36},... | collective-permute-start | bytes 147464 | tf_op jit(solution)/shard_map/ppermute | solution.py:832
  41.9 1.0 %second_step.1 = (f32[3,8,16,256]{3,2,1,0:T(8,128)S(1)}, f32[3,8,16,256]{3,2,1,0:T(8,128)S(1)}) custom-call(f32[3,10,16,256]{3,2,1,0:T(8,128)S(1)} %get-tuple-element.48.u, f32[3,10,16,256]{3,2,1,0:T(8,128)S(1)} %get-tuple-element.49.v, f32[10,16,256]{2,1,0:T(8,128)S(1)} %get-tuple-element.50.dtm, f32[8,16,256]{2,1,0:T(8,128)S(1)} %copy-done.1, ...), custom_call_target="tpu_custom_call" | custom-call | flops 20000000 | bytes 2000000 | tf_op jit(solution)/shard_map/second_step/pallas_call | solution.py:834
  42.9 2.0 %second_contact.1 = (f32[3,8,16,256]{3,2,1,0:T(8,128)}, f32[3,8,16,256]{3,2,1,0:T(8,128)}) custom-call(f32[3,8,16,256]{3,2,1,0:T(8,128)S(1)} %get-tuple-element.55.u_in, f32[3,8,16,256]{3,2,1,0:T(8,128)S(1)} %get-tuple-element.56.v_in, f32[10,16,256]{2,1,0:T(8,128)S(1)} %get-tuple-element.50.dtm, f32[16,640]{1,0:T(8,128)S(1)} %get-tuple-element.57.lists, ...), custom_call_target="tpu_custom_call" | custom-call | flops 10000000 | bytes 2000000 | tf_op jit(solution)/shard_map/second_contact/pallas_call | solution.py:843
  (17 shorter events, 0.1 us)
Async XLA Ops:
  2.7 8.3 %copy-start = (f32[3,8,16,256]{3,2,1,0:T(8,128)S(1)}, f32[3,8,16,256]{3,2,1,0:T(8,128)}, u32[]{:S(2)}) copy-start(f32[3,8,16,256]{3,2,1,0:T(8,128)} %u.7) | copy-start | bytes 1179652
  2.7 3.9 %collective-permute-start = (f32[136,256]{1,0:T(8,128)}, f32[136,256]{1,0:T(8,128)S(1)}, u32[]{:S(2)}, u32[]{:S(2)}) collective-permute-start(f32[136,256]{1,0:T(8,128)} %pack_export.1.src), channel_id=1, source_target_pairs={{0,4},{4,0},{8,12},{12,8},{16,20},{20,16},{24,28},{28,24},{32,36},... | collective-permute-start | bytes 417800 | tf_op jit(solution)/shard_map/ppermute | solution.py:771
  5.5 0.9 %copy-start.4 = (f32[136,256]{1,0:T(8,128)S(1)}, f32[136,256]{1,0:T(8,128)}, u32[]{:S(2)}) copy-start(f32[136,256]{1,0:T(8,128)} %pack_export.1.src) | copy-start | bytes 417796
  6.5 4.5 %copy-start.1 = (f32[8,16,256]{2,1,0:T(8,128)S(1)}, f32[8,16,256]{2,1,0:T(8,128)}, u32[]{:S(2)}) copy-start(f32[8,16,256]{2,1,0:T(8,128)} %dt.11) | copy-start | bytes 393220
  6.5 4.5 %copy-start.2 = (s32[8,16,256]{2,1,0:T(8,128)S(1)}, s32[8,16,256]{2,1,0:T(8,128)}, u32[]{:S(2)}) copy-start(s32[8,16,256]{2,1,0:T(8,128)} %lab.11) | copy-start | bytes 393220
  6.6 4.5 %copy-start.5 = (f32[4,4]{1,0:T(4,128)S(1)}, f32[4,4]{1,0:T(4,128)}, u32[]{:S(2)}) copy-start(f32[4,4]{1,0:T(4,128)} %par.11) | copy-start | bytes 196
  6.7 6.8 %copy-start.3 = (f32[3,8,16,256]{3,2,1,0:T(8,128)S(1)}, f32[3,8,16,256]{3,2,1,0:T(8,128)}, u32[]{:S(2)}) copy-start(f32[3,8,16,256]{3,2,1,0:T(8,128)} %v.5) | copy-start | bytes 1179652
  6.7 6.7 %collective-permute-start.1 = (f32[152,256]{1,0:T(8,128)S(1)}, f32[152,256]{1,0:T(8,128)S(1)}, u32[]{:S(2)}, u32[]{:S(2)}) collective-permute-start(f32[152,256]{1,0:T(8,128)S(1)} %pack_cross.1), channel_id=1, source_target_pairs={{0,8},{8,16},{12,4},{16,24},{20,12},{24,32},{28,20},{32,40},{36,28... | collective-permute-start | bytes 466952 | tf_op jit(solution)/shard_map/ppermute | solution.py:774
  13.5 16.1 %collective-permute-start.2 = (f32[224,256]{1,0:T(8,128)S(1)}, f32[224,256]{1,0:T(8,128)S(1)}, u32[]{:S(2)}, u32[]{:S(2)}) collective-permute-start(f32[224,256]{1,0:T(8,128)S(1)} %get-tuple-element.34), channel_id=1, source_target_pairs={{0,1},{1,2},{2,3},{4,5},{5,6},{6,7},{8,9},{9,10},{10,11},{12,13},{... | collective-permute-start | bytes 688136 | tf_op jit(solution)/shard_map/ppermute | solution.py:757
  16.1 13.5 %collective-permute-start.3 = (f32[192,256]{1,0:T(8,128)S(1)}, f32[192,256]{1,0:T(8,128)S(1)}, u32[]{:S(2)}, u32[]{:S(2)}) collective-permute-start(f32[192,256]{1,0:T(8,128)S(1)} %get-tuple-element.35), channel_id=1, source_target_pairs={{1,0},{2,1},{3,2},{5,4},{6,5},{7,6},{9,8},{10,9},{11,10},{13,12},{... | collective-permute-start | bytes 589832 | tf_op jit(solution)/shard_map/ppermute | solution.py:757
  18.8 7.7 %collective-permute-start.4 = (f32[152,256]{1,0:T(8,128)S(1)}, f32[152,256]{1,0:T(8,128)S(1)}, u32[]{:S(2)}, u32[]{:S(2)}) collective-permute-start(f32[152,256]{1,0:T(8,128)S(1)} %collective-permute-done.1.far), channel_id=1, source_target_pairs={{2,6},{6,2},{10,14},{14,10},{18,22},{22,18},{26,30},{30,26},{34,38... | collective-permute-start | bytes 466952 | tf_op jit(solution)/shard_map/ppermute | solution.py:790
  27.3 3.8 %collective-permute-start.5 = (f32[24,256]{1,0:T(8,128)S(1)}, f32[24,256]{1,0:T(8,128)S(1)}, u32[]{:S(2)}, u32[]{:S(2)}) collective-permute-start(f32[24,256]{1,0:T(8,128)S(1)} %get-tuple-element.52.values), channel_id=1, source_target_pairs={{2,6},{6,2},{10,14},{14,10},{18,22},{22,18},{26,30},{30,26},{34,38... | collective-permute-start | bytes 73736 | tf_op jit(solution)/shard_map/ppermute | solution.py:808
  31.1 5.4 %collective-permute-start.6 = (f32[48,256]{1,0:T(8,128)S(1)}, f32[48,256]{1,0:T(8,128)S(1)}, u32[]{:S(2)}, u32[]{:S(2)}) collective-permute-start(f32[48,256]{1,0:T(8,128)S(1)} %pack_new_cross.1), channel_id=1, source_target_pairs={{4,8},{12,16},{20,24},{28,32},{36,40},{44,48},{52,56},{60,64},{68,... | collective-permute-start | bytes 147464 | tf_op jit(solution)/shard_map/ppermute | solution.py:821
  36.5 6.4 %collective-permute-start.7 = (f32[48,256]{1,0:T(8,128)S(1)}, f32[48,256]{1,0:T(8,128)S(1)}, u32[]{:S(2)}, u32[]{:S(2)}) collective-permute-start(f32[48,256]{1,0:T(8,128)S(1)} %pack_last.1), channel_id=1, source_target_pairs={{0,4},{4,0},{8,12},{12,8},{16,20},{20,16},{24,28},{28,24},{32,36},... | collective-permute-start | bytes 147464 | tf_op jit(solution)/shard_map/ppermute | solution.py:832

commit v6 on v5

--- a/solution.py
+++ b/solution.py
@@ -14,7 +14,8 @@
 QUADS = ((0, 0), (0, 1), (1, 0), (1, 1))
 
 COL_HI, COL_LO, LISTS, PAD, EXPORT_ROWS = 0, 40, 64, 88, 136
-OWN_OPP2, MATE_FAR1, MATE_FAR2, OWN_PAD, MATE_PAD, CROSS_ROWS = 40, 44, 48, 56, 104, 152
+OWN_OPP2, MATE_FAR1, OWN_PAD, MATE_PAD, CROSS_ROWS = 40, 44, 48, 96, 144
+SKIP_LIST, SKIP_PAD, SKIP_ROWS = 0, 8, 232
 COL_LAB, COL_DT, COL_BEYOND, COLS_ROWS = 24, 32, 40, 64
 ZU_U, ZU_V, ZU_LAB, ZU_DT, ZU_CL, ZU_CH, ZU_CLAB, ZU_CDT, ZU_ROWS = 0, 96, 144, 176, 208, 214, 220, 222, 224
 ZD_U, ZD_V, ZD_LAB, ZD_DT, ZD_CL, ZD_CH, ZD_CLAB, ZD_CDT, ZD_ROWS = 0, 96, 144, 160, 176, 182, 188, 189, 192
@@ -99,7 +100,7 @@
     copy.wait()
 
 
-def pack_cross(own, mate, out):
+def pack_cross(own, mate, out, skip):
     even = on_even()
 
     def bucket(ref, if_even, if_odd):
@@ -110,10 +111,11 @@
     out[0:24, :] = jnp.where(even, mate[COL_HI : COL_HI + 24, :], mate[COL_LO : COL_LO + 24, :])
     out[OWN_OPP2 : OWN_OPP2 + 4, :] = bucket(own, 4, 0)
     out[MATE_FAR1 : MATE_FAR1 + 4, :] = bucket(mate, 3, 1)
-    out[MATE_FAR2 : MATE_FAR2 + 4, :] = bucket(mate, 4, 0)
-    out[MATE_FAR2 + 4 : OWN_PAD, :] = jnp.zeros((OWN_PAD - MATE_FAR2 - 4, 256), F32)
     out[OWN_PAD : OWN_PAD + 48, :] = own[PAD : PAD + 48, :]
     out[MATE_PAD : MATE_PAD + 48, :] = mate[PAD : PAD + 48, :]
+    skip[SKIP_LIST : SKIP_LIST + 4, :] = bucket(own, 0, 4)
+    skip[SKIP_LIST + 4 : SKIP_PAD, :] = jnp.zeros((4, 256), F32)
+    skip[SKIP_PAD : SKIP_PAD + 48, :] = own[PAD : PAD + 48, :]
 
 
 def pack_layer(u, v, dt, lab, near, far, up, dn, cols):
@@ -257,7 +259,7 @@
     for c in range(3):
         node = [low[c][q] + pltpu.roll(high[c][q], 1, 0) for q in range(4)]
         t0, t1 = fold_y(node[0], node[1]), fold_y(node[2], node[3])
-        forces.append(t0 + t1 if side > 0 else t0 - t1)
+        forces.append(t0 + side * t1)
     if with_mass:
         rho = rho + pltpu.roll(rho, 1, 1)
         rho = rho + pltpu.roll(rho, 1, 0)
@@ -389,7 +391,7 @@
         FAR1: (far, MATE_FAR1),
         OWN: (own, LISTS + 8),
         FAR2: (far, OWN_OPP2),
-        OPP2: (opp, MATE_FAR2),
+        OPP2: (opp, SKIP_LIST),
     }
     for role, (ref, base) in sources.items():
         cols = slice(128 * role, 128 * role + 128)
@@ -405,7 +407,7 @@
 
 def first_block(layers, u, dt, lab, par, force, mass, modes, saved, saved_m):
     zbase = lax.axis_index("layer") * 8
-    block_forces(layers, 7, 1, zbase, material_scalars(par), u, lab, dt, modes, saved, saved_m, force, mass)
+    block_forces(layers, 7, 7, zbase, material_scalars(par), u, lab, dt, modes, saved, saved_m, force, mass)
 
 
 def first_inner(
@@ -452,7 +454,7 @@
             FAR1: far[MATE_PAD : MATE_PAD + 48, :],
             OWN: own_pad,
             FAR2: far[OWN_PAD : OWN_PAD + 48, :],
-            OPP2: opp[MATE_PAD : MATE_PAD + 48, :],
+            OPP2: opp[SKIP_PAD : SKIP_PAD + 48, :],
         }
         far_pad = []
         for role in range(5):
@@ -606,32 +608,27 @@
     block_forces(layers, 9, 3, zbase, material_scalars(par), u, le, de, modes, saved, None, force, None)
 
 
-def second_column(blocks, layers, at, src, own_row, dt, lab, par, cols, zb, ends, col, col_lab, col_dt):
+def second_column(blocks, layers, right_side, theirs, dt, lab, par, cols, zb, ends, col, col_lab, col_dt):
     layer, here = lax.axis_index("layer"), lax.axis_index("plane")
     zeros = jnp.zeros((8, 256), F32)
+    mine = jnp.where(right_side, ends[NEW_HI : NEW_HI + 32, :], ends[NEW_LO : NEW_LO + 32, :])
+    left, right = jnp.where(right_side, mine, theirs), jnp.where(right_side, theirs, mine)
     for c in range(3):
-        col[0, c, 8:16, :] = zeros
-        col[1, c, 8:16, :] = zeros
-        col[0, c, 0:10, :] = src[10 * c : 10 * c + 10, :]
-        col[1, c, 0:10, :] = ends[own_row + 10 * c : own_row + 10 * c + 10, :]
+        for i, value in enumerate((left, right)):
+            col[i, c, 8:16, :] = zeros
+            col[i, c, 0:10, :] = value[10 * c : 10 * c + 10, :]
     for ref, field, first, zu, zuf in (
         (col_lab, lab, COL_LAB, ZU_CLAB, ZU_LAB),
         (col_dt, dt, COL_DT, ZU_CDT, ZU_DT),
     ):
         ref[8:16, :] = zeros
-        if at:
-            ref[0:1, :] = zb[zuf + 31 : zuf + 32, :]
-            ref[1:9, :] = field[:, 15, :].astype(F32)
-        else:
-            ref[0:1, :] = zb[zu + 1 : zu + 2, :]
-            ref[1:9, :] = cols[first : first + 8, :]
+        ref[0:1, :] = jnp.where(right_side, zb[zuf + 31 : zuf + 32, :], zb[zu + 1 : zu + 2, :])
+        ref[1:9, :] = jnp.where(right_side, field[:, 15, :].astype(F32), cols[first : first + 8, :])
     zg = iota((16, 256), 0) + (layer * 8 - 1)
-    inside = here < blocks - 1 if at else here > 0
-    theirs, mine = [col[0, c] for c in range(3)], [col[1, c] for c in range(3)]
-    left, right = (mine, theirs) if at else (theirs, mine)
+    inside = jnp.where(right_side, here < blocks - 1, here > 0)
     return column_forces(
-        layers, zg, zg < layer * 8 + 8, material_scalars(par), inside, -1 if at else 1, left, right,
-        col_lab[...], col_dt[...], False,
+        layers, zg, zg < layer * 8 + 8, material_scalars(par), inside, jnp.where(right_side, -1.0, 1.0),
+        [col[0, c] for c in range(3)], [col[1, c] for c in range(3)], col_lab[...], col_dt[...], False,
     )[0]
 
 
@@ -641,16 +638,13 @@
     u2, v2,
     col, col_lab, col_dt, col_f,
 ):
-    for at in (0, 1):
-        @pl.when(on_even() == (at == 0))
-        def _():
-            forces = second_column(
-                blocks, layers, at, far, NEW_HI if at else NEW_LO, dt, lab, par, cols, zb, ends, col, col_lab, col_dt
-            )
-            for c in range(3):
-                col_f[at, c] = forces[c]
-                col_f[1 - at, c] = jnp.zeros((16, 256), F32)
-
+    even = on_even()
+    forces = second_column(
+        blocks, layers, jnp.logical_not(even), far[0:32, :], dt, lab, par, cols, zb, ends, col, col_lab, col_dt
+    )
+    for c in range(3):
+        col_f[0, c] = jnp.where(even, forces[c], 0.0)
+        col_f[1, c] = jnp.where(even, 0.0, forces[c])
     for z in range(8):
         e = z + 1
         rate = dtm[e]
@@ -665,65 +659,50 @@
     blocks, layers,
     u_in, v_in, dtm, lists, mate, far, opp, dt, lab, par, cols, zb, ends,
     u2, v2,
-    u, v, col, col_lab, col_dt, sems,
+    u, v, col, col_lab, col_dt, col_f, sems,
 ):
-    u[...] = u_in[...]
-    v[...] = v_in[...]
-    for at in (0, 1):
-        @pl.when(on_even() == (at == 1))
-        def _():
-            forces = second_column(
-                blocks, layers, at, opp, NEW_HI if at else NEW_LO, dt, lab, par, cols, zb, ends, col, col_lab, col_dt
-            )
-            x = 15 if at else 0
-            rate = dtm[1:9, x, :]
-            for c in range(3):
-                change = rate * forces[c][1:9]
-                v[c, :, x, :] = v[c, :, x, :] - change
-                u[c, :, x, :] = u[c, :, x, :] - DT * change
-
-    copies = []
-    for src, dst in ((u, u2), (v, v2)):
-        for first, last in ((0, 3), (5, 8)):
-            copies.append(
-                pltpu.make_async_copy(src.at[:, first:last], dst.at[:, first:last], sems.at[len(copies)])
-            )
+    even = on_even()
+    on_face = lax.axis_index("layer") == layers // 2
+    forces = second_column(
+        blocks, layers, even, opp[0:32, :], dt, lab, par, cols, zb, ends, col, col_lab, col_dt
+    )
+    for c in range(3):
+        col_f[0, c] = jnp.where(even, 0.0, forces[c])
+        col_f[1, c] = jnp.where(even, forces[c], 0.0)
+    sol_y, sol_x = one_hots(lists[0:1, :])
+    land_y, land_x = one_hots(lists[6:7, :])
+
+    def values(i):
+        half = slice(128 * (i % 2), 128 * (i % 2) + 128)
+        own_row = (3, 4, 5, 8, 9, 10)[i]
+        places = (
+            (mate, 4 * NEAR), (far, CROSS_MATE), None, (far, CROSS_OWN), (opp, CROSS_ON)
+        )
+        parts = [
+            lists[own_row : own_row + 1, 256:384] if place is None
+            else place[0][place[1] + i // 2 : place[1] + i // 2 + 1, half]
+            for place in places
+        ]
+        return jnp.concatenate(parts, axis=1)
+
+    far_bump = jnp.concatenate([values(i) for i in range(3)], axis=0)
+    far_pad = jnp.concatenate([values(i) for i in range(3, 6)], axis=0)
+    on_bump = lists[2:3, :] * (far_pad - lists[3:6, :])
+    on_pad = lists[7:8, :] * (far_bump - lists[8:11, :])
+    extra = (scatter(on_pad, land_y, land_x), scatter(on_bump, sol_y, sol_x))
+    for z in (0, 1, 2, 5, 6, 7, 3, 4):
+        e = z + 1
+        rate = dtm[e]
+        for c in range(3):
+            pull = with_columns(jnp.zeros((16, 256), F32), col_f[0, c, e : e + 1, :], col_f[1, c, e : e + 1, :])
+            if z in (3, 4):
+                pull = pull - jnp.where(on_face, extra[z - 3][c], 0.0)
+            change = rate * pull
+            v[c, z] = v_in[c, z] - change
+            u[c, z] = u_in[c, z] - DT * change
+    copies = [pltpu.make_async_copy(src, dst, sems.at[i]) for i, (src, dst) in enumerate(((u, u2), (v, v2)))]
     for copy in copies:
         copy.start()
-
-    @pl.when(lax.axis_index("layer") == layers // 2)
-    def _():
-        sol_y, sol_x = one_hots(lists[0:1, :])
-        land_y, land_x = one_hots(lists[6:7, :])
-
-        def values(i):
-            half = slice(128 * (i % 2), 128 * (i % 2) + 128)
-            own_row = (3, 4, 5, 8, 9, 10)[i]
-            places = (
-                (mate, 4 * NEAR), (far, CROSS_MATE), None, (far, CROSS_OWN), (opp, CROSS_ON)
-            )
-            parts = [
-                lists[own_row : own_row + 1, 256:384] if place is None
-                else place[0][place[1] + i // 2 : place[1] + i // 2 + 1, half]
-                for place in places
-            ]
-            return jnp.concatenate(parts, axis=1)
-
-        far_bump = jnp.concatenate([values(i) for i in range(3)], axis=0)
-        far_pad = jnp.concatenate([values(i) for i in range(3, 6)], axis=0)
-        on_bump = lists[2:3, :] * (far_pad - lists[3:6, :])
-        on_pad = lists[7:8, :] * (far_bump - lists[8:11, :])
-        extra = (scatter(on_pad, land_y, land_x), scatter(on_bump, sol_y, sol_x))
-        for c in range(3):
-            for face in (0, 1):
-                change = dtm[4 + face] * extra[face][c]
-                u[c, 3 + face] = u[c, 3 + face] + DT * change
-                v[c, 3 + face] = v[c, 3 + face] + change
-
-    for i, (src, dst) in enumerate(((u, u2), (v, v2))):
-        copy = pltpu.make_async_copy(src.at[:, 3:5], dst.at[:, 3:5], sems.at[4 + i])
-        copy.start()
-        copies.append(copy)
     for copy in copies:
         copy.wait()
 
@@ -741,7 +720,7 @@
         out_specs=[out_spec] * len(outs),
         scratch_shapes=[pltpu.VMEM(s, F32) if isinstance(s, tuple) else s for s in scratch],
         compiler_params=pltpu.CompilerParams(vmem_limit_bytes=vmem * 1024 * 1024),
-        cost_estimate=pl.CostEstimate(flops=flops, bytes_accessed=2_000_000, transcendentals=0),
+        cost_estimate=pl.CostEstimate(flops=flops, bytes_accessed=flops // 25, transcendentals=0),
         name=name,
     )
 
@@ -770,8 +749,10 @@
     )(u, dt, lab, sol.reshape(5, 1, 128), land.reshape(5, 1, 128), stiff.reshape(5, 1, 128), tally)[0]
     near = lax.ppermute(own, "plane", swaps)
     own = call(stage, [HBM], [own.shape], [pltpu.SemaphoreType.DMA], "stage", 100_000)(own)[0]
-    cross = call(pack_cross, [VM] * 2, [(CROSS_ROWS, 256)], [], "pack_cross", 100_000)(own, near)[0]
+    cross, skip = call(pack_cross, [VM] * 2, [(CROSS_ROWS, 256), (SKIP_ROWS, 256)], [], "pack_cross", 1_000)(own, near)
     far = lax.ppermute(cross, "plane", crossings)
+    skips = [(s * layers + layers // 2, t * layers + layers // 2) for t, s in crossings]
+    opp = lax.ppermute(skip, ("plane", "layer"), skips)
     modes = [(12, 16, 256), (12, 16, 256)]
     plane = (16, 256)
     force, mass = call(
@@ -784,17 +765,16 @@
     )(u, dt, lab, par)
     far, force, mass = lax.optimization_barrier((far, force, mass))
     up, dn, cols = call(
-        pack_layer, [VM] * 6, [(ZU_ROWS, 256), (ZD_ROWS, 256), (COLS_ROWS, 256)], [], "pack_layer", 100_000
+        pack_layer, [VM] * 6, [(ZU_ROWS, 256), (ZD_ROWS, 256), (COLS_ROWS, 256)], [], "pack_layer", 1_000
     )(u, v, dt, lab, near, far)
     zb, za = along_layer(up, 1), along_layer(dn, -1)
-    opp = lax.ppermute(far, ("plane", "layer"), face_swaps)
     u1, v1, dtm, in_f, in_m = call(
         functools.partial(first_inner, blocks, layers),
         [VM] * 2 + [SM] + [VM] * 4,
         [(3, 6, 16, 256), (3, 6, 16, 256), (6, 16, 256), (2, 3, 8, 256), (2, 8, 256)],
         [],
         "first_inner",
-        10_000_000,
+        1_000,
     )(u, v, par, own, cols, force, mass)
     opp, u1, v1 = lax.optimization_barrier((opp, u1, v1))
     u_face, v_face, values, lists = call(
@@ -844,7 +824,7 @@
             functools.partial(second_contact, blocks, layers),
             [VM] * 9 + [SM] + [VM] * 3,
             [(3, 8, 16, 256)] * 2,
-            [(3, 8, 16, 256)] * 2 + column + [pltpu.SemaphoreType.DMA((6,))],
+            [(3, 8, 16, 256)] * 2 + column + [(2, 3, 16, 256), pltpu.SemaphoreType.DMA((2,))],
             "second_contact",
             10_000_000,
             out_spec=HBM,

time: 45.3 us -> 44.7 us (0.987)
  the two profiles are of different devices: /device:TPU:261 before, /device:TPU:259 now
where the time goes in v6:
time: 44.7 us; the launch traced here: 44.3 us
  starting transfers between devices  27.9 us (62%)
  Pallas kernels  11.3 us (25%)
  waiting for transfers between devices  3.3 us (7%)
  local copies, waits for them, and re-layouts  0.93 us (2%)
  between operations  0.9 us (2%)
    ppermute x1, starting transfers between devices, local(): opp = lax.ppermute(last, 'plane', swaps)  8.26 us
    ppermute x2, starting transfers between devices, along_layer(): return lax.ppermute(value, 'layer', pairs)  6.54 us
    ppermute x1, starting transfers between devices, local(): far = lax.ppermute(cross, 'plane', across)  4.77 us
    ppermute x1, starting transfers between devices, local(): far = lax.ppermute(cross, 'plane', crossings)  4.32 us
    ppermute x2, waiting for transfers between devices, along_layer(): return lax.ppermute(value, 'layer', pairs)  3.19 us
    ppermute x1, starting transfers between devices, local(): near = lax.ppermute(own, 'plane', swaps)  2.71 us
    pallas_call x1, Pallas kernels, local(): call(functools.partial(second_block, layers), [VM] * 3 + [SM, VM], [(3, 1...  2.13 us
    pallas_call x1, Pallas kernels, local(): call(functools.partial(second_contact, blocks, layers), [VM] * 9 + [SM] +...  1.99 us
  transfers between devices with their start and end apart: 8, of which 2 were waited for; matrix products, arithmetic and copies ran while one was open for 0% of the time, Pallas kernels for 17%

profile of v6, /device:TPU:259, one launch (start us, length us, event | category | flops | bytes accessed | tf_op | source)
XLA Modules:
  0.0 44.3 jit_solution(14365780815591428899)
XLA Ops:
  0.6 1.9 %pack_export.1.src = f32[136,256]{1,0:T(8,128)} custom-call(f32[3,8,16,256]{3,2,1,0:T(8,128)} %u.7, f32[8,16,256]{2,1,0:T(8,128)} %dt.11, s32[8,16,256]{2,1,0:T(8,128)} %lab.11, s32[5,1,128]{2,1,0:T(1,128)} %bitcast.3, s32[5,1,128]{2,1,0:T(1,128)} %bitcast.4, f32[5,1,128]{2,1,0:T(1,128)} %bitcast.5, s32[1,5]{1,0:T(1,128)} %tally_hbm.1), custom_call_target="tpu_custom_call" | custom-call | flops 100000 | bytes 4000 | tf_op jit(solution)/shard_map/pack_export/pallas_call | solution.py:738
  2.5 0.0 copy-start
  2.5 2.7 %collective-permute-start = (f32[136,256]{1,0:T(8,128)}, f32[136,256]{1,0:T(8,128)S(1)}, u32[]{:S(2)}, u32[]{:S(2)}) collective-permute-start(f32[136,256]{1,0:T(8,128)} %pack_export.1.src), channel_id=1, source_target_pairs={{0,4},{4,0},{8,12},{12,8},{16,20},{20,16},{24,28},{28,24},{32,36},... | collective-permute-start | bytes 417800 | tf_op jit(solution)/shard_map/ppermute | solution.py:750
  5.3 0.0 copy-start.4
  5.3 0.9 %copy-done.4 = f32[136,256]{1,0:T(8,128)S(1)} copy-done((f32[136,256]{1,0:T(8,128)S(1)}, f32[136,256]{1,0:T(8,128)}, u32[]{:S(2)}) %copy-start.4) | copy-done | bytes 139288
  6.2 0.2 stage.1.own
  6.3 0.0 copy-start.1
  6.3 0.1 collective-permute-done.mate.near
  6.5 0.0 copy-start.3
  6.5 4.3 %collective-permute-start.1 = (f32[144,256]{1,0:T(8,128)S(1)}, f32[144,256]{1,0:T(8,128)S(1)}, u32[]{:S(2)}, u32[]{:S(2)}) collective-permute-start(f32[144,256]{1,0:T(8,128)S(1)} %get-tuple-element.32), channel_id=1, source_target_pairs={{0,8},{8,16},{12,4},{16,24},{20,12},{24,32},{28,20},{32,40},{36,28... | collective-permute-start | bytes 442376 | tf_op jit(solution)/shard_map/ppermute | solution.py:753
  10.8 0.7 %collective-permute-start.4 = (f32[232,256]{1,0:T(8,128)S(1)}, f32[232,256]{1,0:T(8,128)S(1)}, u32[]{:S(2)}, u32[]{:S(2)}) collective-permute-start(f32[232,256]{1,0:T(8,128)S(1)} %get-tuple-element.43), channel_id=1, source_target_pairs={{10,2},{18,10},{6,14},{26,18},{14,22},{34,26},{22,30},{42,34},{30,... | collective-permute-start | bytes 712712 | tf_op jit(solution)/shard_map/ppermute | solution.py:755
  11.5 1.8 %first_block.1 = (f32[3,8,16,256]{3,2,1,0:T(8,128)S(1)}, f32[8,16,256]{2,1,0:T(8,128)S(1)}) custom-call(f32[3,8,16,256]{3,2,1,0:T(8,128)S(1)} %copy-done, f32[8,16,256]{2,1,0:T(8,128)S(1)} %copy-done.1, s32[8,16,256]{2,1,0:T(8,128)S(1)} %copy-done.2, f32[4,4]{1,0:T(4,128)S(1)} %copy-done.5), custom_call_target="tpu_custom_call" | custom-call | flops 50000000 | bytes 2000000 | tf_op jit(solution)/shard_map/first_block/pallas_call | solution.py:758
  13.3 0.1 pack_layer.1
  13.4 4.6 %collective-permute-start.2 = (f32[224,256]{1,0:T(8,128)S(1)}, f32[224,256]{1,0:T(8,128)S(1)}, u32[]{:S(2)}, u32[]{:S(2)}) collective-permute-start(f32[224,256]{1,0:T(8,128)S(1)} %get-tuple-element.37), channel_id=1, source_target_pairs={{0,1},{1,2},{2,3},{4,5},{5,6},{6,7},{8,9},{9,10},{10,11},{12,13},{... | collective-permute-start | bytes 688136 | tf_op jit(solution)/shard_map/ppermute | solution.py:736
  18.0 1.9 %collective-permute-start.3 = (f32[192,256]{1,0:T(8,128)S(1)}, f32[192,256]{1,0:T(8,128)S(1)}, u32[]{:S(2)}, u32[]{:S(2)}) collective-permute-start(f32[192,256]{1,0:T(8,128)S(1)} %get-tuple-element.38), channel_id=1, source_target_pairs={{1,0},{2,1},{3,2},{5,4},{6,5},{7,6},{9,8},{10,9},{11,10},{13,12},{... | collective-permute-start | bytes 589832 | tf_op jit(solution)/shard_map/ppermute | solution.py:736
  19.9 0.9 %first_inner.1 = (f32[3,6,16,256]{3,2,1,0:T(8,128)S(1)}, f32[3,6,16,256]{3,2,1,0:T(8,128)S(1)}, f32[6,16,256]{2,1,0:T(8,128)S(1)}, f32[2,3,8,256]{3,2,1,0:T(8,128)S(1)}, f32[2,8,256]{2,1,0:T(8,128)S(1)}) custom-call(f32[3,8,16,256]{3,2,1,0:T(8,128)S(1)} %copy-done, f32[3,8,16,256]{3,2,1,0:T(8,128)S(1)} %copy-done.3, f32[4,4]{1,0:T(4,128)S(1)} %copy-done.5, ...), custom_call_target="tpu_custom_call" | custom-call | flops 1000 | bytes 40 | tf_op jit(solution)/shard_map/first_inner/pallas_call | solution.py:771
  20.9 0.7 %collective-permute-start.5 = (f32[24,256]{1,0:T(8,128)S(1)}, f32[24,256]{1,0:T(8,128)S(1)}, u32[]{:S(2)}, u32[]{:S(2)}) collective-permute-start(f32[24,256]{1,0:T(8,128)S(1)} %get-tuple-element.56.values), channel_id=1, source_target_pairs={{2,6},{6,2},{10,14},{14,10},{18,22},{22,18},{26,30},{30,26},{34,38... | collective-permute-start | bytes 73736 | tf_op jit(solution)/shard_map/ppermute | solution.py:788
  21.5 3.2 %collective-permute-done.3.za = f32[192,256]{1,0:T(8,128)S(1)} collective-permute-done((f32[192,256]{1,0:T(8,128)S(1)}, f32[192,256]{1,0:T(8,128)S(1)}, u32[]{:S(2)}, u32[]{:S(2)}) %collective-permute-start.3) | collective-permute-done | bytes 196640 | tf_op jit(solution)/shard_map/ppermute | solution.py:736
  24.7 1.4 %first_step.1 = (f32[3,10,16,256]{3,2,1,0:T(8,128)S(1)}, f32[3,10,16,256]{3,2,1,0:T(8,128)S(1)}, f32[10,16,256]{2,1,0:T(8,128)S(1)}, f32[64,256]{1,0:T(8,128)S(1)}) custom-call(f32[3,8,16,256]{3,2,1,0:T(8,128)S(1)} %copy-done, f32[3,8,16,256]{3,2,1,0:T(8,128)S(1)} %copy-done.3, f32[8,16,256]{2,1,0:T(8,128)S(1)} %copy-done.1, s32[8,16,256]{2,1,0:T(8,128)S(1)} %copy-done.2, ...), custom_call_target="tpu_custom_call" | custom-call | flops 20000000 | bytes 800000 | tf_op jit(solution)/shard_map/first_step/pallas_call | solution.py:791
  26.2 4.8 %collective-permute-start.6 = (f32[48,256]{1,0:T(8,128)S(1)}, f32[48,256]{1,0:T(8,128)S(1)}, u32[]{:S(2)}, u32[]{:S(2)}) collective-permute-start(f32[48,256]{1,0:T(8,128)S(1)} %pack_new_cross.1), channel_id=1, source_target_pairs={{4,8},{12,16},{20,24},{28,32},{36,40},{44,48},{52,56},{60,64},{68,... | collective-permute-start | bytes 147464 | tf_op jit(solution)/shard_map/ppermute | solution.py:801
  30.9 2.1 %second_block.1.force = f32[3,10,16,256]{3,2,1,0:T(8,128)S(1)} custom-call(f32[3,10,16,256]{3,2,1,0:T(8,128)S(1)} %get-tuple-element.52.u, f32[8,16,256]{2,1,0:T(8,128)S(1)} %copy-done.1, s32[8,16,256]{2,1,0:T(8,128)S(1)} %copy-done.2, f32[4,4]{1,0:T(4,128)S(1)} %copy-done.5, f32[224,256]{1,0:T(8,128)S(1)} %collective-permute-done.2.zb), custom_call_target="tpu_custom_call" | custom-call | flops 50000000 | bytes 2000000 | tf_op jit(solution)/shard_map/second_block/pallas_call | solution.py:802
  33.1 8.3 %collective-permute-start.7 = (f32[48,256]{1,0:T(8,128)S(1)}, f32[48,256]{1,0:T(8,128)S(1)}, u32[]{:S(2)}, u32[]{:S(2)}) collective-permute-start(f32[48,256]{1,0:T(8,128)S(1)} %pack_last.1), channel_id=1, source_target_pairs={{0,4},{4,0},{8,12},{12,8},{16,20},{20,16},{24,28},{28,24},{32,36},... | collective-permute-start | bytes 147464 | tf_op jit(solution)/shard_map/ppermute | solution.py:812
  41.4 0.9 %second_step.1 = (f32[3,8,16,256]{3,2,1,0:T(8,128)S(1)}, f32[3,8,16,256]{3,2,1,0:T(8,128)S(1)}) custom-call(f32[3,10,16,256]{3,2,1,0:T(8,128)S(1)} %get-tuple-element.52.u, f32[3,10,16,256]{3,2,1,0:T(8,128)S(1)} %get-tuple-element.53.v, f32[10,16,256]{2,1,0:T(8,128)S(1)} %get-tuple-element.54.dtm, f32[8,16,256]{2,1,0:T(8,128)S(1)} %copy-done.1, ...), custom_call_target="tpu_custom_call" | custom-call | flops 20000000 | bytes 800000 | tf_op jit(solution)/shard_map/second_step/pallas_call | solution.py:814
  42.3 2.0 %second_contact.1 = (f32[3,8,16,256]{3,2,1,0:T(8,128)}, f32[3,8,16,256]{3,2,1,0:T(8,128)}) custom-call(f32[3,8,16,256]{3,2,1,0:T(8,128)S(1)} %get-tuple-element.59.u_in, f32[3,8,16,256]{3,2,1,0:T(8,128)S(1)} %get-tuple-element.60.v_in, f32[10,16,256]{2,1,0:T(8,128)S(1)} %get-tuple-element.54.dtm, f32[16,640]{1,0:T(8,128)S(1)} %get-tuple-element.61.lists, ...), custom_call_target="tpu_custom_call" | custom-call | flops 10000000 | bytes 400000 | tf_op jit(solution)/shard_map/second_contact/pallas_call | solution.py:823
  (17 shorter events, 0.1 us)
Async XLA Ops:
  0.6 10.9 %copy-start.2 = (s32[8,16,256]{2,1,0:T(8,128)S(1)}, s32[8,16,256]{2,1,0:T(8,128)}, u32[]{:S(2)}) copy-start(s32[8,16,256]{2,1,0:T(8,128)} %lab.11) | copy-start | bytes 393220
  2.5 9.0 %copy-start = (f32[3,8,16,256]{3,2,1,0:T(8,128)S(1)}, f32[3,8,16,256]{3,2,1,0:T(8,128)}, u32[]{:S(2)}) copy-start(f32[3,8,16,256]{3,2,1,0:T(8,128)} %u.7) | copy-start | bytes 1179652
  2.5 3.9 %collective-permute-start = (f32[136,256]{1,0:T(8,128)}, f32[136,256]{1,0:T(8,128)S(1)}, u32[]{:S(2)}, u32[]{:S(2)}) collective-permute-start(f32[136,256]{1,0:T(8,128)} %pack_export.1.src), channel_id=1, source_target_pairs={{0,4},{4,0},{8,12},{12,8},{16,20},{20,16},{24,28},{28,24},{32,36},... | collective-permute-start | bytes 417800 | tf_op jit(solution)/shard_map/ppermute | solution.py:750
  5.3 0.9 %copy-start.4 = (f32[136,256]{1,0:T(8,128)S(1)}, f32[136,256]{1,0:T(8,128)}, u32[]{:S(2)}) copy-start(f32[136,256]{1,0:T(8,128)} %pack_export.1.src) | copy-start | bytes 417796
  6.3 5.2 %copy-start.1 = (f32[8,16,256]{2,1,0:T(8,128)S(1)}, f32[8,16,256]{2,1,0:T(8,128)}, u32[]{:S(2)}) copy-start(f32[8,16,256]{2,1,0:T(8,128)} %dt.11) | copy-start | bytes 393220
  6.4 5.1 %copy-start.5 = (f32[4,4]{1,0:T(4,128)S(1)}, f32[4,4]{1,0:T(4,128)}, u32[]{:S(2)}) copy-start(f32[4,4]{1,0:T(4,128)} %par.11) | copy-start | bytes 196
  6.5 6.8 %copy-start.3 = (f32[3,8,16,256]{3,2,1,0:T(8,128)S(1)}, f32[3,8,16,256]{3,2,1,0:T(8,128)}, u32[]{:S(2)}) copy-start(f32[3,8,16,256]{3,2,1,0:T(8,128)} %v.5) | copy-start | bytes 1179652
  6.5 6.8 %collective-permute-start.1 = (f32[144,256]{1,0:T(8,128)S(1)}, f32[144,256]{1,0:T(8,128)S(1)}, u32[]{:S(2)}, u32[]{:S(2)}) collective-permute-start(f32[144,256]{1,0:T(8,128)S(1)} %get-tuple-element.32), channel_id=1, source_target_pairs={{0,8},{8,16},{12,4},{16,24},{20,12},{24,32},{28,20},{32,40},{36,28... | collective-permute-start | bytes 442376 | tf_op jit(solution)/shard_map/ppermute | solution.py:753
  10.8 10.0 %collective-permute-start.4 = (f32[232,256]{1,0:T(8,128)S(1)}, f32[232,256]{1,0:T(8,128)S(1)}, u32[]{:S(2)}, u32[]{:S(2)}) collective-permute-start(f32[232,256]{1,0:T(8,128)S(1)} %get-tuple-element.43), channel_id=1, source_target_pairs={{10,2},{18,10},{6,14},{26,18},{14,22},{34,26},{22,30},{42,34},{30,... | collective-permute-start | bytes 712712 | tf_op jit(solution)/shard_map/ppermute | solution.py:755
  13.4 11.3 %collective-permute-start.2 = (f32[224,256]{1,0:T(8,128)S(1)}, f32[224,256]{1,0:T(8,128)S(1)}, u32[]{:S(2)}, u32[]{:S(2)}) collective-permute-start(f32[224,256]{1,0:T(8,128)S(1)} %get-tuple-element.37), channel_id=1, source_target_pairs={{0,1},{1,2},{2,3},{4,5},{5,6},{6,7},{8,9},{9,10},{10,11},{12,13},{... | collective-permute-start | bytes 688136 | tf_op jit(solution)/shard_map/ppermute | solution.py:736
  18.0 6.7 %collective-permute-start.3 = (f32[192,256]{1,0:T(8,128)S(1)}, f32[192,256]{1,0:T(8,128)S(1)}, u32[]{:S(2)}, u32[]{:S(2)}) collective-permute-start(f32[192,256]{1,0:T(8,128)S(1)} %get-tuple-element.38), channel_id=1, source_target_pairs={{1,0},{2,1},{3,2},{5,4},{6,5},{7,6},{9,8},{10,9},{11,10},{13,12},{... | collective-permute-start | bytes 589832 | tf_op jit(solution)/shard_map/ppermute | solution.py:736
  20.9 5.3 %collective-permute-start.5 = (f32[24,256]{1,0:T(8,128)S(1)}, f32[24,256]{1,0:T(8,128)S(1)}, u32[]{:S(2)}, u32[]{:S(2)}) collective-permute-start(f32[24,256]{1,0:T(8,128)S(1)} %get-tuple-element.56.values), channel_id=1, source_target_pairs={{2,6},{6,2},{10,14},{14,10},{18,22},{22,18},{26,30},{30,26},{34,38... | collective-permute-start | bytes 73736 | tf_op jit(solution)/shard_map/ppermute | solution.py:788
  26.2 6.9 %collective-permute-start.6 = (f32[48,256]{1,0:T(8,128)S(1)}, f32[48,256]{1,0:T(8,128)S(1)}, u32[]{:S(2)}, u32[]{:S(2)}) collective-permute-start(f32[48,256]{1,0:T(8,128)S(1)} %pack_new_cross.1), channel_id=1, source_target_pairs={{4,8},{12,16},{20,24},{28,32},{36,40},{44,48},{52,56},{60,64},{68,... | collective-permute-start | bytes 147464 | tf_op jit(solution)/shard_map/ppermute | solution.py:801
  33.1 9.2 %collective-permute-start.7 = (f32[48,256]{1,0:T(8,128)S(1)}, f32[48,256]{1,0:T(8,128)S(1)}, u32[]{:S(2)}, u32[]{:S(2)}) collective-permute-start(f32[48,256]{1,0:T(8,128)S(1)} %pack_last.1), channel_id=1, source_target_pairs={{0,4},{4,0},{8,12},{12,8},{16,20},{20,16},{24,28},{28,24},{32,36},... | collective-permute-start | bytes 147464 | tf_op jit(solution)/shard_map/ppermute | solution.py:812

commit v7 on v6

--- a/solution.py
+++ b/solution.py
@@ -19,8 +19,8 @@
 COL_LAB, COL_DT, COL_BEYOND, COLS_ROWS = 24, 32, 40, 64
 ZU_U, ZU_V, ZU_LAB, ZU_DT, ZU_CL, ZU_CH, ZU_CLAB, ZU_CDT, ZU_ROWS = 0, 96, 144, 176, 208, 214, 220, 222, 224
 ZD_U, ZD_V, ZD_LAB, ZD_DT, ZD_CL, ZD_CH, ZD_CLAB, ZD_CDT, ZD_ROWS = 0, 96, 144, 160, 176, 182, 188, 189, 192
-NEW_HI, NEW_LO, NEW_ROWS, VALUES_ROWS = 0, 32, 64, 24
-CROSS_OWN, CROSS_MATE, CROSS_ON, NEW_CROSS_ROWS = 32, 36, 40, 48
+NEW_HI, NEW_LO, NEW_ROWS, VALUES_ROWS = 0, 48, 96, 24
+CROSS_OWN, CROSS_MATE, CROSS_ON, NEW_CROSS_ROWS = 48, 52, 56, 64
 NEAR, FAR1, OWN, FAR2, OPP2 = range(5)
 OFFSETS = (1, -1, 0, -2, 2)
 
@@ -251,19 +251,24 @@
     shape = (rows, 256)
     ok = (zg >= 0) & (zg <= layers * 8 - 2) & (zg != layers // 2 * 8 + 3) & (iota(shape, 1) < 255)
     mask = jnp.where(ok & valid & inside, 1.0, 0.0)
-    l1, m1, k3, th, rho = cell_fields(mats, lab, dt, mask, with_mass)
+    *fields, rho = cell_fields(mats, lab, dt, mask, with_mass)
+    if with_mass:
+        rho = rho + pltpu.roll(rho, 1, 1)
+        rho = rho + pltpu.roll(rho, 1, 0)
+    return column_part(fields, side, left, right), rho
+
+
+def column_part(fields, side, left, right):
+    rows = left[0].shape[0]
     lower = [plane_modes(left[c], right[c]) for c in range(3)]
     upper = [[pltpu.roll(a, rows - 1, 0) for a in comp] for comp in lower]
-    low, high = cell_forces(lower, upper, l1, m1, k3, th)
+    low, high = cell_forces(lower, upper, *fields)
     forces = []
     for c in range(3):
         node = [low[c][q] + pltpu.roll(high[c][q], 1, 0) for q in range(4)]
         t0, t1 = fold_y(node[0], node[1]), fold_y(node[2], node[3])
         forces.append(t0 + side * t1)
-    if with_mass:
-        rho = rho + pltpu.roll(rho, 1, 1)
-        rho = rho + pltpu.roll(rho, 1, 0)
-    return forces, rho
+    return forces
 
 
 def block_forces(layers, cells, group, zbase, mats, u, lab, dt, modes, saved, saved_m, force, mass):
@@ -582,66 +587,62 @@
 
     for x, row in ((15, NEW_HI), (0, NEW_LO)):
         for c in range(3):
-            ends[row + 10 * c : row + 10 * c + 8, :] = u1[c, 0:8, x, :]
-            ends[row + 10 * c + 8 : row + 10 * c + 10, :] = u1[c, 8:10, x, :]
-        ends[row + 30 : row + 32, :] = jnp.zeros((2, 256), F32)
+            ends[row + 16 * c : row + 16 * c + 8, :] = u1[c, 0:8, x, :]
+            ends[row + 16 * c + 8 : row + 16 * c + 16, :] = jnp.zeros((8, 256), F32)
+            ends[row + 16 * c + 8 : row + 16 * c + 10, :] = u1[c, 8:10, x, :]
 
 
 def pack_new_cross(ends, values, mate, out):
-    out[0:32, :] = jnp.where(on_even(), ends[NEW_LO : NEW_LO + 32, :], ends[NEW_HI : NEW_HI + 32, :])
+    out[0:48, :] = jnp.where(on_even(), ends[NEW_LO : NEW_LO + 48, :], ends[NEW_HI : NEW_HI + 48, :])
     for row, src, role in ((CROSS_OWN, mate, OPP2), (CROSS_MATE, values, FAR1), (CROSS_ON, values, FAR2)):
         out[row : row + 4, :] = src[4 * role : 4 * role + 4, :]
-    out[44:48, :] = jnp.zeros((4, 256), F32)
+    out[60:64, :] = jnp.zeros((4, 256), F32)
 
 
 def pack_last(ends, far, out):
-    out[0:32, :] = jnp.where(on_even(), ends[NEW_HI : NEW_HI + 32, :], ends[NEW_LO : NEW_LO + 32, :])
-    out[32:48, :] = far[32:48, :]
-
-
-def second_block(layers, u, dt, lab, par, zb, force, le, de, modes, saved):
+    out[0:48, :] = jnp.where(on_even(), ends[NEW_HI : NEW_HI + 48, :], ends[NEW_LO : NEW_LO + 48, :])
+    out[48:64, :] = far[48:64, :]
+
+
+def second_block(blocks, layers, u, dt, lab, par, zb, cols, force, fields, le, de, col, modes, saved):
+    layer, here = lax.axis_index("layer"), lax.axis_index("plane")
+    mats = material_scalars(par)
     le[0] = zb[ZU_LAB + 16 : ZU_LAB + 32, :]
     de[0] = zb[ZU_DT + 16 : ZU_DT + 32, :]
     le[1:9] = lab[...].astype(F32)
     de[1:9] = dt[...]
-    zbase = lax.axis_index("layer") * 8 - 1
-    block_forces(layers, 9, 3, zbase, material_scalars(par), u, le, de, modes, saved, None, force, None)
-
-
-def second_column(blocks, layers, right_side, theirs, dt, lab, par, cols, zb, ends, col, col_lab, col_dt):
-    layer, here = lax.axis_index("layer"), lax.axis_index("plane")
-    zeros = jnp.zeros((8, 256), F32)
-    mine = jnp.where(right_side, ends[NEW_HI : NEW_HI + 32, :], ends[NEW_LO : NEW_LO + 32, :])
-    left, right = jnp.where(right_side, mine, theirs), jnp.where(right_side, theirs, mine)
+    row = iota((16, 256), 0)
+    zg = row + (layer * 8 - 1)
+    ok = (zg >= 0) & (zg <= layers * 8 - 2) & (zg != layers // 2 * 8 + 3) & (row < 9) & (iota((16, 256), 1) < 255)
+    for at in (0, 1):
+        right_side = on_even() if at else jnp.logical_not(on_even())
+        for i, (field, first, zu, zuf) in enumerate(
+            ((lab, COL_LAB, ZU_CLAB, ZU_LAB), (dt, COL_DT, ZU_CDT, ZU_DT))
+        ):
+            col[i, 8:16, :] = jnp.zeros((8, 256), F32)
+            col[i, 0:1, :] = jnp.where(right_side, zb[zuf + 31 : zuf + 32, :], zb[zu + 1 : zu + 2, :])
+            col[i, 1:9, :] = jnp.where(right_side, field[:, 15, :].astype(F32), cols[first : first + 8, :])
+        inside = jnp.where(right_side, here < blocks - 1, here > 0)
+        mask = jnp.where(ok & inside, 1.0, 0.0)
+        for i, value in enumerate(cell_fields(mats, col[0], col[1], mask, False)[:4]):
+            fields[at, i] = value
+    block_forces(layers, 9, 3, layer * 8 - 1, mats, u, le, de, modes, saved, None, force, None)
+
+
+def second_column(at, fields, ends, theirs):
+    right_side = on_even() if at else jnp.logical_not(on_even())
+    left, right = [], []
     for c in range(3):
-        for i, value in enumerate((left, right)):
-            col[i, c, 8:16, :] = zeros
-            col[i, c, 0:10, :] = value[10 * c : 10 * c + 10, :]
-    for ref, field, first, zu, zuf in (
-        (col_lab, lab, COL_LAB, ZU_CLAB, ZU_LAB),
-        (col_dt, dt, COL_DT, ZU_CDT, ZU_DT),
-    ):
-        ref[8:16, :] = zeros
-        ref[0:1, :] = jnp.where(right_side, zb[zuf + 31 : zuf + 32, :], zb[zu + 1 : zu + 2, :])
-        ref[1:9, :] = jnp.where(right_side, field[:, 15, :].astype(F32), cols[first : first + 8, :])
-    zg = iota((16, 256), 0) + (layer * 8 - 1)
-    inside = jnp.where(right_side, here < blocks - 1, here > 0)
-    return column_forces(
-        layers, zg, zg < layer * 8 + 8, material_scalars(par), inside, jnp.where(right_side, -1.0, 1.0),
-        [col[0, c] for c in range(3)], [col[1, c] for c in range(3)], col_lab[...], col_dt[...], False,
-    )[0]
-
-
-def second_step(
-    blocks, layers,
-    u, v, dtm, dt, lab, par, force, cols, zb, ends, far,
-    u2, v2,
-    col, col_lab, col_dt, col_f,
-):
+        hi, lo, other = NEW_HI + 16 * c, NEW_LO + 16 * c, theirs[16 * c : 16 * c + 16, :]
+        left.append(jnp.where(right_side, ends[hi : hi + 16, :], other))
+        right.append(jnp.where(right_side, other, ends[lo : lo + 16, :]))
+    side = jnp.where(right_side, -1.0, 1.0)
+    return column_part([fields[at, i] for i in range(4)], side, left, right)
+
+
+def second_step(u, v, dtm, force, fields, ends, far, u2, v2, col_f):
     even = on_even()
-    forces = second_column(
-        blocks, layers, jnp.logical_not(even), far[0:32, :], dt, lab, par, cols, zb, ends, col, col_lab, col_dt
-    )
+    forces = second_column(0, fields, ends, far)
     for c in range(3):
         col_f[0, c] = jnp.where(even, forces[c], 0.0)
         col_f[1, c] = jnp.where(even, 0.0, forces[c])
@@ -656,19 +657,37 @@
 
 
 def second_contact(
-    blocks, layers,
-    u_in, v_in, dtm, lists, mate, far, opp, dt, lab, par, cols, zb, ends,
-    u2, v2,
-    u, v, col, col_lab, col_dt, col_f, sems,
+    layers, u_in, v_in, dtm, lists, mate, far, opp, fields, ends, u2, v2, u, v, col_f, sems
 ):
     even = on_even()
     on_face = lax.axis_index("layer") == layers // 2
-    forces = second_column(
-        blocks, layers, even, opp[0:32, :], dt, lab, par, cols, zb, ends, col, col_lab, col_dt
-    )
+    forces = second_column(1, fields, ends, opp)
     for c in range(3):
         col_f[0, c] = jnp.where(even, 0.0, forces[c])
         col_f[1, c] = jnp.where(even, forces[c], 0.0)
+
+    def update(z, extra):
+        e = z + 1
+        rate = dtm[e]
+        for c in range(3):
+            pull = with_columns(jnp.zeros((16, 256), F32), col_f[0, c, e : e + 1, :], col_f[1, c, e : e + 1, :])
+            if extra is not None:
+                pull = pull - jnp.where(on_face, extra[c], 0.0)
+            change = rate * pull
+            v[c, z] = v_in[c, z] - change
+            u[c, z] = u_in[c, z] - DT * change
+
+    def copy_out(first, last):
+        for src, dst in ((u, u2), (v, v2)):
+            copy = pltpu.make_async_copy(src.at[:, first:last], dst.at[:, first:last], sems.at[len(copies)])
+            copy.start()
+            copies.append(copy)
+
+    copies = []
+    for first in (0, 5):
+        for z in range(first, first + 3):
+            update(z, None)
+        copy_out(first, first + 3)
     sol_y, sol_x = one_hots(lists[0:1, :])
     land_y, land_x = one_hots(lists[6:7, :])
 
@@ -690,19 +709,9 @@
     on_bump = lists[2:3, :] * (far_pad - lists[3:6, :])
     on_pad = lists[7:8, :] * (far_bump - lists[8:11, :])
     extra = (scatter(on_pad, land_y, land_x), scatter(on_bump, sol_y, sol_x))
-    for z in (0, 1, 2, 5, 6, 7, 3, 4):
-        e = z + 1
-        rate = dtm[e]
-        for c in range(3):
-            pull = with_columns(jnp.zeros((16, 256), F32), col_f[0, c, e : e + 1, :], col_f[1, c, e : e + 1, :])
-            if z in (3, 4):
-                pull = pull - jnp.where(on_face, extra[z - 3][c], 0.0)
-            change = rate * pull
-            v[c, z] = v_in[c, z] - change
-            u[c, z] = u_in[c, z] - DT * change
-    copies = [pltpu.make_async_copy(src, dst, sems.at[i]) for i, (src, dst) in enumerate(((u, u2), (v, v2)))]
-    for copy in copies:
-        copy.start()
+    for z in (3, 4):
+        update(z, extra[z - 3])
+    copy_out(3, 5)
     for copy in copies:
         copy.wait()
 
@@ -799,36 +808,30 @@
     across = [(s, s + 1) for s in range(1, blocks - 1, 2)] + [(s, s - 1) for s in range(2, blocks, 2)]
     cross = call(pack_new_cross, [VM] * 3, [(NEW_CROSS_ROWS, 256)], [], "pack_new_cross", 100_000)(ends, values, mate)[0]
     far = lax.ppermute(cross, "plane", across)
-    force = call(
-        functools.partial(second_block, layers),
-        [VM] * 3 + [SM, VM],
-        [(3, 10, 16, 256)],
-        [(9, 16, 256), (9, 16, 256)] + modes,
+    force, fields = call(
+        functools.partial(second_block, blocks, layers),
+        [VM] * 3 + [SM] + [VM] * 2,
+        [(3, 10, 16, 256), (2, 4, 16, 256)],
+        [(9, 16, 256), (9, 16, 256), (2, 16, 256)] + modes,
         "second_block",
         50_000_000,
-    )(u1, dt, lab, par, zb)[0]
+    )(u1, dt, lab, par, zb, cols)
     far, force = lax.optimization_barrier((far, force))
     last = call(pack_last, [VM] * 2, [(NEW_CROSS_ROWS, 256)], [], "pack_last", 100_000)(ends, far)[0]
     opp = lax.ppermute(last, "plane", swaps)
-    column = [(2, 3, 16, 256), (16, 256), (16, 256)]
     u2, v2 = call(
-        functools.partial(second_step, blocks, layers),
-        [VM] * 5 + [SM] + [VM] * 5,
-        [(3, 8, 16, 256)] * 2,
-        column + [(2, 3, 16, 256)],
-        "second_step",
-        20_000_000,
-    )(u1, v1, dtm, dt, lab, par, force, cols, zb, ends, far)
+        second_step, [VM] * 7, [(3, 8, 16, 256)] * 2, [(2, 3, 16, 256)], "second_step", 20_000_000
+    )(u1, v1, dtm, force, fields, ends, far)
     return tuple(
         call(
-            functools.partial(second_contact, blocks, layers),
-            [VM] * 9 + [SM] + [VM] * 3,
+            functools.partial(second_contact, layers),
+            [VM] * 9,
             [(3, 8, 16, 256)] * 2,
-            [(3, 8, 16, 256)] * 2 + column + [(2, 3, 16, 256), pltpu.SemaphoreType.DMA((2,))],
+            [(3, 8, 16, 256)] * 2 + [(2, 3, 16, 256), pltpu.SemaphoreType.DMA((6,))],
             "second_contact",
             10_000_000,
             out_spec=HBM,
-        )(u2, v2, dtm, lists, mate, far, opp, dt, lab, par, cols, zb, ends)
+        )(u2, v2, dtm, lists, mate, far, opp, fields, ends)
     )
 
 

time: 44.7 us -> 44.1 us (0.987)
  Pallas kernels: 11.3 us -> 10.1 us
  waiting for transfers between devices: 3.3 us -> 3.8 us
    pallas_call x3, Pallas kernels: 5.07 us -> 3.85 us  [the longest x1 2.15 us: local(): call(functools.partial(second_block, blocks, layers), [VM] * 3 + [SM] + [...]
    ppermute x1, waiting for transfers between devices: 0.01 us -> 0.5 us  [local(): opp = lax.ppermute(last, 'plane', swaps)]
  transfers between devices with their start and end apart: 8 -> 8, of which waited for: 2 -> 3; matrix products, arithmetic and copies ran while one was open for 0% -> 0% of each run, Pallas kernels for 17% -> 16%
where the time goes in v7:
time: 44.1 us; the launch traced here: 43.8 us
  starting transfers between devices  28.1 us (64%)
  Pallas kernels  10.1 us (23%)
  waiting for transfers between devices  3.8 us (9%)
  local copies, waits for them, and re-layouts  0.93 us (2%)
  between operations  0.89 us (2%)
    ppermute x1, starting transfers between devices, local(): opp = lax.ppermute(last, 'plane', swaps)  8.42 us
    ppermute x2, starting transfers between devices, along_layer(): return lax.ppermute(value, 'layer', pairs)  6.54 us
    ppermute x1, starting transfers between devices, local(): far = lax.ppermute(cross, 'plane', across)  4.77 us
    ppermute x1, starting transfers between devices, local(): far = lax.ppermute(cross, 'plane', crossings)  4.32 us
    ppermute x2, waiting for transfers between devices, along_layer(): return lax.ppermute(value, 'layer', pairs)  3.19 us
    ppermute x1, starting transfers between devices, local(): near = lax.ppermute(own, 'plane', swaps)  2.71 us
    pallas_call x1, Pallas kernels, local(): call(functools.partial(second_block, blocks, layers), [VM] * 3 + [SM] + [...  2.15 us
    pallas_call x1, Pallas kernels, local(): call(functools.partial(pack_export, blocks, layers), [HBM] * 7, [(EXPORT_...  1.87 us
  transfers between devices with their start and end apart: 8, of which 3 were waited for; matrix products, arithmetic and copies ran while one was open for 0% of the time, Pallas kernels for 16%

profile of v7, /device:TPU:259, one launch (start us, length us, event | category | flops | bytes accessed | tf_op | source)
XLA Modules:
  0.0 43.8 jit_solution(15799907967393020099)
XLA Ops:
  0.6 1.9 %pack_export.1.src = f32[136,256]{1,0:T(8,128)} custom-call(f32[3,8,16,256]{3,2,1,0:T(8,128)} %u.7, f32[8,16,256]{2,1,0:T(8,128)} %dt.7, s32[8,16,256]{2,1,0:T(8,128)} %lab.7, s32[5,1,128]{2,1,0:T(1,128)} %bitcast.3, s32[5,1,128]{2,1,0:T(1,128)} %bitcast.4, f32[5,1,128]{2,1,0:T(1,128)} %bitcast.5, s32[1,5]{1,0:T(1,128)} %tally_hbm.1), custom_call_target="tpu_custom_call" | custom-call | flops 100000 | bytes 4000 | tf_op jit(solution)/shard_map/pack_export/pallas_call | solution.py:747
  2.5 0.0 copy-start
  2.5 2.7 %collective-permute-start = (f32[136,256]{1,0:T(8,128)}, f32[136,256]{1,0:T(8,128)S(1)}, u32[]{:S(2)}, u32[]{:S(2)}) collective-permute-start(f32[136,256]{1,0:T(8,128)} %pack_export.1.src), channel_id=1, source_target_pairs={{0,4},{4,0},{8,12},{12,8},{16,20},{20,16},{24,28},{28,24},{32,36},... | collective-permute-start | bytes 417800 | tf_op jit(solution)/shard_map/ppermute | solution.py:759
  5.3 0.0 copy-start.4
  5.3 0.9 %copy-done.4 = f32[136,256]{1,0:T(8,128)S(1)} copy-done((f32[136,256]{1,0:T(8,128)S(1)}, f32[136,256]{1,0:T(8,128)}, u32[]{:S(2)}) %copy-start.4) | copy-done | bytes 139288
  6.2 0.2 stage.1.own
  6.3 0.1 collective-permute-done.mate.near
  6.5 0.0 copy-start.1
  6.5 4.3 %collective-permute-start.1 = (f32[144,256]{1,0:T(8,128)S(1)}, f32[144,256]{1,0:T(8,128)S(1)}, u32[]{:S(2)}, u32[]{:S(2)}) collective-permute-start(f32[144,256]{1,0:T(8,128)S(1)} %get-tuple-element.34), channel_id=1, source_target_pairs={{0,8},{8,16},{12,4},{16,24},{20,12},{24,32},{28,20},{32,40},{36,28... | collective-permute-start | bytes 442376 | tf_op jit(solution)/shard_map/ppermute | solution.py:762
  10.8 0.7 %collective-permute-start.4 = (f32[232,256]{1,0:T(8,128)S(1)}, f32[232,256]{1,0:T(8,128)S(1)}, u32[]{:S(2)}, u32[]{:S(2)}) collective-permute-start(f32[232,256]{1,0:T(8,128)S(1)} %get-tuple-element.45), channel_id=1, source_target_pairs={{10,2},{18,10},{6,14},{26,18},{14,22},{34,26},{22,30},{42,34},{30,... | collective-permute-start | bytes 712712 | tf_op jit(solution)/shard_map/ppermute | solution.py:764
  11.5 1.8 %first_block.1 = (f32[3,8,16,256]{3,2,1,0:T(8,128)S(1)}, f32[8,16,256]{2,1,0:T(8,128)S(1)}) custom-call(f32[3,8,16,256]{3,2,1,0:T(8,128)S(1)} %copy-done, f32[8,16,256]{2,1,0:T(8,128)S(1)} %copy-done.2, s32[8,16,256]{2,1,0:T(8,128)S(1)} %copy-done.3, f32[4,4]{1,0:T(4,128)S(1)} %copy-done.5), custom_call_target="tpu_custom_call" | custom-call | flops 50000000 | bytes 2000000 | tf_op jit(solution)/shard_map/first_block/pallas_call | solution.py:767
  13.3 0.1 pack_layer.1
  13.4 4.6 %collective-permute-start.2 = (f32[224,256]{1,0:T(8,128)S(1)}, f32[224,256]{1,0:T(8,128)S(1)}, u32[]{:S(2)}, u32[]{:S(2)}) collective-permute-start(f32[224,256]{1,0:T(8,128)S(1)} %get-tuple-element.39), channel_id=1, source_target_pairs={{0,1},{1,2},{2,3},{4,5},{5,6},{6,7},{8,9},{9,10},{10,11},{12,13},{... | collective-permute-start | bytes 688136 | tf_op jit(solution)/shard_map/ppermute | solution.py:745
  18.0 1.9 %collective-permute-start.3 = (f32[192,256]{1,0:T(8,128)S(1)}, f32[192,256]{1,0:T(8,128)S(1)}, u32[]{:S(2)}, u32[]{:S(2)}) collective-permute-start(f32[192,256]{1,0:T(8,128)S(1)} %get-tuple-element.40), channel_id=1, source_target_pairs={{1,0},{2,1},{3,2},{5,4},{6,5},{7,6},{9,8},{10,9},{11,10},{13,12},{... | collective-permute-start | bytes 589832 | tf_op jit(solution)/shard_map/ppermute | solution.py:745
  19.9 0.9 %first_inner.1 = (f32[3,6,16,256]{3,2,1,0:T(8,128)S(1)}, f32[3,6,16,256]{3,2,1,0:T(8,128)S(1)}, f32[6,16,256]{2,1,0:T(8,128)S(1)}, f32[2,3,8,256]{3,2,1,0:T(8,128)S(1)}, f32[2,8,256]{2,1,0:T(8,128)S(1)}) custom-call(f32[3,8,16,256]{3,2,1,0:T(8,128)S(1)} %copy-done, f32[3,8,16,256]{3,2,1,0:T(8,128)S(1)} %copy-done.1, f32[4,4]{1,0:T(4,128)S(1)} %copy-done.5, ...), custom_call_target="tpu_custom_call" | custom-call | flops 1000 | bytes 40 | tf_op jit(solution)/shard_map/first_inner/pallas_call | solution.py:780
  20.9 0.7 %collective-permute-start.5 = (f32[24,256]{1,0:T(8,128)S(1)}, f32[24,256]{1,0:T(8,128)S(1)}, u32[]{:S(2)}, u32[]{:S(2)}) collective-permute-start(f32[24,256]{1,0:T(8,128)S(1)} %get-tuple-element.58.values), channel_id=1, source_target_pairs={{2,6},{6,2},{10,14},{14,10},{18,22},{22,18},{26,30},{30,26},{34,38... | collective-permute-start | bytes 73736 | tf_op jit(solution)/shard_map/ppermute | solution.py:797
  21.5 3.2 %collective-permute-done.3.za = f32[192,256]{1,0:T(8,128)S(1)} collective-permute-done((f32[192,256]{1,0:T(8,128)S(1)}, f32[192,256]{1,0:T(8,128)S(1)}, u32[]{:S(2)}, u32[]{:S(2)}) %collective-permute-start.3) | collective-permute-done | bytes 196640 | tf_op jit(solution)/shard_map/ppermute | solution.py:745
  24.7 1.4 %first_step.1 = (f32[3,10,16,256]{3,2,1,0:T(8,128)S(1)}, f32[3,10,16,256]{3,2,1,0:T(8,128)S(1)}, f32[10,16,256]{2,1,0:T(8,128)S(1)}, f32[96,256]{1,0:T(8,128)S(1)}) custom-call(f32[3,8,16,256]{3,2,1,0:T(8,128)S(1)} %copy-done, f32[3,8,16,256]{3,2,1,0:T(8,128)S(1)} %copy-done.1, f32[8,16,256]{2,1,0:T(8,128)S(1)} %copy-done.2, s32[8,16,256]{2,1,0:T(8,128)S(1)} %copy-done.3, ...), custom_call_target="tpu_custom_call" | custom-call | flops 20000000 | bytes 800000 | tf_op jit(solution)/shard_map/first_step/pallas_call | solution.py:800
  26.2 4.8 %collective-permute-start.6 = (f32[64,256]{1,0:T(8,128)S(1)}, f32[64,256]{1,0:T(8,128)S(1)}, u32[]{:S(2)}, u32[]{:S(2)}) collective-permute-start(f32[64,256]{1,0:T(8,128)S(1)} %pack_new_cross.1), channel_id=1, source_target_pairs={{4,8},{12,16},{20,24},{28,32},{36,40},{44,48},{52,56},{60,64},{68,... | collective-permute-start | bytes 196616 | tf_op jit(solution)/shard_map/ppermute | solution.py:810
  31.0 2.2 %second_block.1 = (f32[3,10,16,256]{3,2,1,0:T(8,128)S(1)}, f32[2,4,16,256]{3,2,1,0:T(8,128)S(1)}) custom-call(f32[3,10,16,256]{3,2,1,0:T(8,128)S(1)} %get-tuple-element.54.u, f32[8,16,256]{2,1,0:T(8,128)S(1)} %copy-done.2, s32[8,16,256]{2,1,0:T(8,128)S(1)} %copy-done.3, f32[4,4]{1,0:T(4,128)S(1)} %copy-done.5, f32[224,256]{1,0:T(8,128)S(1)} %collective-permute-done.2.zb, ...), custom_call_target="tpu_custom_call" | custom-call | flops 50000000 | bytes 2000000 | tf_op jit(solution)/shard_map/second_block/pallas_call | solution.py:811
  33.2 8.4 %collective-permute-start.7 = (f32[64,256]{1,0:T(8,128)S(1)}, f32[64,256]{1,0:T(8,128)S(1)}, u32[]{:S(2)}, u32[]{:S(2)}) collective-permute-start(f32[64,256]{1,0:T(8,128)S(1)} %pack_last.1), channel_id=1, source_target_pairs={{0,4},{4,0},{8,12},{12,8},{16,20},{20,16},{24,28},{28,24},{32,36},... | collective-permute-start | bytes 196616 | tf_op jit(solution)/shard_map/ppermute | solution.py:821
  41.6 0.4 second_step.1
  42.0 0.5 %collective-permute-done.7.opp = f32[64,256]{1,0:T(8,128)S(1)} collective-permute-done((f32[64,256]{1,0:T(8,128)S(1)}, f32[64,256]{1,0:T(8,128)S(1)}, u32[]{:S(2)}, u32[]{:S(2)}) %collective-permute-start.7) | collective-permute-done | bytes 65568 | tf_op jit(solution)/shard_map/ppermute | solution.py:821
  42.5 1.3 %second_contact.1 = (f32[3,8,16,256]{3,2,1,0:T(8,128)}, f32[3,8,16,256]{3,2,1,0:T(8,128)}) custom-call(f32[3,8,16,256]{3,2,1,0:T(8,128)S(1)} %get-tuple-element.63.u_in, f32[3,8,16,256]{3,2,1,0:T(8,128)S(1)} %get-tuple-element.64.v_in, f32[10,16,256]{2,1,0:T(8,128)S(1)} %get-tuple-element.56.dtm, f32[16,640]{1,0:T(8,128)S(1)} %get-tuple-element.65.lists, ...), custom_call_target="tpu_custom_call" | custom-call | flops 10000000 | bytes 400000 | tf_op jit(solution)/shard_map/second_contact/pallas_call | solution.py:826
  (17 shorter events, 0.1 us)
Async XLA Ops:
  0.6 10.9 %copy-start.3 = (s32[8,16,256]{2,1,0:T(8,128)S(1)}, s32[8,16,256]{2,1,0:T(8,128)}, u32[]{:S(2)}) copy-start(s32[8,16,256]{2,1,0:T(8,128)} %lab.7) | copy-start | bytes 393220
  2.5 9.0 %copy-start = (f32[3,8,16,256]{3,2,1,0:T(8,128)S(1)}, f32[3,8,16,256]{3,2,1,0:T(8,128)}, u32[]{:S(2)}) copy-start(f32[3,8,16,256]{3,2,1,0:T(8,128)} %u.7) | copy-start | bytes 1179652
  2.5 3.9 %collective-permute-start = (f32[136,256]{1,0:T(8,128)}, f32[136,256]{1,0:T(8,128)S(1)}, u32[]{:S(2)}, u32[]{:S(2)}) collective-permute-start(f32[136,256]{1,0:T(8,128)} %pack_export.1.src), channel_id=1, source_target_pairs={{0,4},{4,0},{8,12},{12,8},{16,20},{20,16},{24,28},{28,24},{32,36},... | collective-permute-start | bytes 417800 | tf_op jit(solution)/shard_map/ppermute | solution.py:759
  5.3 0.9 %copy-start.4 = (f32[136,256]{1,0:T(8,128)S(1)}, f32[136,256]{1,0:T(8,128)}, u32[]{:S(2)}) copy-start(f32[136,256]{1,0:T(8,128)} %pack_export.1.src) | copy-start | bytes 417796
  6.3 5.2 %copy-start.2 = (f32[8,16,256]{2,1,0:T(8,128)S(1)}, f32[8,16,256]{2,1,0:T(8,128)}, u32[]{:S(2)}) copy-start(f32[8,16,256]{2,1,0:T(8,128)} %dt.7) | copy-start | bytes 393220
  6.4 5.1 %copy-start.5 = (f32[4,4]{1,0:T(4,128)S(1)}, f32[4,4]{1,0:T(4,128)}, u32[]{:S(2)}) copy-start(f32[4,4]{1,0:T(4,128)} %par.7) | copy-start | bytes 196
  6.5 6.9 %copy-start.1 = (f32[3,8,16,256]{3,2,1,0:T(8,128)S(1)}, f32[3,8,16,256]{3,2,1,0:T(8,128)}, u32[]{:S(2)}) copy-start(f32[3,8,16,256]{3,2,1,0:T(8,128)} %v.5) | copy-start | bytes 1179652
  6.5 6.8 %collective-permute-start.1 = (f32[144,256]{1,0:T(8,128)S(1)}, f32[144,256]{1,0:T(8,128)S(1)}, u32[]{:S(2)}, u32[]{:S(2)}) collective-permute-start(f32[144,256]{1,0:T(8,128)S(1)} %get-tuple-element.34), channel_id=1, source_target_pairs={{0,8},{8,16},{12,4},{16,24},{20,12},{24,32},{28,20},{32,40},{36,28... | collective-permute-start | bytes 442376 | tf_op jit(solution)/shard_map/ppermute | solution.py:762
  10.8 10.0 %collective-permute-start.4 = (f32[232,256]{1,0:T(8,128)S(1)}, f32[232,256]{1,0:T(8,128)S(1)}, u32[]{:S(2)}, u32[]{:S(2)}) collective-permute-start(f32[232,256]{1,0:T(8,128)S(1)} %get-tuple-element.45), channel_id=1, source_target_pairs={{10,2},{18,10},{6,14},{26,18},{14,22},{34,26},{22,30},{42,34},{30,... | collective-permute-start | bytes 712712 | tf_op jit(solution)/shard_map/ppermute | solution.py:764
  13.4 11.3 %collective-permute-start.2 = (f32[224,256]{1,0:T(8,128)S(1)}, f32[224,256]{1,0:T(8,128)S(1)}, u32[]{:S(2)}, u32[]{:S(2)}) collective-permute-start(f32[224,256]{1,0:T(8,128)S(1)} %get-tuple-element.39), channel_id=1, source_target_pairs={{0,1},{1,2},{2,3},{4,5},{5,6},{6,7},{8,9},{9,10},{10,11},{12,13},{... | collective-permute-start | bytes 688136 | tf_op jit(solution)/shard_map/ppermute | solution.py:745
  18.0 6.7 %collective-permute-start.3 = (f32[192,256]{1,0:T(8,128)S(1)}, f32[192,256]{1,0:T(8,128)S(1)}, u32[]{:S(2)}, u32[]{:S(2)}) collective-permute-start(f32[192,256]{1,0:T(8,128)S(1)} %get-tuple-element.40), channel_id=1, source_target_pairs={{1,0},{2,1},{3,2},{5,4},{6,5},{7,6},{9,8},{10,9},{11,10},{13,12},{... | collective-permute-start | bytes 589832 | tf_op jit(solution)/shard_map/ppermute | solution.py:745
  20.9 5.3 %collective-permute-start.5 = (f32[24,256]{1,0:T(8,128)S(1)}, f32[24,256]{1,0:T(8,128)S(1)}, u32[]{:S(2)}, u32[]{:S(2)}) collective-permute-start(f32[24,256]{1,0:T(8,128)S(1)} %get-tuple-element.58.values), channel_id=1, source_target_pairs={{2,6},{6,2},{10,14},{14,10},{18,22},{22,18},{26,30},{30,26},{34,38... | collective-permute-start | bytes 73736 | tf_op jit(solution)/shard_map/ppermute | solution.py:797
  26.2 6.9 %collective-permute-start.6 = (f32[64,256]{1,0:T(8,128)S(1)}, f32[64,256]{1,0:T(8,128)S(1)}, u32[]{:S(2)}, u32[]{:S(2)}) collective-permute-start(f32[64,256]{1,0:T(8,128)S(1)} %pack_new_cross.1), channel_id=1, source_target_pairs={{4,8},{12,16},{20,24},{28,32},{36,40},{44,48},{52,56},{60,64},{68,... | collective-permute-start | bytes 196616 | tf_op jit(solution)/shard_map/ppermute | solution.py:810
  33.2 9.3 %collective-permute-start.7 = (f32[64,256]{1,0:T(8,128)S(1)}, f32[64,256]{1,0:T(8,128)S(1)}, u32[]{:S(2)}, u32[]{:S(2)}) collective-permute-start(f32[64,256]{1,0:T(8,128)S(1)} %pack_last.1), channel_id=1, source_target_pairs={{0,4},{4,0},{8,12},{12,8},{16,20},{20,16},{24,28},{28,24},{32,36},... | collective-permute-start | bytes 196616 | tf_op jit(solution)/shard_map/ppermute | solution.py:821

commit v8 on v7

--- a/solution.py
+++ b/solution.py
@@ -640,7 +640,30 @@
     return column_part([fields[at, i] for i in range(4)], side, left, right)
 
 
-def second_step(u, v, dtm, force, fields, ends, far, u2, v2, col_f):
+def second_ties(lists, part, places):
+    def values(i):
+        half = slice(128 * (i % 2), 128 * (i % 2) + 128)
+        own_row = (3, 4, 5, 8, 9, 10)[i]
+        parts = [
+            lists[own_row : own_row + 1, 256:384] if place is None
+            else place[0][place[1] + i // 2 : place[1] + i // 2 + 1, half]
+            for place in places
+        ]
+        return jnp.concatenate(parts, axis=1) if len(parts) > 1 else parts[0]
+
+    sol_y, sol_x = one_hots(lists[0:1, part])
+    land_y, land_x = one_hots(lists[6:7, part])
+    far_bump = jnp.concatenate([values(i) for i in range(3)], axis=0)
+    far_pad = jnp.concatenate([values(i) for i in range(3, 6)], axis=0)
+    on_bump = lists[2:3, part] * (far_pad - lists[3:6, part])
+    on_pad = lists[7:8, part] * (far_bump - lists[8:11, part])
+    return scatter(on_pad, land_y, land_x), scatter(on_bump, sol_y, sol_x)
+
+
+def second_step(layers, u, v, dtm, force, fields, ends, far, lists, mate, u2, v2, col_f):
+    on_face = lax.axis_index("layer") == layers // 2
+    places = ((mate, 4 * NEAR), (far, CROSS_MATE), None, (far, CROSS_OWN))
+    extra = second_ties(lists, slice(0, 512), places)
     even = on_even()
     forces = second_column(0, fields, ends, far)
     for c in range(3):
@@ -651,13 +674,15 @@
         rate = dtm[e]
         for c in range(3):
             pull = with_columns(force[c, e], col_f[0, c, e : e + 1, :], col_f[1, c, e : e + 1, :])
+            if z in (3, 4):
+                pull = pull - jnp.where(on_face, extra[z - 3][c], 0.0)
             speed = v[c, e] - rate * pull
             v2[c, z] = speed
             u2[c, z] = u[c, e] + DT * speed
 
 
 def second_contact(
-    layers, u_in, v_in, dtm, lists, mate, far, opp, fields, ends, u2, v2, u, v, col_f, sems
+    layers, u_in, v_in, dtm, lists, opp, fields, ends, u2, v2, u, v, col_f, sems
 ):
     even = on_even()
     on_face = lax.axis_index("layer") == layers // 2
@@ -688,27 +713,7 @@
         for z in range(first, first + 3):
             update(z, None)
         copy_out(first, first + 3)
-    sol_y, sol_x = one_hots(lists[0:1, :])
-    land_y, land_x = one_hots(lists[6:7, :])
-
-    def values(i):
-        half = slice(128 * (i % 2), 128 * (i % 2) + 128)
-        own_row = (3, 4, 5, 8, 9, 10)[i]
-        places = (
-            (mate, 4 * NEAR), (far, CROSS_MATE), None, (far, CROSS_OWN), (opp, CROSS_ON)
-        )
-        parts = [
-            lists[own_row : own_row + 1, 256:384] if place is None
-            else place[0][place[1] + i // 2 : place[1] + i // 2 + 1, half]
-            for place in places
-        ]
-        return jnp.concatenate(parts, axis=1)
-
-    far_bump = jnp.concatenate([values(i) for i in range(3)], axis=0)
-    far_pad = jnp.concatenate([values(i) for i in range(3, 6)], axis=0)
-    on_bump = lists[2:3, :] * (far_pad - lists[3:6, :])
-    on_pad = lists[7:8, :] * (far_bump - lists[8:11, :])
-    extra = (scatter(on_pad, land_y, land_x), scatter(on_bump, sol_y, sol_x))
+    extra = second_ties(lists, slice(512, 640), ((opp, CROSS_ON),))
     for z in (3, 4):
         update(z, extra[z - 3])
     copy_out(3, 5)
@@ -820,18 +825,18 @@
     last = call(pack_last, [VM] * 2, [(NEW_CROSS_ROWS, 256)], [], "pack_last", 100_000)(ends, far)[0]
     opp = lax.ppermute(last, "plane", swaps)
     u2, v2 = call(
-        second_step, [VM] * 7, [(3, 8, 16, 256)] * 2, [(2, 3, 16, 256)], "second_step", 20_000_000
-    )(u1, v1, dtm, force, fields, ends, far)
+        functools.partial(second_step, layers), [VM] * 9, [(3, 8, 16, 256)] * 2, [(2, 3, 16, 256)], "second_step", 20_000_000
+    )(u1, v1, dtm, force, fields, ends, far, lists, mate)
     return tuple(
         call(
             functools.partial(second_contact, layers),
-            [VM] * 9,
+            [VM] * 7,
             [(3, 8, 16, 256)] * 2,
             [(3, 8, 16, 256)] * 2 + [(2, 3, 16, 256), pltpu.SemaphoreType.DMA((6,))],
             "second_contact",
             10_000_000,
             out_spec=HBM,
-        )(u2, v2, dtm, lists, mate, far, opp, fields, ends)
+        )(u2, v2, dtm, lists, opp, fields, ends)
     )
 
 

time: 44.1 us -> 44.1 us (level)
  no operation moved by 1% of the time
where the time goes in v8:
time: 44.1 us; the launch traced here: 43.7 us
  starting transfers between devices  28.1 us (64%)
  Pallas kernels  10.1 us (23%)
  waiting for transfers between devices  3.72 us (8%)
  local copies, waits for them, and re-layouts  0.93 us (2%)
  between operations  0.89 us (2%)
    ppermute x1, starting transfers between devices, local(): opp = lax.ppermute(last, 'plane', swaps)  8.41 us
    ppermute x2, starting transfers between devices, along_layer(): return lax.ppermute(value, 'layer', pairs)  6.54 us
    ppermute x1, starting transfers between devices, local(): far = lax.ppermute(cross, 'plane', across)  4.77 us
    ppermute x1, starting transfers between devices, local(): far = lax.ppermute(cross, 'plane', crossings)  4.32 us
    ppermute x2, waiting for transfers between devices, along_layer(): return lax.ppermute(value, 'layer', pairs)  3.19 us
    ppermute x1, starting transfers between devices, local(): near = lax.ppermute(own, 'plane', swaps)  2.71 us
    pallas_call x1, Pallas kernels, local(): call(functools.partial(second_block, blocks, layers), [VM] * 3 + [SM] + [...  2.15 us
    pallas_call x1, Pallas kernels, local(): call(functools.partial(pack_export, blocks, layers), [HBM] * 7, [(EXPORT_...  1.87 us
  transfers between devices with their start and end apart: 8, of which 3 were waited for; matrix products, arithmetic and copies ran while one was open for 0% of the time, Pallas kernels for 16%

profile of v8, /device:TPU:259, one launch (start us, length us, event | category | flops | bytes accessed | tf_op | source)
XLA Modules:
  0.0 43.7 jit_solution(5840146294100991863)
XLA Ops:
  0.6 1.9 %pack_export.1.src = f32[136,256]{1,0:T(8,128)} custom-call(f32[3,8,16,256]{3,2,1,0:T(8,128)} %u.7, f32[8,16,256]{2,1,0:T(8,128)} %dt.7, s32[8,16,256]{2,1,0:T(8,128)} %lab.7, s32[5,1,128]{2,1,0:T(1,128)} %bitcast.3, s32[5,1,128]{2,1,0:T(1,128)} %bitcast.4, f32[5,1,128]{2,1,0:T(1,128)} %bitcast.5, s32[1,5]{1,0:T(1,128)} %tally_hbm.1), custom_call_target="tpu_custom_call" | custom-call | flops 100000 | bytes 4000 | tf_op jit(solution)/shard_map/pack_export/pallas_call | solution.py:752
  2.5 0.0 copy-start
  2.5 2.7 %collective-permute-start = (f32[136,256]{1,0:T(8,128)}, f32[136,256]{1,0:T(8,128)S(1)}, u32[]{:S(2)}, u32[]{:S(2)}) collective-permute-start(f32[136,256]{1,0:T(8,128)} %pack_export.1.src), channel_id=1, source_target_pairs={{0,4},{4,0},{8,12},{12,8},{16,20},{20,16},{24,28},{28,24},{32,36},... | collective-permute-start | bytes 417800 | tf_op jit(solution)/shard_map/ppermute | solution.py:764
  5.3 0.0 copy-start.4
  5.3 0.9 %copy-done.4 = f32[136,256]{1,0:T(8,128)S(1)} copy-done((f32[136,256]{1,0:T(8,128)S(1)}, f32[136,256]{1,0:T(8,128)}, u32[]{:S(2)}) %copy-start.4) | copy-done | bytes 139288
  6.2 0.2 stage.1.own
  6.3 0.0 copy-start.2
  6.3 0.1 collective-permute-done.mate.near
  6.5 4.3 %collective-permute-start.1 = (f32[144,256]{1,0:T(8,128)S(1)}, f32[144,256]{1,0:T(8,128)S(1)}, u32[]{:S(2)}, u32[]{:S(2)}) collective-permute-start(f32[144,256]{1,0:T(8,128)S(1)} %get-tuple-element.34), channel_id=1, source_target_pairs={{0,8},{8,16},{12,4},{16,24},{20,12},{24,32},{28,20},{32,40},{36,28... | collective-permute-start | bytes 442376 | tf_op jit(solution)/shard_map/ppermute | solution.py:767
  10.8 0.7 %collective-permute-start.4 = (f32[232,256]{1,0:T(8,128)S(1)}, f32[232,256]{1,0:T(8,128)S(1)}, u32[]{:S(2)}, u32[]{:S(2)}) collective-permute-start(f32[232,256]{1,0:T(8,128)S(1)} %get-tuple-element.45), channel_id=1, source_target_pairs={{10,2},{18,10},{6,14},{26,18},{14,22},{34,26},{22,30},{42,34},{30,... | collective-permute-start | bytes 712712 | tf_op jit(solution)/shard_map/ppermute | solution.py:769
  11.5 1.8 %first_block.1 = (f32[3,8,16,256]{3,2,1,0:T(8,128)S(1)}, f32[8,16,256]{2,1,0:T(8,128)S(1)}) custom-call(f32[3,8,16,256]{3,2,1,0:T(8,128)S(1)} %copy-done, f32[8,16,256]{2,1,0:T(8,128)S(1)} %copy-done.2, s32[8,16,256]{2,1,0:T(8,128)S(1)} %copy-done.3, f32[4,4]{1,0:T(4,128)S(1)} %copy-done.5), custom_call_target="tpu_custom_call" | custom-call | flops 50000000 | bytes 2000000 | tf_op jit(solution)/shard_map/first_block/pallas_call | solution.py:772
  13.3 0.1 pack_layer.1
  13.4 4.6 %collective-permute-start.2 = (f32[224,256]{1,0:T(8,128)S(1)}, f32[224,256]{1,0:T(8,128)S(1)}, u32[]{:S(2)}, u32[]{:S(2)}) collective-permute-start(f32[224,256]{1,0:T(8,128)S(1)} %get-tuple-element.39), channel_id=1, source_target_pairs={{0,1},{1,2},{2,3},{4,5},{5,6},{6,7},{8,9},{9,10},{10,11},{12,13},{... | collective-permute-start | bytes 688136 | tf_op jit(solution)/shard_map/ppermute | solution.py:750
  18.0 1.9 %collective-permute-start.3 = (f32[192,256]{1,0:T(8,128)S(1)}, f32[192,256]{1,0:T(8,128)S(1)}, u32[]{:S(2)}, u32[]{:S(2)}) collective-permute-start(f32[192,256]{1,0:T(8,128)S(1)} %get-tuple-element.40), channel_id=1, source_target_pairs={{1,0},{2,1},{3,2},{5,4},{6,5},{7,6},{9,8},{10,9},{11,10},{13,12},{... | collective-permute-start | bytes 589832 | tf_op jit(solution)/shard_map/ppermute | solution.py:750
  19.9 0.9 %first_inner.1 = (f32[3,6,16,256]{3,2,1,0:T(8,128)S(1)}, f32[3,6,16,256]{3,2,1,0:T(8,128)S(1)}, f32[6,16,256]{2,1,0:T(8,128)S(1)}, f32[2,3,8,256]{3,2,1,0:T(8,128)S(1)}, f32[2,8,256]{2,1,0:T(8,128)S(1)}) custom-call(f32[3,8,16,256]{3,2,1,0:T(8,128)S(1)} %copy-done, f32[3,8,16,256]{3,2,1,0:T(8,128)S(1)} %copy-done.1, f32[4,4]{1,0:T(4,128)S(1)} %copy-done.5, ...), custom_call_target="tpu_custom_call" | custom-call | flops 1000 | bytes 40 | tf_op jit(solution)/shard_map/first_inner/pallas_call | solution.py:785
  20.9 0.7 %collective-permute-start.5 = (f32[24,256]{1,0:T(8,128)S(1)}, f32[24,256]{1,0:T(8,128)S(1)}, u32[]{:S(2)}, u32[]{:S(2)}) collective-permute-start(f32[24,256]{1,0:T(8,128)S(1)} %get-tuple-element.58.values), channel_id=1, source_target_pairs={{2,6},{6,2},{10,14},{14,10},{18,22},{22,18},{26,30},{30,26},{34,38... | collective-permute-start | bytes 73736 | tf_op jit(solution)/shard_map/ppermute | solution.py:802
  21.5 3.2 %collective-permute-done.3.za = f32[192,256]{1,0:T(8,128)S(1)} collective-permute-done((f32[192,256]{1,0:T(8,128)S(1)}, f32[192,256]{1,0:T(8,128)S(1)}, u32[]{:S(2)}, u32[]{:S(2)}) %collective-permute-start.3) | collective-permute-done | bytes 196640 | tf_op jit(solution)/shard_map/ppermute | solution.py:750
  24.7 1.4 %first_step.1 = (f32[3,10,16,256]{3,2,1,0:T(8,128)S(1)}, f32[3,10,16,256]{3,2,1,0:T(8,128)S(1)}, f32[10,16,256]{2,1,0:T(8,128)S(1)}, f32[96,256]{1,0:T(8,128)S(1)}) custom-call(f32[3,8,16,256]{3,2,1,0:T(8,128)S(1)} %copy-done, f32[3,8,16,256]{3,2,1,0:T(8,128)S(1)} %copy-done.1, f32[8,16,256]{2,1,0:T(8,128)S(1)} %copy-done.2, s32[8,16,256]{2,1,0:T(8,128)S(1)} %copy-done.3, ...), custom_call_target="tpu_custom_call" | custom-call | flops 20000000 | bytes 800000 | tf_op jit(solution)/shard_map/first_step/pallas_call | solution.py:805
  26.2 4.8 %collective-permute-start.6 = (f32[64,256]{1,0:T(8,128)S(1)}, f32[64,256]{1,0:T(8,128)S(1)}, u32[]{:S(2)}, u32[]{:S(2)}) collective-permute-start(f32[64,256]{1,0:T(8,128)S(1)} %pack_new_cross.1), channel_id=1, source_target_pairs={{4,8},{12,16},{20,24},{28,32},{36,40},{44,48},{52,56},{60,64},{68,... | collective-permute-start | bytes 196616 | tf_op jit(solution)/shard_map/ppermute | solution.py:815
  31.0 2.2 %second_block.1 = (f32[3,10,16,256]{3,2,1,0:T(8,128)S(1)}, f32[2,4,16,256]{3,2,1,0:T(8,128)S(1)}) custom-call(f32[3,10,16,256]{3,2,1,0:T(8,128)S(1)} %get-tuple-element.54.u, f32[8,16,256]{2,1,0:T(8,128)S(1)} %copy-done.2, s32[8,16,256]{2,1,0:T(8,128)S(1)} %copy-done.3, f32[4,4]{1,0:T(4,128)S(1)} %copy-done.5, f32[224,256]{1,0:T(8,128)S(1)} %collective-permute-done.2.zb, ...), custom_call_target="tpu_custom_call" | custom-call | flops 50000000 | bytes 2000000 | tf_op jit(solution)/shard_map/second_block/pallas_call | solution.py:816
  33.2 8.4 %collective-permute-start.7 = (f32[64,256]{1,0:T(8,128)S(1)}, f32[64,256]{1,0:T(8,128)S(1)}, u32[]{:S(2)}, u32[]{:S(2)}) collective-permute-start(f32[64,256]{1,0:T(8,128)S(1)} %pack_last.1), channel_id=1, source_target_pairs={{0,4},{4,0},{8,12},{12,8},{16,20},{20,16},{24,28},{28,24},{32,36},... | collective-permute-start | bytes 196616 | tf_op jit(solution)/shard_map/ppermute | solution.py:826
  41.6 0.4 %second_step.1 = (f32[3,8,16,256]{3,2,1,0:T(8,128)S(1)}, f32[3,8,16,256]{3,2,1,0:T(8,128)S(1)}) custom-call(f32[3,10,16,256]{3,2,1,0:T(8,128)S(1)} %get-tuple-element.54.u, f32[3,10,16,256]{3,2,1,0:T(8,128)S(1)} %get-tuple-element.55.v, f32[10,16,256]{2,1,0:T(8,128)S(1)} %get-tuple-element.56.dtm, f32[3,10,16,256]{3,2,1,0:T(8,128)S(1)} %get-tuple-element.60.force, ...), custom_call_target="tpu_custom_call" | custom-call | flops 20000000 | bytes 800000 | tf_op jit(solution)/shard_map/second_step/pallas_call | solution.py:827
  42.0 0.4 collective-permute-done.7.opp
  42.5 1.3 %second_contact.1 = (f32[3,8,16,256]{3,2,1,0:T(8,128)}, f32[3,8,16,256]{3,2,1,0:T(8,128)}) custom-call(f32[3,8,16,256]{3,2,1,0:T(8,128)S(1)} %get-tuple-element.64.u_in, f32[3,8,16,256]{3,2,1,0:T(8,128)S(1)} %get-tuple-element.65.v_in, f32[10,16,256]{2,1,0:T(8,128)S(1)} %get-tuple-element.56.dtm, f32[16,640]{1,0:T(8,128)S(1)} %get-tuple-element.63.lists, ...), custom_call_target="tpu_custom_call" | custom-call | flops 10000000 | bytes 400000 | tf_op jit(solution)/shard_map/second_contact/pallas_call | solution.py:831
  (17 shorter events, 0.1 us)
Async XLA Ops:
  0.6 10.9 %copy-start.3 = (s32[8,16,256]{2,1,0:T(8,128)S(1)}, s32[8,16,256]{2,1,0:T(8,128)}, u32[]{:S(2)}) copy-start(s32[8,16,256]{2,1,0:T(8,128)} %lab.7) | copy-start | bytes 393220
  2.5 9.0 %copy-start = (f32[3,8,16,256]{3,2,1,0:T(8,128)S(1)}, f32[3,8,16,256]{3,2,1,0:T(8,128)}, u32[]{:S(2)}) copy-start(f32[3,8,16,256]{3,2,1,0:T(8,128)} %u.7) | copy-start | bytes 1179652
  2.5 3.9 %collective-permute-start = (f32[136,256]{1,0:T(8,128)}, f32[136,256]{1,0:T(8,128)S(1)}, u32[]{:S(2)}, u32[]{:S(2)}) collective-permute-start(f32[136,256]{1,0:T(8,128)} %pack_export.1.src), channel_id=1, source_target_pairs={{0,4},{4,0},{8,12},{12,8},{16,20},{20,16},{24,28},{28,24},{32,36},... | collective-permute-start | bytes 417800 | tf_op jit(solution)/shard_map/ppermute | solution.py:764
  5.3 0.9 %copy-start.4 = (f32[136,256]{1,0:T(8,128)S(1)}, f32[136,256]{1,0:T(8,128)}, u32[]{:S(2)}) copy-start(f32[136,256]{1,0:T(8,128)} %pack_export.1.src) | copy-start | bytes 417796
  6.3 5.2 %copy-start.2 = (f32[8,16,256]{2,1,0:T(8,128)S(1)}, f32[8,16,256]{2,1,0:T(8,128)}, u32[]{:S(2)}) copy-start(f32[8,16,256]{2,1,0:T(8,128)} %dt.7) | copy-start | bytes 393220
  6.4 5.1 %copy-start.5 = (f32[4,4]{1,0:T(4,128)S(1)}, f32[4,4]{1,0:T(4,128)}, u32[]{:S(2)}) copy-start(f32[4,4]{1,0:T(4,128)} %par.7) | copy-start | bytes 196
  6.5 6.9 %copy-start.1 = (f32[3,8,16,256]{3,2,1,0:T(8,128)S(1)}, f32[3,8,16,256]{3,2,1,0:T(8,128)}, u32[]{:S(2)}) copy-start(f32[3,8,16,256]{3,2,1,0:T(8,128)} %v.5) | copy-start | bytes 1179652
  6.5 6.8 %collective-permute-start.1 = (f32[144,256]{1,0:T(8,128)S(1)}, f32[144,256]{1,0:T(8,128)S(1)}, u32[]{:S(2)}, u32[]{:S(2)}) collective-permute-start(f32[144,256]{1,0:T(8,128)S(1)} %get-tuple-element.34), channel_id=1, source_target_pairs={{0,8},{8,16},{12,4},{16,24},{20,12},{24,32},{28,20},{32,40},{36,28... | collective-permute-start | bytes 442376 | tf_op jit(solution)/shard_map/ppermute | solution.py:767
  10.8 10.0 %collective-permute-start.4 = (f32[232,256]{1,0:T(8,128)S(1)}, f32[232,256]{1,0:T(8,128)S(1)}, u32[]{:S(2)}, u32[]{:S(2)}) collective-permute-start(f32[232,256]{1,0:T(8,128)S(1)} %get-tuple-element.45), channel_id=1, source_target_pairs={{10,2},{18,10},{6,14},{26,18},{14,22},{34,26},{22,30},{42,34},{30,... | collective-permute-start | bytes 712712 | tf_op jit(solution)/shard_map/ppermute | solution.py:769
  13.4 11.3 %collective-permute-start.2 = (f32[224,256]{1,0:T(8,128)S(1)}, f32[224,256]{1,0:T(8,128)S(1)}, u32[]{:S(2)}, u32[]{:S(2)}) collective-permute-start(f32[224,256]{1,0:T(8,128)S(1)} %get-tuple-element.39), channel_id=1, source_target_pairs={{0,1},{1,2},{2,3},{4,5},{5,6},{6,7},{8,9},{9,10},{10,11},{12,13},{... | collective-permute-start | bytes 688136 | tf_op jit(solution)/shard_map/ppermute | solution.py:750
  18.0 6.7 %collective-permute-start.3 = (f32[192,256]{1,0:T(8,128)S(1)}, f32[192,256]{1,0:T(8,128)S(1)}, u32[]{:S(2)}, u32[]{:S(2)}) collective-permute-start(f32[192,256]{1,0:T(8,128)S(1)} %get-tuple-element.40), channel_id=1, source_target_pairs={{1,0},{2,1},{3,2},{5,4},{6,5},{7,6},{9,8},{10,9},{11,10},{13,12},{... | collective-permute-start | bytes 589832 | tf_op jit(solution)/shard_map/ppermute | solution.py:750
  20.9 5.3 %collective-permute-start.5 = (f32[24,256]{1,0:T(8,128)S(1)}, f32[24,256]{1,0:T(8,128)S(1)}, u32[]{:S(2)}, u32[]{:S(2)}) collective-permute-start(f32[24,256]{1,0:T(8,128)S(1)} %get-tuple-element.58.values), channel_id=1, source_target_pairs={{2,6},{6,2},{10,14},{14,10},{18,22},{22,18},{26,30},{30,26},{34,38... | collective-permute-start | bytes 73736 | tf_op jit(solution)/shard_map/ppermute | solution.py:802
  26.2 6.9 %collective-permute-start.6 = (f32[64,256]{1,0:T(8,128)S(1)}, f32[64,256]{1,0:T(8,128)S(1)}, u32[]{:S(2)}, u32[]{:S(2)}) collective-permute-start(f32[64,256]{1,0:T(8,128)S(1)} %pack_new_cross.1), channel_id=1, source_target_pairs={{4,8},{12,16},{20,24},{28,32},{36,40},{44,48},{52,56},{60,64},{68,... | collective-permute-start | bytes 196616 | tf_op jit(solution)/shard_map/ppermute | solution.py:815
  33.2 9.3 %collective-permute-start.7 = (f32[64,256]{1,0:T(8,128)S(1)}, f32[64,256]{1,0:T(8,128)S(1)}, u32[]{:S(2)}, u32[]{:S(2)}) collective-permute-start(f32[64,256]{1,0:T(8,128)S(1)} %pack_last.1), channel_id=1, source_target_pairs={{0,4},{4,0},{8,12},{12,8},{16,20},{20,16},{24,28},{28,24},{32,36},... | collective-permute-start | bytes 196616 | tf_op jit(solution)/shard_map/ppermute | solution.py:826
